TPU v7x, 32 devices: a whole 2x2x4 slice. The times are simulated.
32 devices in a mesh: seq: 8 (over z, x), head: 4 (over y, core).
Axes of the slice: x: 2, y: 2, z: 4, core: 2. Of those that a mesh axis runs over, the one named last changes fastest.
Arguments:
- queries: bfloat16 [4096, 4096], P('seq', 'head'), may hold values from -24 to 24
- key_states: bfloat16 [4096, 4096], P('seq', 'head'), may hold values from -24 to 24
- value_states: bfloat16 [4096, 4096], P('seq', 'head'), may hold values from -6 to 6
- forward_out: bfloat16 [4096, 4096], P('seq', 'head'), may hold values from -3 to 3
- grad_out: bfloat16 [4096, 4096], P('seq', 'head'), may hold values from -96 to 96
- random_blocks: int32 [64, 32, 3], P(None, 'head'), may hold values from 0 to 63, as said below
- global_blocks: int32 [2], replicated, may hold values from 0 to 63, as said below
Outputs:
- grad_queries: bfloat16 [4096, 4096], P(('seq', 'head'))
- grad_keys: bfloat16 [4096, 4096], P(('seq', 'head'))
- grad_values: bfloat16 [4096, 4096], P(('seq', 'head'))
Inputs may be any that keep to these rules, and one draw needn't show every extreme that they name: `random_blocks`: for the query blocks of one shard of 512 tokens and the 8 heads of one head group, at most 30 of the 192 entries name blocks held by any one shard of 8 blocks, and one shard, the same for every group, is named exactly 30 times by every group. `global_blocks`: two different blocks, one of them the last block 63.
All inputs are finite; a program needn't handle non-finite values.
Results may differ from a plain program's by a relative error of at most 0.0053.
Values may be sent and summed in bfloat16 or wider, within the bound.
No kernel may reach another device: no remote copies, remote signals or barrier semaphores. Data moves between devices by JAX's collectives and lax.ppermute only.
A program may use at most 128 MiB of HBM per device.

v0:
```python
from functools import partial

import jax
import jax.numpy as jnp
from jax import lax
from jax.sharding import PartitionSpec as P

DH = 128
BS = 64


def padded(cells, sides, width):
    for axis, dim in sides:
        count = lax.axis_size(axis)
        ends = count - 1
        head = lax.slice_in_dim(cells, 0, width, axis=dim)
        tail = lax.slice_in_dim(cells, cells.shape[dim] - width, cells.shape[dim], axis=dim)
        cells = jnp.concatenate(
            [
                lax.ppermute(tail, axis, [(i, (i + 1) % count) for i in range(ends)]),
                cells,
                lax.ppermute(head, axis, [((i + 1) % count, i) for i in range(ends)]),
            ],
            axis=dim,
        )
    return cells


def scaled(values):
    return values * DH ** (-0.5)


def attend(
    query_row_block,
    gradient_row_block,
    saved_rows,
    gathered_key_block,
    gathered_value_block,
    usable,
    outer_max,
    outer_sum,
):
    logit_scores = scaled(
        jnp.einsum(
            "zxp,zufp->zxuf",
            query_row_block,
            gathered_key_block,
            preferred_element_type=jnp.float32,
        )
    )
    logit_scores = jnp.where(usable[:, None, :, None], logit_scores, -jnp.inf)
    peak_score = jnp.maximum(jnp.max(logit_scores, axis=(2, 3)), outer_max)
    row_sum = jnp.sum(jnp.exp(logit_scores - peak_score[:, :, None, None]), axis=(2, 3))
    row_sum = row_sum + outer_sum * jnp.exp(outer_max - peak_score)
    log_norm = peak_score + jnp.log(row_sum)
    weights = jnp.exp(logit_scores - log_norm[:, :, None, None])
    row_dot = jnp.sum(
        gradient_row_block.astype(jnp.float32) * saved_rows.astype(jnp.float32), axis=-1
    )
    weight_gradient = jnp.einsum(
        "zxp,zufp->zxuf",
        gradient_row_block,
        gathered_value_block,
        preferred_element_type=jnp.float32,
    )
    dscores = weights * (weight_gradient - row_dot[:, :, None, None])
    weight_lowp = weights.astype(jnp.bfloat16)
    score_gradient_lowp = dscores.astype(jnp.bfloat16)
    dq_terms = scaled(
        jnp.einsum(
            "bqjk,bjkd->bqjd",
            score_gradient_lowp,
            gathered_key_block,
            preferred_element_type=jnp.float32,
        )
    )
    key_gradient_parts = scaled(
        jnp.einsum(
            "rmnf,rmc->rnfc",
            score_gradient_lowp,
            query_row_block,
            preferred_element_type=jnp.float32,
        )
    )
    value_gradient_parts = jnp.einsum(
        "rmnf,rmc->rnfc", weight_lowp, gradient_row_block, preferred_element_type=jnp.float32
    )
    return (log_norm, row_dot, dq_terms, key_gradient_parts, value_gradient_parts)


def head_pass(operands, usable):
    (
        query_row_block,
        gradient_row_block,
        saved_rows,
        wide_keys,
        wide_values,
        glob_keys,
        glob_values,
        far_keys,
        far_values,
        outer_max,
        outer_sum,
    ) = operands
    block_count = query_row_block.shape[0]

    def listed(wide_rows, glob_rows, far_rows):
        window_set = jnp.stack([wide_rows[:-2], wide_rows[1:-1], wide_rows[2:]], axis=1)
        glob_set = jnp.broadcast_to(glob_rows[None], (block_count,) + glob_rows.shape)
        return jnp.concatenate([window_set, glob_set, far_rows], axis=1)

    log_norm, row_dot, dq_terms, key_gradient_parts, value_gradient_parts = attend(
        query_row_block,
        gradient_row_block,
        saved_rows,
        listed(wide_keys, glob_keys, far_keys),
        listed(wide_values, glob_values, far_values),
        usable,
        outer_max,
        outer_sum,
    )
    far_query = lax.optimization_barrier(dq_terms[:, :, 5:].astype(jnp.bfloat16)).astype(
        jnp.float32
    )
    grad_query = jnp.sum(dq_terms, axis=2) + jnp.sum(far_query, axis=2)

    def spread(slot_terms):
        widths = ((0, 0), (0, 0), (0, 0))
        first = jnp.pad(slot_terms[:, 0], ((0, 2),) + widths[1:])
        middle = jnp.pad(slot_terms[:, 1], ((1, 1),) + widths[1:])
        last_part = jnp.pad(slot_terms[:, 2], ((2, 0),) + widths[1:])
        return first + middle + last_part

    return (
        grad_query,
        log_norm,
        row_dot,
        spread(key_gradient_parts),
        spread(value_gradient_parts),
        jnp.sum(key_gradient_parts[:, 3:5], axis=0),
        jnp.sum(value_gradient_parts[:, 3:5], axis=0),
        key_gradient_parts[:, 5:].astype(jnp.bfloat16),
        value_gradient_parts[:, 5:].astype(jnp.bfloat16),
    )


def on_device(
    queries, key_states, value_states, forward_out, grad_out, random_blocks, global_blocks
):
    seq_count = lax.axis_size("seq")
    my_seq = lax.axis_index("seq")
    tokens = queries.shape[0]
    blocks = tokens // BS
    head_count = queries.shape[1] // DH
    requests = blocks * head_count * 3
    slot_count = max(2, (5 * requests + 4 * seq_count - 1) // (4 * seq_count))
    kv_pair = jnp.stack([key_states, value_states])
    kv_wide = padded(kv_pair, (("seq", 1),), BS)
    kv_heads = kv_wide.reshape(2, blocks + 2, BS, head_count, DH).transpose(0, 3, 1, 2, 4)
    kv_owned = kv_heads[:, :, 1:-1]
    kv_flat = (
        kv_pair.reshape(2, blocks, BS, head_count, DH)
        .transpose(0, 1, 3, 2, 4)
        .reshape(2, blocks * head_count, BS, DH)
    )
    glob_owner = global_blocks // blocks
    glob_local = global_blocks % blocks
    glob_mine = glob_owner == my_seq
    picked = kv_owned[:, :, glob_local] * glob_mine.astype(jnp.bfloat16)[None, None, :, None, None]
    glob_kv = lax.psum(picked, "seq").astype(jnp.float32).astype(jnp.bfloat16)
    table = random_blocks.reshape(seq_count, requests)
    owner_of = table // blocks
    local_of = table % blocks
    seq_ids = jnp.arange(seq_count, dtype=jnp.int32)
    onehot = (owner_of[:, :, None] == seq_ids[None, None, :]).astype(jnp.int32)
    before = jnp.cumsum(onehot, axis=1) - onehot
    rank_of = jnp.sum(before * onehot, axis=2)
    my_owner = lax.dynamic_index_in_dim(owner_of, my_seq, 0, keepdims=False)
    my_rank = lax.dynamic_index_in_dim(rank_of, my_seq, 0, keepdims=False)
    send_pos = my_owner * slot_count + my_rank
    request_ids = jnp.arange(requests, dtype=jnp.int32)
    pair_of = request_ids // 3
    spill_slot = seq_count * slot_count
    target = jnp.where(
        owner_of == my_seq, seq_ids[:, None] * slot_count + rank_of, spill_slot
    ).reshape(-1)
    head_all = jnp.broadcast_to(pair_of % head_count, (seq_count, requests)).reshape(-1)
    recv_block = (
        jnp.zeros((spill_slot + 1,), jnp.int32).at[target].set(local_of.reshape(-1))[:spill_slot]
    )
    recv_head = jnp.zeros((spill_slot + 1,), jnp.int32).at[target].set(head_all)[:spill_slot]
    recv_used = jnp.zeros((spill_slot + 1,), jnp.float32).at[target].set(1.0)[:spill_slot]
    recv_index = recv_block * head_count + recv_head

    def head_major(array):
        return array.reshape(blocks, BS, head_count, DH).transpose(2, 0, 1, 3)

    query_heads = head_major(queries)
    grad_heads = head_major(grad_out)
    saved_heads = head_major(forward_out)
    block_ids = jnp.arange(blocks)
    always = jnp.ones((blocks,), bool)
    has_prev = (block_ids > 0) | (my_seq > 0)
    has_next = (block_ids < blocks - 1) | (my_seq < seq_count - 1)
    qd_flat = jnp.stack([queries, grad_out]).reshape(2, blocks, BS, head_count, DH)
    qd_flat = qd_flat.transpose(0, 1, 3, 2, 4).reshape(2, blocks * head_count, BS, DH)
    outgoing = (
        jnp.zeros((2, spill_slot, BS, DH), jnp.bfloat16).at[:, send_pos].set(qd_flat[:, pair_of])
    )
    arrived = lax.all_to_all(outgoing, "seq", split_axis=1, concat_axis=1, tiled=True)
    owned_kv = kv_flat[:, recv_index]
    far_scores = scaled(
        jnp.einsum("sqd,skd->sqk", arrived[0], owned_kv[0], preferred_element_type=jnp.float32)
    )
    far_max = jnp.max(far_scores, axis=-1)
    far_sum = jnp.sum(jnp.exp(far_scores - far_max[:, :, None]), axis=-1)
    back_max, back_sum = (
        lax.all_to_all(far_max, "seq", split_axis=0, concat_axis=0, tiled=True),
        lax.all_to_all(far_sum, "seq", split_axis=0, concat_axis=0, tiled=True),
    )
    far_peak = back_max[send_pos].reshape(blocks, head_count, 3, BS).transpose(1, 0, 3, 2)
    far_total = back_sum[send_pos].reshape(blocks, head_count, 3, BS).transpose(1, 0, 3, 2)
    outer_max = jnp.max(far_peak, axis=-1)
    outer_sum = jnp.sum(far_total * jnp.exp(far_peak - outer_max[..., None]), axis=-1)
    usable = jnp.stack([has_prev, always, has_next, always, always], axis=1)
    empty_far = jnp.zeros((head_count, blocks, 0, BS, DH), jnp.bfloat16)
    results = lax.map(
        partial(head_pass, usable=usable),
        (
            query_heads,
            grad_heads,
            saved_heads,
            kv_heads[0],
            kv_heads[1],
            glob_kv[0],
            glob_kv[1],
            empty_far,
            empty_far,
            outer_max,
            outer_sum,
        ),
    )
    norm_pairs = results[1].transpose(1, 0, 2).reshape(blocks * head_count, BS)
    dot_pairs = results[2].transpose(1, 0, 2).reshape(blocks * head_count, BS)
    norm_send = jnp.zeros((spill_slot, BS), jnp.float32).at[send_pos].set(norm_pairs[pair_of])
    dot_send = jnp.zeros((spill_slot, BS), jnp.float32).at[send_pos].set(dot_pairs[pair_of])
    got_norm, got_dot = (
        lax.all_to_all(norm_send, "seq", split_axis=0, concat_axis=0, tiled=True),
        lax.all_to_all(dot_send, "seq", split_axis=0, concat_axis=0, tiled=True),
    )
    far_weights = jnp.exp(far_scores - got_norm[:, :, None])
    far_dweights = jnp.einsum(
        "sqd,skd->sqk", arrived[1], owned_kv[1], preferred_element_type=jnp.float32
    )
    far_dscores = far_weights * (far_dweights - got_dot[:, :, None])
    far_weights_b = far_weights.astype(jnp.bfloat16)
    far_dscores_b = far_dscores.astype(jnp.bfloat16)
    far_dq = scaled(
        jnp.einsum("sqk,skd->sqd", far_dscores_b, owned_kv[0], preferred_element_type=jnp.float32)
    ).astype(jnp.bfloat16)
    far_dk = scaled(
        jnp.einsum("sqk,sqd->skd", far_dscores_b, arrived[0], preferred_element_type=jnp.float32)
    ).astype(jnp.bfloat16)
    far_dv = jnp.einsum(
        "sqk,sqd->skd", far_weights_b, arrived[1], preferred_element_type=jnp.float32
    ).astype(jnp.bfloat16)
    came_back = lax.all_to_all(far_dq, "seq", split_axis=0, concat_axis=0, tiled=True)
    far_rows = came_back[send_pos].reshape(blocks, head_count, 3, BS, DH).transpose(1, 0, 2, 3, 4)
    grad_query = results[0] + jnp.sum(far_rows.astype(jnp.float32), axis=2)
    far_kv = lax.optimization_barrier(jnp.stack([far_dk, far_dv])).astype(jnp.float32)
    far_grads = far_kv * recv_used[None, :, None, None]
    owned_far = (
        jnp.zeros((2, blocks * head_count, BS, DH), jnp.float32).at[:, recv_index].add(far_grads)
    )
    rim_pack = jnp.stack([results[3], results[4]])
    rim_out = jnp.concatenate([rim_pack[:, :, 0], rim_pack[:, :, -1]], axis=2)
    rim_in = padded(rim_out, (("seq", 2),), BS)
    owned = rim_pack[:, :, 1:-1]
    owned = owned.at[:, :, 0].add(rim_in[:, :, :BS]).at[:, :, -1].add(rim_in[:, :, -BS:])
    glob_sum = lax.psum(jnp.stack([results[5], results[6]]), "seq")
    glob_sum = glob_sum * glob_mine.astype(jnp.float32)[None, None, :, None, None]
    owned = owned.at[:, :, glob_local].add(glob_sum)
    owned = owned + owned_far.reshape(2, blocks, head_count, BS, DH).transpose(0, 2, 1, 3, 4)
    grads_kv = (
        owned.astype(jnp.bfloat16).transpose(0, 2, 3, 1, 4).reshape(2, tokens, head_count * DH)
    )
    dq_rows = grad_query.astype(jnp.bfloat16).transpose(1, 2, 0, 3).reshape(tokens, head_count * DH)
    out_query, out_keys, out_values = (
        lax.all_to_all(dq_rows, "head", split_axis=0, concat_axis=1, tiled=True),
        lax.all_to_all(grads_kv[0], "head", split_axis=0, concat_axis=1, tiled=True),
        lax.all_to_all(grads_kv[1], "head", split_axis=0, concat_axis=1, tiled=True),
    )
    return (out_query, out_keys, out_values)


def solution(mesh):
    return jax.shard_map(
        on_device,
        mesh=mesh,
        in_specs=(
            P("seq", "head"),
            P("seq", "head"),
            P("seq", "head"),
            P("seq", "head"),
            P("seq", "head"),
            P(None, "head", None),
            P(),
        ),
        out_specs=(P(("seq", "head"), None), P(("seq", "head"), None), P(("seq", "head"), None)),
        check_vma=False,
    )
```

profile of v0, /device:TPU:8, one launch (start us, length us, event | category | flops | bytes accessed | tf_op | source)
XLA Modules:
  0.0 801.3 jit_solution(4355752847193994815)
XLA Ops:
  16.2 8.1 %gather_fusion.1 = bf16[192,2,64,128]{3,2,1,0:T(8,128)(2,1)} fusion(bf16[2,64,64,128]{3,2,1,0:T(8,128)(2,1)S(1)} %bitcast.339, s32[1024]{0:T(1024)S(1)} %pad_clamp_fusion.2), kind=kCustom, calls=%fused_computation.1 | custom fusion | bytes 12583680 | tf_op jit(solution)/shard_map/gather | solution.py:208
  24.3 5.1 broadcast_in_dim.145
  29.4 29.2 %scatter_fusion = bf16[2,240,64,128]{3,2,1,0:T(8,128)(2,1)} fusion(bf16[2,240,64,128]{3,2,1,0:T(8,128)(2,1)} %broadcast_in_dim.145, s32[192]{0:T(256)S(1)} %bitcast.386, bf16[192,2,64,128]{3,2,1,0:T(8,128)(2,1)} %gather_fusion.1), kind=kCustom, calls=%fused_computation.8 | custom fusion | bytes 18875136 | tf_op jit(solution)/shard_map/scatter | solution.py:208
  58.7 9.2 %copy.176 = bf16[2,240,64,128]{3,2,0,1:T(8,128)(2,1)} copy(bf16[2,240,64,128]{3,2,1,0:T(8,128)(2,1)} %scatter_fusion) | data formatting | bytes 15728640 | tf_op jit(solution)/shard_map/scatter | solution.py:208
  67.9 6.5 all-to-all-start
  84.5 6.2 scatter_custom_fusion.2
  90.7 6.4 scatter_custom_fusion.1
  108.7 8.5 %gather_fusion.2 = bf16[240,2,64,128]{3,2,1,0:T(8,128)(2,1)} fusion(bf16[2,64,64,128]{3,2,1,0:T(8,128)(2,1)S(1)} %bitcast.338, s32[1024]{0:T(1024)S(1)} %pad_clamp_fusion.1), kind=kCustom, calls=%fused_computation.2 | custom fusion | bytes 15729600 | tf_op jit(solution)/shard_map/gather | solution.py:211
  117.2 8.9 %copy.249 = bf16[240,2,64,128]{3,2,0,1:T(8,128)(2,1)} copy(bf16[240,2,64,128]{3,2,1,0:T(8,128)(2,1)} %gather_fusion.2) | data formatting | bytes 15728640 | tf_op jit(solution)/shard_map/gather | solution.py:211
  128.6 6.7 scatter_custom_fusion.5
  135.3 30.2 %collective-permute-done.1 = bf16[2,64,1024]{2,1,0:T(8,128)(2,1)} collective-permute-done((bf16[2,64,1024]{2,1,0:T(8,128)(2,1)}, bf16[2,64,1024]{2,1,0:T(8,128)(2,1)}, u32[]{:S(2)}, u32[]{:S(2)}) %collective-permute-start.1) | collective-permute-done | bytes 262176 | tf_op jit(solution)/shard_map/ppermute | solution.py:22
  165.5 47.5 %collective-permute-done = bf16[2,64,1024]{2,1,0:T(8,128)(2,1)} collective-permute-done((bf16[2,64,1024]{2,1,0:T(8,128)(2,1)}, bf16[2,64,1024]{2,1,0:T(8,128)(2,1)}, u32[]{:S(2)}, u32[]{:S(2)}) %collective-permute-start) | collective-permute-done | bytes 262176 | tf_op jit(solution)/shard_map/ppermute | solution.py:20
  223.5 105.4 %all-reduce.10.cloned.1.call-done = bf16[2,8,2,64,128]{4,3,1,0,2:T(8,128)(2,1)} async-done(((bf16[2,8,2,64,128]{4,3,1,0,2:T(8,128)(2,1)}), bf16[2,8,2,64,128]{4,3,1,0,2:T(8,128)(2,1)}) %all-reduce.10.cloned.1.call-update) | async-done | bytes 524304 | tf_op jit(solution)/shard_map/psum | solution.py:170
  330.0 8.7 %multiply_reduce_fusion = (f32[240,64]{1,0:T(8,128)S(1)}, f32[240,64,64]{1,2,0:T(8,128)}) fusion(bf16[2,240,64,128]{3,2,1,0:T(8,128)(2,1)} %bitcast.340, bf16[2,240,64,128]{3,2,0,1:T(8,128)(2,1)} %all-to-all-done), kind=kOutput, calls=%fused_computation.99 | convolution fusion | flops 253608960 | bytes 11857920 | tf_op jit(solution)/shard_map/sqd,skd->sqk/dot_general | solution.py:213
  339.4 15.9 %all-to-all-start.1 = ((f32[8,1,1920]{2,1,0:T(1,128)}), f32[8,1,1920]{2,1,0:T(1,128)S(1)}, u32[]{:S(2)}, u32[]{:S(2)}) async-start(f32[8,1,1920]{2,1,0:T(1,128)} %reshape.668), calls=%async_computation.1 | async-start | bytes 122880 | tf_op jit(solution)/shard_map/all_to_all | solution.py:218
  355.3 5.3 exponential_reduce_fusion.1
  361.4 6.1 all-to-all-start.2
  378.2 109.5 %while.26 = (s32[]{:T(128)}, f32[8,8,64,128]{3,2,0,1:T(8,128)}, f32[8,8,64]{2,1,0:T(8,128)}, f32[8,8,64]{2,1,0:T(8,128)}, f32[8,10,64,128]{3,2,0,1:T(8,128)S(1)}...) while((s32[]{:T(128)}, f32[8,8,64,128]{3,2,0,1:T(8,128)}, ...), condition=%wide.region_18.19_spmd, body=%wide.region_11.18_spmd.sunk | while | flops 219483648 | bytes 18933040 | solution.py:227
  507.5 5.1 all-to-all-start.3
  518.7 7.8 convert_bitcast_fusion
  526.4 7.8 multiply_convert_fusion.2
  536.2 5.3 fusion.37
  551.9 6.6 multiply_bitcast_fusion
  558.5 14.6 %copy.201 = f32[240,2,64,128]{3,2,1,0:T(8,128)} copy(f32[240,2,64,128]{3,2,0,1:T(8,128)} %multiply_bitcast_fusion) | data formatting | bytes 31457280 | tf_op jit(solution)/shard_map/mul | solution.py:271
  575.6 49.1 %scatter_fusion.1 = f32[2,64,64,128]{3,2,1,0:T(8,128)} fusion(f32[2,64,64,128]{3,2,1,0:T(8,128)} %broadcast_in_dim.149, s32[240]{0:T(256)S(1)} %compare_select_fusion.7, f32[240,2,64,128]{3,2,1,0:T(8,128)} %copy.201), kind=kCustom, calls=%fused_computation.14 | custom fusion | flops 3932160 | bytes 47186880 | tf_op jit(solution)/shard_map/scatter-add | solution.py:273
  633.1 5.1 bitcast_add_fusion.1
  649.6 6.7 multiply_convert_fusion.1
  656.4 7.7 all-to-all-done.7
  664.1 6.1 all-to-all-start.5
  672.1 82.9 %all-to-all-done.5 = bf16[240,64,128]{2,1,0:T(8,128)(2,1)} async-done(((bf16[240,64,128]{2,1,0:T(8,128)(2,1)}), bf16[240,64,128]{2,1,0:T(8,128)(2,1)}, u32[]{:S(2)}, u32[]{:S(2)}) %all-to-all-start.5) | async-done | bytes 3932192 | tf_op jit(solution)/shard_map/all_to_all | solution.py:267
  766.9 7.2 all-to-all-done.8
  782.5 9.5 %all-to-all-done.6 = bf16[4,128,1024]{2,1,0:T(8,128)(2,1)S(1)} async-done(((bf16[4,128,1024]{2,1,0:T(8,128)(2,1)}), bf16[4,128,1024]{2,1,0:T(8,128)(2,1)S(1)}, u32[]{:S(2)}, u32[]{:S(2)}) %all-to-all-start.6) | async-done | bytes 1048608 | tf_op jit(solution)/shard_map/all_to_all | solution.py:289
  (397 shorter events, 249.8 us)
Async XLA Ops:
  7.2 7.7 copy-start.17
  8.8 6.4 copy-start.8
  67.9 6.5 copy-start.5
  67.9 6.5 copy-start.6
  67.9 262.1 %all-to-all-start = ((bf16[2,240,64,128]{3,2,0,1:T(8,128)(2,1)}), bf16[2,240,64,128]{3,2,0,1:T(8,128)(2,1)}, u32[]{:S(2)}, u32[]{:S(2)}) async-start(bf16[2,240,64,128]{3,2,0,1:T(8,128)(2,1)} %copy.176), calls=%async_computation | async-start | bytes 15728640 | tf_op jit(solution)/shard_map/all_to_all | solution.py:210
  74.4 254.5 %all-reduce.10.cloned.1.call-start = ((), (), s32[]{:S(2)}) async-start(), calls=%async_computation.9 | async-start | bytes 1048576 | tf_op jit(solution)/shard_map/psum | solution.py:170
  75.2 23.5 %copy-start.23 = (s32[2]{0:T(128)S(1)}, s32[2]{0:T(128)}, u32[]{:S(2)}) copy-start(s32[2]{0:T(128)} %param.19) | copy-start | bytes 28
  75.2 90.3 %collective-permute-start.1 = (bf16[2,64,1024]{2,1,0:T(8,128)(2,1)}, bf16[2,64,1024]{2,1,0:T(8,128)(2,1)}, u32[]{:S(2)}, u32[]{:S(2)}) collective-permute-start(bf16[2,64,1024]{2,1,0:T(8,128)(2,1)} %get-tuple-element.407), channel_id=1, source_target_pairs={{4,0},{8,4},{12,8},{16,12},{20,16},{24,20},{28,24},{5,1},{9,5},{13... | collective-permute-start | bytes 786440 | tf_op jit(solution)/shard_map/ppermute | solution.py:22
  78.7 134.2 %collective-permute-start = (bf16[2,64,1024]{2,1,0:T(8,128)(2,1)}, bf16[2,64,1024]{2,1,0:T(8,128)(2,1)}, u32[]{:S(2)}, u32[]{:S(2)}) collective-permute-start(bf16[2,64,1024]{2,1,0:T(8,128)(2,1)} %get-tuple-element.406), channel_id=1, source_target_pairs={{0,4},{4,8},{8,12},{12,16},{16,20},{20,24},{24,28},{1,5},{5,9},{9,... | collective-permute-start | bytes 786440 | tf_op jit(solution)/shard_map/ppermute | solution.py:20
  82.9 20.0 %copy-start.9 = (bf16[64,8,8,128]{3,2,1,0:T(8,128)(2,1)S(1)}, bf16[64,8,8,128]{3,2,1,0:T(8,128)(2,1)}, u32[]{:S(2)}) copy-start(bf16[64,8,8,128]{3,2,1,0:T(8,128)(2,1)} %copy-done.8) | copy-start | bytes 3145732
  97.1 5.9 copy-start.11
  117.2 8.9 %copy-start.14 = (bf16[8,8,64,128]{3,0,2,1:T(8,128)(2,1)S(1)}, bf16[8,8,64,128]{3,0,2,1:T(8,128)(2,1)}, u32[]{:S(2)}) copy-start(bf16[8,8,64,128]{3,0,2,1:T(8,128)(2,1)} %bitcast_bitcast_fusion.1) | copy-start | bytes 3145732
  117.2 10.1 %copy-start.15 = (bf16[8,8,64,128]{3,0,2,1:T(8,128)(2,1)S(1)}, bf16[8,8,64,128]{3,0,2,1:T(8,128)(2,1)}, u32[]{:S(2)}) copy-start(bf16[8,8,64,128]{3,0,2,1:T(8,128)(2,1)} %bitcast_bitcast_fusion) | copy-start | bytes 3145732
  126.1 86.9 %copy-start.7 = (bf16[512,1024]{1,0:T(8,128)(2,1)S(1)}, bf16[512,1024]{1,0:T(8,128)(2,1)}, u32[]{:S(2)}) copy-start(bf16[512,1024]{1,0:T(8,128)(2,1)} %param.14) | copy-start | bytes 3145732
  339.4 22.0 %all-to-all-start.1 = ((f32[8,1,1920]{2,1,0:T(1,128)}), f32[8,1,1920]{2,1,0:T(1,128)S(1)}, u32[]{:S(2)}, u32[]{:S(2)}) async-start(f32[8,1,1920]{2,1,0:T(1,128)} %reshape.668), calls=%async_computation.1 | async-start | bytes 122880 | tf_op jit(solution)/shard_map/all_to_all | solution.py:218
  360.6 17.6 %copy-start.1 = (f32[8,10,64,128]{3,2,0,1:T(8,128)S(1)}, f32[8,10,64,128]{3,2,0,1:T(8,128)}, u32[]{:S(2)}) copy-start(f32[8,10,64,128]{3,2,0,1:T(8,128)} %custom-call.19) | copy-start | bytes 7864324
  361.4 11.3 %all-to-all-start.2 = ((f32[8,1,1920]{2,1,0:T(1,128)}), f32[8,1,1920]{2,1,0:T(1,128)}, u32[]{:S(2)}, u32[]{:S(2)}) async-start(f32[8,1,1920]{2,1,0:T(1,128)} %reshape.670), calls=%async_computation.2 | async-start | bytes 122880 | tf_op jit(solution)/shard_map/all_to_all | solution.py:219
  487.7 15.5 %copy-start.2 = (f32[8,10,64,128]{3,2,0,1:T(8,128)}, f32[8,10,64,128]{3,2,0,1:T(8,128)S(1)}, u32[]{:S(2)}) copy-start(f32[8,10,64,128]{3,2,0,1:T(8,128)S(1)} %get-tuple-element.257) | copy-start | bytes 7864324
  490.9 16.6 %all-to-all-start.4 = ((f32[8,1,1920]{2,1,0:T(1,128)}), f32[8,1,1920]{2,1,0:T(1,128)S(1)}, u32[]{:S(2)}, u32[]{:S(2)}) async-start(f32[8,1,1920]{2,1,0:T(1,128)} %reshape.672), calls=%async_computation.4 | async-start | bytes 122880 | tf_op jit(solution)/shard_map/all_to_all | solution.py:249
  503.3 9.4 %copy-start.18 = (f32[8,2,64,128]{3,2,1,0:T(8,128)S(1)}, f32[8,2,64,128]{3,2,1,0:T(8,128)}, u32[]{:S(2)}) copy-start(f32[8,2,64,128]{3,2,1,0:T(8,128)} %get-tuple-element.259) | copy-start | bytes 1572868
  504.1 41.5 %collective-permute-start.2 = (f32[2,8,64,128]{3,2,1,0:T(8,128)}, f32[2,8,64,128]{3,2,1,0:T(8,128)}, u32[]{:S(2)}, u32[]{:S(2)}) collective-permute-start(f32[2,8,64,128]{3,2,1,0:T(8,128)} %fusion.49), channel_id=1, source_target_pairs={{0,4},{4,8},{8,12},{12,16},{16,20},{20,24},{24,28},{1,5},{5,9},{9,... | collective-permute-start | bytes 1572872 | tf_op jit(solution)/shard_map/ppermute | solution.py:20
  507.5 10.2 %all-to-all-start.3 = ((f32[8,1,1920]{2,1,0:T(1,128)}), f32[8,1,1920]{2,1,0:T(1,128)S(1)}, u32[]{:S(2)}, u32[]{:S(2)}) async-start(f32[8,1,1920]{2,1,0:T(1,128)} %reshape.674), calls=%async_computation.3 | async-start | bytes 122880 | tf_op jit(solution)/shard_map/all_to_all | solution.py:248
  512.6 116.7 %all-reduce.12.cloned.1.call-start = ((), (), s32[]{:S(2)}) async-start(), calls=%async_computation.10 | async-start | bytes 2097152 | tf_op jit(solution)/shard_map/psum | solution.py:280
  545.6 6.3 copy-start.22
  548.1 82.9 %collective-permute-start.3 = (f32[2,8,64,128]{3,2,1,0:T(8,128)}, f32[2,8,64,128]{3,2,1,0:T(8,128)}, u32[]{:S(2)}, u32[]{:S(2)}) collective-permute-start(f32[2,8,64,128]{3,2,1,0:T(8,128)} %get-tuple-element.400), channel_id=1, source_target_pairs={{4,0},{8,4},{12,8},{16,12},{20,16},{24,20},{28,24},{5,1},{9,5},{13... | collective-permute-start | bytes 1572872 | tf_op jit(solution)/shard_map/ppermute | solution.py:22
  633.1 5.1 copy-start.21
  646.1 18.0 %all-to-all-start.7 = ((bf16[4,128,1024]{2,1,0:T(8,128)(2,1)}), bf16[4,128,1024]{2,1,0:T(8,128)(2,1)S(1)}, u32[]{:S(2)}, u32[]{:S(2)}) async-start(bf16[4,128,1024]{2,1,0:T(8,128)(2,1)} %all_to_all.92), calls=%async_computation.7 | async-start | bytes 2097152 | tf_op jit(solution)/shard_map/all_to_all | solution.py:290
  664.0 6.1 copy-start.12
  664.1 91.0 %all-to-all-start.5 = ((bf16[240,64,128]{2,1,0:T(8,128)(2,1)}), bf16[240,64,128]{2,1,0:T(8,128)(2,1)}, u32[]{:S(2)}, u32[]{:S(2)}) async-start(bf16[240,64,128]{2,1,0:T(8,128)(2,1)} %multiply_convert_fusion.1), calls=%async_computation.5 | async-start | bytes 7864320 | tf_op jit(solution)/shard_map/all_to_all | solution.py:267
  755.0 19.0 %all-to-all-start.8 = ((bf16[4,128,1024]{2,1,0:T(8,128)(2,1)}), bf16[4,128,1024]{2,1,0:T(8,128)(2,1)}, u32[]{:S(2)}, u32[]{:S(2)}) async-start(bf16[4,128,1024]{2,1,0:T(8,128)(2,1)} %all_to_all.96), calls=%async_computation.8 | async-start | bytes 2097152 | tf_op jit(solution)/shard_map/all_to_all | solution.py:291
  764.9 12.7 %copy-start.13 = (bf16[4,128,1024]{2,1,0:T(8,128)(2,1)S(1)}, bf16[4,128,1024]{2,1,0:T(8,128)(2,1)}, u32[]{:S(2)}) copy-start(bf16[4,128,1024]{2,1,0:T(8,128)(2,1)} %copy-done.12) | copy-start | bytes 3145732
  774.1 18.0 %all-to-all-start.6 = ((bf16[4,128,1024]{2,1,0:T(8,128)(2,1)}), bf16[4,128,1024]{2,1,0:T(8,128)(2,1)S(1)}, u32[]{:S(2)}, u32[]{:S(2)}) async-start(bf16[4,128,1024]{2,1,0:T(8,128)(2,1)} %all_to_all.88), calls=%async_computation.6 | async-start | bytes 2097152 | tf_op jit(solution)/shard_map/all_to_all | solution.py:289
  (7 other events, 17.8 us)
Sparse Core Ops, SparseCore 0:
  220.6 108.2 all-reduce.9
  518.0 79.4 all-reduce.11
where the time goes:
time: 818 us; the launch traced here: 801 us
  waiting for transfers between devices  295 us (36%)
  local copies, waits for them, and re-layouts  210 us (26%)
  other arithmetic  132 us (16%)
  matrix products  79.4 us (10%)
  starting transfers between devices  69.4 us (8%)
  between operations  15.2 us (2%)
    psum x1, waiting for transfers between devices, on_device(): glob_kv = lax.psum(picked, 'seq').astype(jnp.float32).astype(jnp.bfloat16)  105 us
    all_to_all x1, waiting for transfers between devices, on_device(): lax.all_to_all(far_dq, 'seq', split_axis=0, concat_axis=0, tiled=True)  82.9 us
    scatter-add x1, other arithmetic, on_device(): jnp.zeros((2, blocks * head_count, BS, DH), jnp.float32).at[:, recv_index]  49.1 us
    ppermute x2, waiting for transfers between devices, padded(): lax.ppermute(tail, axis, [(i, (i + 1) % count) for i in range(ends)])  47.5 us
    scatter x2, local copies, waits for them, and re-layouts, on_device(): jnp.zeros((2, spill_slot, BS, DH), jnp.bfloat16).at[:, send_pos]  38.5 us
    ppermute x2, waiting for transfers between devices, padded(): lax.ppermute(head, axis, [((i + 1) % count, i) for i in range(ends)])  30.2 us
    unnamed x66, local copies, waits for them, and re-layouts  18.3 us
    another operation x16, local copies, waits for them, and re-layouts, listed(): jnp.stack([wide_rows[:-2], wide_rows[1:-1], wide_rows[2:]], axis=1)  17.5 us
  transfers between devices with their start and end apart: 15, of which 9 were waited for; matrix products, arithmetic and copies ran while one was open for 26% of the time, Pallas kernels for 0%

commit v1 on v0

v1 whole, which is shorter than its diff:
```python
from functools import partial
import math

import jax
import jax.numpy as jnp
from jax import lax
from jax.experimental import pallas as pl
from jax.experimental.pallas import tpu as pltpu
from jax.sharding import PartitionSpec as P

DH = 128
BS = 64
GROUP = 4
BATCH = 8
LOG2E = math.log2(math.e)
SCALE = DH**-0.5
OFF = 1e30
NT = (((1,), (1,)), ((), ()))
TN = (((0,), (0,)), ((), ()))


def dot(a, b, dims=(((1,), (0,)), ((), ()))):
    return lax.dot_general(a, b, dims, preferred_element_type=jnp.float32)


def aligned(start):
    return pl.multiple_of(start, BS)


def place_group(me, key_refs, key_rows, tokens):
    for j, ref in enumerate(key_refs):
        start = aligned(BS + (lax.rem(me, GROUP) ^ j) * tokens)
        key_rows[pl.ds(start, tokens), :] = ref[...]


def zero_ends(key_rows):
    edge = jnp.zeros((BS, DH), key_rows.dtype)
    key_rows[pl.ds(0, BS), :] = edge
    key_rows[pl.ds(key_rows.shape[0] - BS, BS), :] = edge


def local_block(block, group, group_blocks):
    place = block - group * group_blocks
    inside = (place >= 0) & (place < group_blocks)
    return jnp.where(inside, place, 0), inside


def edge_block(src, b, blocks, seq_count, group, group_blocks):
    last = blocks - 1
    if b == 0:
        return local_block(src * blocks - 1, group, group_blocks)
    if b == last:
        return local_block((src + 1) * blocks, group, group_blocks)
    return None


def norm_kernel(sizes, meta, table, *refs):
    seq_count, remote, blocks, heads = sizes
    sources = remote + 1
    tokens = blocks * BS
    q_refs = refs[:sources]
    k_refs = refs[sources : sources + GROUP]
    out_ref, key_rows = refs[sources + GROUP :]
    head = pl.program_id(0)
    me = meta[0]
    group = me // GROUP
    group_blocks = GROUP * blocks
    c2 = SCALE * LOG2E

    @pl.when(head == 0)
    def _():
        zero_ends(key_rows)

    place_group(me, k_refs, key_rows, tokens)
    globs = [local_block(meta[1 + j], group, group_blocks) for j in range(2)]
    glob_keys = [key_rows[pl.ds(aligned(BS + p * BS), BS), :] for p, _ in globs]

    for r in range(sources):
        src = lax.rem(me - GROUP * r + seq_count, seq_count)
        for b in range(blocks):
            q = q_refs[r][pl.ds(b * BS, BS), :]
            tiles, ok = [], []
            if r == 0:
                start = aligned((lax.rem(me, GROUP) * blocks + b) * BS)
                window = key_rows[pl.ds(start, 3 * BS), :]
                tiles += [window[j * BS : (j + 1) * BS] for j in range(3)]
                at_first = (lax.rem(me, GROUP) > 0) if b == 0 else None
                at_last = (lax.rem(me, GROUP) < GROUP - 1) if b == blocks - 1 else None
                ok += [at_first, None, at_last]
            else:
                found = edge_block(src, b, blocks, seq_count, group, group_blocks)
                if found is not None:
                    tiles.append(key_rows[pl.ds(aligned(BS + found[0] * BS), BS), :])
                    ok.append(found[1])
            for j in range(2):
                tiles.append(glob_keys[j])
                ok.append(globs[j][1])
            for j in range(3):
                entry = table[((src * blocks + b) * heads + head) * 3 + j]
                place, inside = local_block(entry, group, group_blocks)
                tiles.append(key_rows[pl.ds(aligned(BS + place * BS), BS), :])
                ok.append(inside)
            scores = []
            for tile, flag in zip(tiles, ok):
                s = dot(tile, q, NT) * c2
                if flag is not None:
                    s = s - jnp.where(flag, 0.0, OFF)
                scores.append(s)
            top = scores[0]
            for s in scores[1:]:
                top = jnp.maximum(top, s)
            top = jnp.max(top, axis=0, keepdims=True)
            total = jnp.exp2(scores[0] - top)
            for s in scores[1:]:
                total = total + jnp.exp2(s - top)
            total = jnp.sum(total, axis=0, keepdims=True)
            out_ref[r, 0, pl.ds(b, 1), :] = top + jnp.log2(total)


def grads_kernel(sizes, head0, meta, table, *refs):
    seq_count, remote, blocks, heads = sizes
    sources = remote + 1
    tokens = blocks * BS
    refs = list(refs)

    def take(count):
        taken = refs[:count]
        del refs[:count]
        return taken

    q_refs, g_refs = take(sources), take(sources)
    k_refs, v_refs = take(GROUP), take(GROUP)
    norm_ref, dot_ref, norm_flat, dot_flat = take(4)
    (dq_own,) = take(1)
    dq_far = take(remote)
    dk_keep, dk_send, dv_keep, dv_send = take(4)
    q_rows, g_rows, k_rows, v_rows, dq_sum, dk_sum, dv_sum, listed = refs
    head = pl.program_id(0) + head0
    me = meta[0]
    pos = lax.rem(me, GROUP)
    group = me // GROUP
    group_blocks = GROUP * blocks
    c2 = SCALE * LOG2E

    @pl.when(pl.program_id(0) == 0)
    def _():
        zero_ends(k_rows)
        zero_ends(v_rows)

    place_group(me, k_refs, k_rows, tokens)
    place_group(me, v_refs, v_rows, tokens)
    for r in range(sources):
        q_rows[pl.ds(r * tokens, tokens), :] = q_refs[r][...]
        g_rows[pl.ds(r * tokens, tokens), :] = g_refs[r][...]
    dk_sum[...] = jnp.zeros_like(dk_sum)
    dv_sum[...] = jnp.zeros_like(dv_sum)
    dq_sum[...] = jnp.zeros_like(dq_sum)

    count = jnp.int32(0)

    def note(count, item, place, inside):
        listed[count] = item * group_blocks + place
        return count + inside.astype(jnp.int32)

    for r in range(sources):
        src = lax.rem(me - GROUP * r + seq_count, seq_count)
        for b in range(blocks):
            item = r * blocks + b
            for j in range(3):
                entry = table[((src * blocks + b) * heads + head) * 3 + j]
                count = note(count, item, *local_block(entry, group, group_blocks))
            if r > 0:
                found = edge_block(src, b, blocks, seq_count, group, group_blocks)
                if found is not None:
                    count = note(count, item, *found)
    for u in range(BATCH):
        listed[count + u] = 0

    def terms(q, g, k, v, norm, rdot):
        w = jnp.exp2(dot(k, q, NT) * c2 - norm)
        ds = w * (dot(v, g, NT) - rdot)
        wb, dsb = w.astype(jnp.bfloat16), ds.astype(jnp.bfloat16)
        return dot(dsb, k, TN), dot(dsb, q), dot(wb, g)

    lane = lax.broadcasted_iota(jnp.int32, (1, 2 * BS), 1)
    pairs = blocks // 2
    for t in range(pairs):
        rows = pl.ds(t * 2 * BS, 2 * BS)
        q, g = q_refs[0][rows, :], g_refs[0][rows, :]
        start = aligned((pos * blocks + 2 * t) * BS)
        span = pl.ds(start, 4 * BS)
        k, v = k_rows[span, :], v_rows[span, :]
        norm = norm_flat[0, 0, :, t * 2 * BS : (t + 1) * 2 * BS]
        rdot = dot_flat[0, 0, :, t * 2 * BS : (t + 1) * 2 * BS]
        first = jnp.where(lane < BS, norm, OFF)
        last = jnp.where(lane < BS, OFF, norm)
        if t == 0:
            first = first + jnp.where(pos > 0, 0.0, OFF)
        if t == pairs - 1:
            last = last + jnp.where(pos < GROUP - 1, 0.0, OFF)
        s = dot(k, q, NT) * c2
        w = jnp.concatenate(
            [
                jnp.exp2(s[:BS] - first),
                jnp.exp2(s[BS : 3 * BS] - norm),
                jnp.exp2(s[3 * BS :] - last),
            ],
            axis=0,
        )
        ds = w * (dot(v, g, NT) - rdot)
        wb, dsb = w.astype(jnp.bfloat16), ds.astype(jnp.bfloat16)
        dq_sum[rows, :] += dot(dsb, k, TN)
        dk_sum[span, :] += dot(dsb, q)
        dv_sum[span, :] += dot(wb, g)

    globs = [local_block(meta[1 + j], group, group_blocks) for j in range(2)]
    wide = 4 * BS if blocks % 4 == 0 else 2 * BS

    @pl.when(globs[0][1] | globs[1][1])
    def _():
        spans = [pl.ds(aligned(BS + p * BS), BS) for p, _ in globs]
        k = jnp.concatenate([k_rows[s, :] for s in spans], axis=0)
        v = jnp.concatenate([v_rows[s, :] for s in spans], axis=0)
        off = [jnp.where(inside, 0.0, OFF) for _, inside in globs]
        dk = jnp.zeros((2 * BS, DH), jnp.float32)
        dv = jnp.zeros((2 * BS, DH), jnp.float32)
        for r in range(sources):
            for t in range(tokens // wide):
                rows = pl.ds(r * tokens + t * wide, wide)
                q, g = q_rows[rows, :], g_rows[rows, :]
                norm = norm_flat[r, 0, :, t * wide : (t + 1) * wide]
                rdot = dot_flat[r, 0, :, t * wide : (t + 1) * wide]
                s = dot(k, q, NT) * c2
                w = jnp.concatenate(
                    [jnp.exp2(s[:BS] - (norm + off[0])), jnp.exp2(s[BS:] - (norm + off[1]))],
                    axis=0,
                )
                ds = w * (dot(v, g, NT) - rdot)
                wb, dsb = w.astype(jnp.bfloat16), ds.astype(jnp.bfloat16)
                dq_sum[rows, :] += dot(dsb, k, TN)
                dk = dk + dot(dsb, q)
                dv = dv + dot(wb, g)
        for j, span in enumerate(spans):
            dk_sum[span, :] += dk[j * BS : (j + 1) * BS]
            dv_sum[span, :] += dv[j * BS : (j + 1) * BS]

    def batch(step, carry):
        found = []
        for u in range(BATCH):
            i = step * BATCH + u
            code = listed[i]
            item = code // group_blocks
            place = code - item * group_blocks
            rows = pl.ds(aligned(item * BS), BS)
            span = pl.ds(aligned(BS + place * BS), BS)
            norm = norm_ref[0, pl.ds(item, 1), :] + jnp.where(i < count, 0.0, OFF)
            rdot = dot_ref[0, pl.ds(item, 1), :]
            found.append(
                (
                    rows,
                    span,
                    terms(
                        q_rows[rows, :], g_rows[rows, :], k_rows[span, :], v_rows[span, :], norm, rdot
                    ),
                )
            )
        for rows, span, (dq, dk, dv) in found:
            dq_sum[rows, :] += dq
            dk_sum[span, :] += dk
            dv_sum[span, :] += dv
        return carry

    lax.fori_loop(0, (count + BATCH - 1) // BATCH, batch, 0)

    dq_own[...] = dq_sum[pl.ds(0, tokens), :] * SCALE
    for r in range(remote):
        dq_far[r][...] = (dq_sum[pl.ds((r + 1) * tokens, tokens), :] * SCALE).astype(jnp.bfloat16)
    for j in range(GROUP):
        rows = pl.ds(aligned(BS + (pos ^ j) * tokens), tokens)
        for total, keep, send, axis, factor in (
            (dk_sum, dk_keep, dk_send, 1, SCALE),
            (dv_sum, dv_keep, dv_send, 2, 1.0),
        ):
            slot = (j >> 1) if axis == 1 else (j & 1)
            target = send if j & axis else keep
            part = total[rows, :]
            part = part * factor if factor != 1.0 else part
            target[slot] = part.astype(jnp.bfloat16)


def on_device(
    queries, key_states, value_states, forward_out, grad_out, random_blocks, global_blocks
):
    seq_count = lax.axis_size("seq")
    me = lax.axis_index("seq")
    tokens = queries.shape[0]
    blocks = tokens // BS
    heads = queries.shape[1] // DH
    sources = seq_count // GROUP
    remote = sources - 1
    sizes = (seq_count, remote, blocks, heads)

    def shift(array, r):
        pairs = [(i, (i + GROUP * r) % seq_count) for i in range(seq_count)]
        return lax.ppermute(array, "seq", pairs)

    def flip(array, j):
        return lax.ppermute(array, "seq", [(i, i ^ j) for i in range(seq_count)])

    def collect(array):
        across = flip(array, 2)
        return [array, flip(array, 1), across, flip(across, 1)]

    k_group = collect(key_states)
    q_all = [queries] + [shift(queries, r) for r in range(1, sources)]
    v_group = collect(value_states)
    g_all = [grad_out] + [shift(grad_out, r) for r in range(1, sources)]

    meta = jnp.concatenate([me.astype(jnp.int32)[None], global_blocks.astype(jnp.int32)])
    table = random_blocks.reshape(-1)

    def column(offset):
        return pl.BlockSpec((tokens, DH), lambda h, *_: (0, h + offset))

    padded_rows = (GROUP * tokens + 2 * BS, DH)
    partial_norms = pl.pallas_call(
        partial(norm_kernel, sizes),
        grid_spec=pltpu.PrefetchScalarGridSpec(
            num_scalar_prefetch=2,
            grid=(heads,),
            in_specs=[column(0)] * (sources + GROUP),
            out_specs=pl.BlockSpec((sources, 1, blocks, BS), lambda h, *_: (0, h, 0, 0)),
            scratch_shapes=[pltpu.VMEM(padded_rows, jnp.bfloat16)],
        ),
        out_shape=jax.ShapeDtypeStruct((sources, heads, blocks, BS), jnp.float32),
        compiler_params=pltpu.CompilerParams(vmem_limit_bytes=48 * 2**20),
        name="partial_norms",
    )(meta, table, *q_all, *k_group)

    row_dot = jnp.sum(
        grad_out.astype(jnp.float32).reshape(tokens, heads, DH)
        * forward_out.astype(jnp.float32).reshape(tokens, heads, DH),
        axis=-1,
    )
    row_dot = row_dot.reshape(blocks, BS, heads).transpose(2, 0, 1)

    mine = jnp.concatenate([partial_norms, row_dot[None]], axis=0)
    told = [mine] + [shift(mine, r) for r in range(1, sources)]
    norms, dots = [], []
    for r in range(sources):
        parts = jnp.stack([told[k][(r - k) % sources] for k in range(sources)])
        top = jnp.max(parts, axis=0)
        norms.append(top + jnp.log2(jnp.sum(jnp.exp2(parts - top), axis=0)))
        dots.append(told[r][sources])
    norms, dots = jnp.stack(norms), jnp.stack(dots)

    def by_item(array):
        return array.transpose(1, 0, 2, 3).reshape(heads, sources * blocks, BS)

    def flat(array):
        return array.reshape(sources, heads, 1, tokens)

    def gradients(head0, count):
        width = count * DH
        item_spec = pl.BlockSpec((1, sources * blocks, BS), lambda h, *_: (h + head0, 0, 0))
        flat_spec = pl.BlockSpec((sources, 1, 1, tokens), lambda h, *_: (0, h + head0, 0, 0))
        out_column = pl.BlockSpec((tokens, DH), lambda h, *_: (0, h))
        half_spec = pl.BlockSpec((GROUP // 2, tokens, DH), lambda h, *_: (0, 0, h))
        half_shape = jax.ShapeDtypeStruct((GROUP // 2, tokens, width), jnp.bfloat16)
        return pl.pallas_call(
            partial(grads_kernel, sizes, head0),
            grid_spec=pltpu.PrefetchScalarGridSpec(
                num_scalar_prefetch=2,
                grid=(count,),
                in_specs=[column(head0)] * (2 * sources + 2 * GROUP)
                + [item_spec] * 2
                + [flat_spec] * 2,
                out_specs=[out_column] * sources + [half_spec] * 4,
                scratch_shapes=[
                    pltpu.VMEM((sources * tokens, DH), jnp.bfloat16),
                    pltpu.VMEM((sources * tokens, DH), jnp.bfloat16),
                    pltpu.VMEM(padded_rows, jnp.bfloat16),
                    pltpu.VMEM(padded_rows, jnp.bfloat16),
                    pltpu.VMEM((sources * tokens, DH), jnp.float32),
                    pltpu.VMEM(padded_rows, jnp.float32),
                    pltpu.VMEM(padded_rows, jnp.float32),
                    pltpu.SMEM((sources * (3 * blocks + 2) + BATCH,), jnp.int32),
                ],
            ),
            out_shape=[jax.ShapeDtypeStruct((tokens, width), jnp.float32)]
            + [jax.ShapeDtypeStruct((tokens, width), jnp.bfloat16)] * remote
            + [half_shape] * 4,
            compiler_params=pltpu.CompilerParams(vmem_limit_bytes=48 * 2**20),
            name="gradients",
        )(
            meta,
            table,
            *q_all,
            *g_all,
            *k_group,
            *v_group,
            by_item(norms),
            by_item(dots),
            flat(norms),
            flat(dots),
        )

    def wide(array):
        return array.astype(jnp.float32)

    def reduced(keep, send, first, second):
        got = flip(send, first)
        onward = flip((wide(keep[1]) + wide(got[1])).astype(jnp.bfloat16), second)
        return (wide(keep[0]) + wide(got[0]) + wide(onward)).astype(jnp.bfloat16)

    def to_tokens(array):
        return lax.all_to_all(array, "head", split_axis=0, concat_axis=1, tiled=True)

    outs = gradients(0, heads)
    dq_own, dq_far = outs[0], outs[1:sources]
    dk_keep, dk_send, dv_keep, dv_send = outs[sources:]
    dk = to_tokens(reduced(dk_keep, dk_send, 1, 2))
    dv = to_tokens(reduced(dv_keep, dv_send, 2, 1))
    dq = dq_own
    for r in range(1, sources):
        dq = dq + wide(shift(dq_far[r - 1], -r))
    dq = to_tokens(dq.astype(jnp.bfloat16))
    return dq, dk, dv


def solution(mesh):
    return jax.shard_map(
        on_device,
        mesh=mesh,
        in_specs=(
            P("seq", "head"),
            P("seq", "head"),
            P("seq", "head"),
            P("seq", "head"),
            P("seq", "head"),
            P(None, "head", None),
            P(),
        ),
        out_specs=(P(("seq", "head"), None), P(("seq", "head"), None), P(("seq", "head"), None)),
        check_vma=False,
    )
```

time: 818 us -> 344 us (0.42); the launches traced: 801 us -> 341 us
  local copies, waits for them, and re-layouts: 210 us -> 6.54 us
  other arithmetic: 132 us -> 17.7 us
  waiting for transfers between devices: 295 us -> 187 us
  Pallas kernels: 0 us -> 81 us
  matrix products: 79.4 us -> 0 us
  starting transfers between devices: 69.4 us -> 47.1 us
  between operations: 15.2 us -> 0.82 us
    psum x2 -> x0, waiting for transfers between devices: 105 us -> none  [the longest x1 105 us: on_device(): glob_kv = lax.psum(picked, 'seq').astype(jnp.float32).astype(jnp.bfloat16)]
    all_to_all x9 -> x3, waiting for transfers between devices: 112 us -> 15.1 us  [to_tokens(): lax.all_to_all(array, 'head', split_axis=0, concat_axis=1, tiled=True)]
    ppermute x4 -> x14, waiting for transfers between devices: 77.6 us -> 172 us  [the longest x10 101 us: flip(): return lax.ppermute(array, 'seq', [(i, i ^ j) for i in range(seq_count)])]
    pallas_call x0 -> x2, Pallas kernels: none -> 81 us  [the longest x1 68.9 us: gradients(): pl.pallas_call(partial(grads_kernel, sizes, head0), grid_spec=pltpu.Prefe...]
    dot_general x45 -> x0, matrix products: 79.4 us -> none  [the longest x8 10.3 us: attend(): jnp.einsum('zxp,zufp->zxuf', gradient_row_block, gathered_value_block, pr...]
    scatter x7 -> x0, local copies, waits for them, and re-layouts: 61 us -> none  [the longest x2 38.5 us: on_device(): jnp.zeros((2, spill_slot, BS, DH), jnp.bfloat16).at[:, send_pos]]
    scatter-add x3 -> x0, other arithmetic: 54.2 us -> none  [the longest x1 49.1 us: on_device(): jnp.zeros((2, blocks * head_count, BS, DH), jnp.float32).at[:, recv_index]]
    all_to_all x9 -> x3, starting transfers between devices: 56.3 us -> 11.6 us  [to_tokens(): lax.all_to_all(array, 'head', split_axis=0, concat_axis=1, tiled=True)]
  transfers between devices with their start and end apart: 15 -> 17, of which waited for: 9 -> 11; matrix products, arithmetic and copies ran while one was open for 26% -> 7% of each run, Pallas kernels for 0% -> 4%
where the time goes in v1:
time: 344 us; the launch traced here: 341 us
  waiting for transfers between devices  187 us (54%)
  Pallas kernels  81 us (24%)
  starting transfers between devices  47.1 us (14%)
  other arithmetic  17.7 us (5%)
  local copies, waits for them, and re-layouts  6.54 us (2%)
    ppermute x10, waiting for transfers between devices, flip(): return lax.ppermute(array, 'seq', [(i, i ^ j) for i in range(seq_count)])  101 us
    ppermute x4, waiting for transfers between devices, shift(): return lax.ppermute(array, 'seq', pairs)  70.8 us
    pallas_call x1, Pallas kernels, gradients(): pl.pallas_call(partial(grads_kernel, sizes, head0), grid_spec=pltpu.Prefe...  68.9 us
    ppermute x10, starting transfers between devices, flip(): return lax.ppermute(array, 'seq', [(i, i ^ j) for i in range(seq_count)])  21.6 us
    all_to_all x3, waiting for transfers between devices, to_tokens(): lax.all_to_all(array, 'head', split_axis=0, concat_axis=1, tiled=True)  15.1 us
    ppermute x4, starting transfers between devices, shift(): return lax.ppermute(array, 'seq', pairs)  13.9 us
    pallas_call x1, Pallas kernels, on_device(): pl.pallas_call(partial(norm_kernel, sizes), grid_spec=pltpu.PrefetchScala...  12.1 us
    all_to_all x3, starting transfers between devices, to_tokens(): lax.all_to_all(array, 'head', split_axis=0, concat_axis=1, tiled=True)  11.6 us
  transfers between devices with their start and end apart: 17, of which 11 were waited for; matrix products, arithmetic and copies ran while one was open for 7% of the time, Pallas kernels for 4%

profile of v1, /device:TPU:8, one launch (start us, length us, event | category | flops | bytes accessed | tf_op | source)
XLA Modules:
  0.0 340.5 jit_solution(10764505755293477976)
XLA Ops:
  0.7 1.9 collective-permute-start.2
  2.6 2.6 collective-permute-start
  5.2 39.6 %collective-permute-done.3.refs_4_.refs_6_ = bf16[512,1024]{1,0:T(8,128)(2,1)S(1)} collective-permute-done((bf16[512,1024]{1,0:T(8,128)(2,1)}, bf16[512,1024]{1,0:T(8,128)(2,1)S(1)}, u32[]{:S(2)}, u32[]{:S(2)}) %collective-permute-start.3) | collective-permute-done | bytes 1048608 | tf_op jit(solution)/shard_map/ppermute | solution.py:308
  44.9 2.6 collective-permute-start.4
  47.5 2.4 collective-permute-start.6
  50.9 1.9 multiply_bitcast_fusion
  52.9 1.8 copy.32
  54.7 2.4 reduce_sum.27
  57.2 12.6 %collective-permute-done.4.refs_5_.refs_7_ = bf16[512,1024]{1,0:T(8,128)(2,1)} collective-permute-done((bf16[512,1024]{1,0:T(8,128)(2,1)S(1)}, bf16[512,1024]{1,0:T(8,128)(2,1)}, u32[]{:S(2)}, u32[]{:S(2)}) %collective-permute-start.4) | collective-permute-done | bytes 1048608 | tf_op jit(solution)/shard_map/ppermute | solution.py:308
  69.9 12.1 %partial_norms.1 = f32[2,8,8,64]{3,2,1,0:T(8,128)S(1)} custom-call(s32[3]{0:T(128)S(1)} %pad_add_fusion.meta, s32[1536]{0:T(1024)S(1)} %reshape.81.table, bf16[512,1024]{1,0:T(8,128)(2,1)S(1)} %copy-done, bf16[512,1024]{1,0:T(8,128)(2,1)} %collective-permute-done.refs_1_, bf16[512,1024]{1,0:T(8,128)(2,1)S(1)} %copy-done.1, ...), custom_call_target="tpu_custom_call" | custom-call | tf_op jit(solution)/shard_map/partial_norms/pallas_call | solution.py:326
  82.0 3.6 %collective-permute-start.8 = (f32[3,8,8,64]{3,2,1,0:T(8,128)S(1)}, f32[3,8,8,64]{3,2,1,0:T(8,128)S(1)}, u32[]{:S(2)}, u32[]{:S(2)}) collective-permute-start(f32[3,8,8,64]{3,2,1,0:T(8,128)S(1)} %pad_maximum_fusion), channel_id=1, source_target_pairs={{0,16},{4,20},{8,24},{12,28},{16,0},{20,4},{24,8},{28,12},{1,17},{... | collective-permute-start | bytes 147464 | tf_op jit(solution)/shard_map/ppermute | solution.py:305
  85.5 1.7 collective-permute-start.5
  87.7 23.6 %collective-permute-done.8 = f32[3,8,8,64]{3,2,1,0:T(8,128)S(1)} collective-permute-done((f32[3,8,8,64]{3,2,1,0:T(8,128)S(1)}, f32[3,8,8,64]{3,2,1,0:T(8,128)S(1)}, u32[]{:S(2)}, u32[]{:S(2)}) %collective-permute-start.8) | collective-permute-done | bytes 49184 | tf_op jit(solution)/shard_map/ppermute | solution.py:305
  111.8 20.8 %collective-permute-done.1.refs_3_ = bf16[512,1024]{1,0:T(8,128)(2,1)S(1)} collective-permute-done((bf16[512,1024]{1,0:T(8,128)(2,1)}, bf16[512,1024]{1,0:T(8,128)(2,1)S(1)}, u32[]{:S(2)}, u32[]{:S(2)}) %collective-permute-start.1) | collective-permute-done | bytes 1048608 | tf_op jit(solution)/shard_map/ppermute | solution.py:305
  132.7 68.9 %gradients.1 = (f32[512,1024]{1,0:T(8,128)}, bf16[512,1024]{1,0:T(8,128)(2,1)S(1)}, bf16[2,512,1024]{2,1,0:T(8,128)(2,1)}, bf16[2,512,1024]{2,1,0:T(8,128)(2,1)}...) custom-call(s32[3]{0:T(128)S(1)} %pad_add_fusion.meta, s32[1536]{0:T(1024)S(1)} %reshape.81.table, ...), custom_call_target="tpu_custom_call" | custom-call | tf_op jit(solution)/shard_map/gradients/pallas_call | solution.py:370
  201.7 4.6 %collective-permute-start.12 = (bf16[2,512,1024]{2,1,0:T(8,128)(2,1)}, bf16[2,512,1024]{2,1,0:T(8,128)(2,1)}, u32[]{:S(2)}, u32[]{:S(2)}) collective-permute-start(bf16[2,512,1024]{2,1,0:T(8,128)(2,1)} %get-tuple-element.14), channel_id=1, source_target_pairs={{0,8},{4,12},{8,0},{12,4},{16,24},{20,28},{24,16},{28,20},{1,9},{5... | collective-permute-start | bytes 6291464 | tf_op jit(solution)/shard_map/ppermute | solution.py:308
  206.3 7.7 %collective-permute-start.9 = (bf16[512,1024]{1,0:T(8,128)(2,1)S(1)}, bf16[512,1024]{1,0:T(8,128)(2,1)S(1)}, u32[]{:S(2)}, u32[]{:S(2)}) collective-permute-start(bf16[512,1024]{1,0:T(8,128)(2,1)S(1)} %get-tuple-element.10), channel_id=1, source_target_pairs={{0,16},{4,20},{8,24},{12,28},{16,0},{20,4},{24,8},{28,12},{1,17},{... | collective-permute-start | bytes 3145736 | tf_op jit(solution)/shard_map/ppermute | solution.py:305
  213.9 32.6 %collective-permute-done.10 = bf16[2,512,1024]{2,1,0:T(8,128)(2,1)S(1)} collective-permute-done((bf16[2,512,1024]{2,1,0:T(8,128)(2,1)}, bf16[2,512,1024]{2,1,0:T(8,128)(2,1)S(1)}, u32[]{:S(2)}, u32[]{:S(2)}) %collective-permute-start.10) | collective-permute-done | bytes 2097184 | tf_op jit(solution)/shard_map/ppermute | solution.py:308
  246.6 2.3 fusion.2
  248.9 7.9 %collective-permute-start.11 = (bf16[512,1024]{1,0:T(8,128)(2,1)S(1)}, bf16[512,1024]{1,0:T(8,128)(2,1)}, u32[]{:S(2)}, u32[]{:S(2)}) collective-permute-start(bf16[512,1024]{1,0:T(8,128)(2,1)S(1)} %fusion.2), channel_id=1, source_target_pairs={{0,8},{4,12},{8,0},{12,4},{16,24},{20,28},{24,16},{28,20},{1,9},{5... | collective-permute-start | bytes 3145736 | tf_op jit(solution)/shard_map/ppermute | solution.py:308
  256.8 26.4 %collective-permute-done.9 = bf16[512,1024]{1,0:T(8,128)(2,1)S(1)} collective-permute-done((bf16[512,1024]{1,0:T(8,128)(2,1)S(1)}, bf16[512,1024]{1,0:T(8,128)(2,1)S(1)}, u32[]{:S(2)}, u32[]{:S(2)}) %collective-permute-start.9) | collective-permute-done | bytes 1048608 | tf_op jit(solution)/shard_map/ppermute | solution.py:305
  283.2 1.4 add_convert_fusion.2
  284.5 4.5 %all-to-all-start = ((bf16[4,128,1024]{2,1,0:T(8,128)(2,1)}), bf16[4,128,1024]{2,1,0:T(8,128)(2,1)S(1)}, u32[]{:S(2)}, u32[]{:S(2)}) async-start(bf16[4,128,1024]{2,1,0:T(8,128)(2,1)} %bitcast.13), calls=%async_computation | async-start | bytes 2097152 | tf_op jit(solution)/shard_map/all_to_all | solution.py:417
  289.1 3.1 fusion.3
  292.2 5.6 %collective-permute-done.11 = bf16[512,1024]{1,0:T(8,128)(2,1)} collective-permute-done((bf16[512,1024]{1,0:T(8,128)(2,1)S(1)}, bf16[512,1024]{1,0:T(8,128)(2,1)}, u32[]{:S(2)}, u32[]{:S(2)}) %collective-permute-start.11) | collective-permute-done | bytes 1048608 | tf_op jit(solution)/shard_map/ppermute | solution.py:308
  297.8 3.0 fusion.1
  300.8 2.8 all-to-all-done
  303.5 3.5 %all-to-all-start.1 = ((bf16[4,128,1024]{2,1,0:T(8,128)(2,1)}), bf16[4,128,1024]{2,1,0:T(8,128)(2,1)S(1)}, u32[]{:S(2)}, u32[]{:S(2)}) async-start(bf16[4,128,1024]{2,1,0:T(8,128)(2,1)} %bitcast.17), calls=%async_computation.1 | async-start | bytes 2097152 | tf_op jit(solution)/shard_map/all_to_all | solution.py:417
  307.1 11.0 %collective-permute-done.13 = bf16[512,1024]{1,0:T(8,128)(2,1)} collective-permute-done((bf16[512,1024]{1,0:T(8,128)(2,1)}, bf16[512,1024]{1,0:T(8,128)(2,1)}, u32[]{:S(2)}, u32[]{:S(2)}) %collective-permute-start.13) | collective-permute-done | bytes 1048608 | tf_op jit(solution)/shard_map/ppermute | solution.py:308
  318.0 3.5 %fusion = bf16[512,1024]{1,0:T(8,128)(2,1)} fusion(bf16[512,1024]{1,0:T(8,128)(2,1)} %collective-permute-done.13, bf16[2,512,1024]{2,1,0:T(8,128)(2,1)} %collective-permute-done.12, bf16[2,512,1024]{2,1,0:T(8,128)(2,1)} %get-tuple-element.13), kind=kLoop, calls=%fused_computation.1 | loop fusion | flops 3145728 | bytes 4194304 | tf_op jit(solution)/shard_map/convert_element_type | solution.py:414
  321.5 3.5 %all-to-all-start.2 = ((bf16[4,128,1024]{2,1,0:T(8,128)(2,1)}), bf16[4,128,1024]{2,1,0:T(8,128)(2,1)S(1)}, u32[]{:S(2)}, u32[]{:S(2)}) async-start(bf16[4,128,1024]{2,1,0:T(8,128)(2,1)} %bitcast.60), calls=%async_computation.2 | async-start | bytes 2097152 | tf_op jit(solution)/shard_map/all_to_all | solution.py:417
  327.2 12.3 %all-to-all-done.2 = bf16[4,128,1024]{2,1,0:T(8,128)(2,1)S(1)} async-done(((bf16[4,128,1024]{2,1,0:T(8,128)(2,1)}), bf16[4,128,1024]{2,1,0:T(8,128)(2,1)S(1)}, u32[]{:S(2)}, u32[]{:S(2)}) %all-to-all-start.2) | async-done | bytes 1048608 | tf_op jit(solution)/shard_map/all_to_all | solution.py:417
  (47 shorter events, 5.7 us)
Async XLA Ops:
  0.6 44.2 %collective-permute-start.3 = (bf16[512,1024]{1,0:T(8,128)(2,1)}, bf16[512,1024]{1,0:T(8,128)(2,1)S(1)}, u32[]{:S(2)}, u32[]{:S(2)}) collective-permute-start(bf16[512,1024]{1,0:T(8,128)(2,1)} %refs_4_.1), channel_id=1, source_target_pairs={{0,8},{4,12},{8,0},{12,4},{16,24},{20,28},{24,16},{28,20},{1,9},{5... | collective-permute-start | bytes 3145736 | tf_op jit(solution)/shard_map/ppermute | solution.py:308
  0.7 56.5 %collective-permute-start.2 = (bf16[512,1024]{1,0:T(8,128)(2,1)}, bf16[512,1024]{1,0:T(8,128)(2,1)}, u32[]{:S(2)}, u32[]{:S(2)}) collective-permute-start(bf16[512,1024]{1,0:T(8,128)(2,1)} %refs_4_.1), channel_id=1, source_target_pairs={{0,4},{4,0},{8,12},{12,8},{16,20},{20,16},{24,28},{28,24},{1,5},{5... | collective-permute-start | bytes 3145736 | tf_op jit(solution)/shard_map/ppermute | solution.py:308
  2.6 54.6 %collective-permute-start = (bf16[512,1024]{1,0:T(8,128)(2,1)}, bf16[512,1024]{1,0:T(8,128)(2,1)}, u32[]{:S(2)}, u32[]{:S(2)}) collective-permute-start(bf16[512,1024]{1,0:T(8,128)(2,1)} %refs_0_.3), channel_id=1, source_target_pairs={{0,16},{4,20},{8,24},{12,28},{16,0},{20,4},{24,8},{28,12},{1,17},{... | collective-permute-start | bytes 3145736 | tf_op jit(solution)/shard_map/ppermute | solution.py:305
  44.9 25.0 %copy-start.2 = (bf16[512,1024]{1,0:T(8,128)(2,1)}, bf16[512,1024]{1,0:T(8,128)(2,1)S(1)}, u32[]{:S(2)}) copy-start(bf16[512,1024]{1,0:T(8,128)(2,1)S(1)} %collective-permute-done.3.refs_4_.refs_6_) | copy-start | bytes 3145732
  44.9 25.0 %collective-permute-start.4 = (bf16[512,1024]{1,0:T(8,128)(2,1)S(1)}, bf16[512,1024]{1,0:T(8,128)(2,1)}, u32[]{:S(2)}, u32[]{:S(2)}) collective-permute-start(bf16[512,1024]{1,0:T(8,128)(2,1)S(1)} %collective-permute-done.3.refs_4_.refs_6_), channel_id=1, source_target_pairs={{0,4},{4,0},{8,12},{12,8},{16,20},{20,16},{24,28},{28,24},{1,5},{5... | collective-permute-start | bytes 3145736 | tf_op jit(solution)/shard_map/ppermute | solution.py:308
  47.5 39.9 %collective-permute-start.6 = (bf16[512,1024]{1,0:T(8,128)(2,1)}, bf16[512,1024]{1,0:T(8,128)(2,1)}, u32[]{:S(2)}, u32[]{:S(2)}) collective-permute-start(bf16[512,1024]{1,0:T(8,128)(2,1)} %refs_8_.1), channel_id=1, source_target_pairs={{0,8},{4,12},{8,0},{12,4},{16,24},{20,28},{24,16},{28,20},{1,9},{5... | collective-permute-start | bytes 3145736 | tf_op jit(solution)/shard_map/ppermute | solution.py:308
  54.7 2.5 copy-start.7
  54.7 15.2 %copy-start = (bf16[512,1024]{1,0:T(8,128)(2,1)S(1)}, bf16[512,1024]{1,0:T(8,128)(2,1)}, u32[]{:S(2)}) copy-start(bf16[512,1024]{1,0:T(8,128)(2,1)} %refs_0_.3) | copy-start | bytes 3145732
  54.7 15.2 %copy-start.1 = (bf16[512,1024]{1,0:T(8,128)(2,1)S(1)}, bf16[512,1024]{1,0:T(8,128)(2,1)}, u32[]{:S(2)}) copy-start(bf16[512,1024]{1,0:T(8,128)(2,1)} %refs_4_.1) | copy-start | bytes 3145732
  82.0 29.3 %collective-permute-start.8 = (f32[3,8,8,64]{3,2,1,0:T(8,128)S(1)}, f32[3,8,8,64]{3,2,1,0:T(8,128)S(1)}, u32[]{:S(2)}, u32[]{:S(2)}) collective-permute-start(f32[3,8,8,64]{3,2,1,0:T(8,128)S(1)} %pad_maximum_fusion), channel_id=1, source_target_pairs={{0,16},{4,20},{8,24},{12,28},{16,0},{20,4},{24,8},{28,12},{1,17},{... | collective-permute-start | bytes 147464 | tf_op jit(solution)/shard_map/ppermute | solution.py:305
  85.5 26.3 %collective-permute-start.5 = (bf16[512,1024]{1,0:T(8,128)(2,1)}, bf16[512,1024]{1,0:T(8,128)(2,1)S(1)}, u32[]{:S(2)}, u32[]{:S(2)}) collective-permute-start(bf16[512,1024]{1,0:T(8,128)(2,1)} %refs_8_.1), channel_id=1, source_target_pairs={{0,4},{4,0},{8,12},{12,8},{16,20},{20,16},{24,28},{28,24},{1,5},{5... | collective-permute-start | bytes 3145736 | tf_op jit(solution)/shard_map/ppermute | solution.py:308
  87.3 45.4 %collective-permute-start.1 = (bf16[512,1024]{1,0:T(8,128)(2,1)}, bf16[512,1024]{1,0:T(8,128)(2,1)S(1)}, u32[]{:S(2)}, u32[]{:S(2)}) collective-permute-start(bf16[512,1024]{1,0:T(8,128)(2,1)} %refs_2_.3), channel_id=1, source_target_pairs={{0,16},{4,20},{8,24},{12,28},{16,0},{20,4},{24,8},{28,12},{1,17},{... | collective-permute-start | bytes 3145736 | tf_op jit(solution)/shard_map/ppermute | solution.py:305
  87.3 45.3 %collective-permute-start.7 = (bf16[512,1024]{1,0:T(8,128)(2,1)}, bf16[512,1024]{1,0:T(8,128)(2,1)}, u32[]{:S(2)}, u32[]{:S(2)}) collective-permute-start(bf16[512,1024]{1,0:T(8,128)(2,1)} %collective-permute-done.6.refs_10_), channel_id=1, source_target_pairs={{0,4},{4,0},{8,12},{12,8},{16,20},{20,16},{24,28},{28,24},{1,5},{5... | collective-permute-start | bytes 3145736 | tf_op jit(solution)/shard_map/ppermute | solution.py:308
  111.8 20.8 %copy-start.6 = (bf16[512,1024]{1,0:T(8,128)(2,1)}, bf16[512,1024]{1,0:T(8,128)(2,1)S(1)}, u32[]{:S(2)}) copy-start(bf16[512,1024]{1,0:T(8,128)(2,1)S(1)} %collective-permute-done.5.refs_9_) | copy-start | bytes 3145732
  201.6 81.6 %copy-start.5 = (f32[512,1024]{1,0:T(8,128)S(1)}, f32[512,1024]{1,0:T(8,128)}, u32[]{:S(2)}) copy-start(f32[512,1024]{1,0:T(8,128)} %get-tuple-element.9) | copy-start | bytes 6291460
  201.6 45.0 %collective-permute-start.10 = (bf16[2,512,1024]{2,1,0:T(8,128)(2,1)}, bf16[2,512,1024]{2,1,0:T(8,128)(2,1)S(1)}, u32[]{:S(2)}, u32[]{:S(2)}) collective-permute-start(bf16[2,512,1024]{2,1,0:T(8,128)(2,1)} %get-tuple-element.12), channel_id=1, source_target_pairs={{0,4},{4,0},{8,12},{12,8},{16,20},{20,16},{24,28},{28,24},{1,5},{5... | collective-permute-start | bytes 6291464 | tf_op jit(solution)/shard_map/ppermute | solution.py:308
  201.7 87.4 %collective-permute-start.12 = (bf16[2,512,1024]{2,1,0:T(8,128)(2,1)}, bf16[2,512,1024]{2,1,0:T(8,128)(2,1)}, u32[]{:S(2)}, u32[]{:S(2)}) collective-permute-start(bf16[2,512,1024]{2,1,0:T(8,128)(2,1)} %get-tuple-element.14), channel_id=1, source_target_pairs={{0,8},{4,12},{8,0},{12,4},{16,24},{20,28},{24,16},{28,20},{1,9},{5... | collective-permute-start | bytes 6291464 | tf_op jit(solution)/shard_map/ppermute | solution.py:308
  206.3 76.9 %collective-permute-start.9 = (bf16[512,1024]{1,0:T(8,128)(2,1)S(1)}, bf16[512,1024]{1,0:T(8,128)(2,1)S(1)}, u32[]{:S(2)}, u32[]{:S(2)}) collective-permute-start(bf16[512,1024]{1,0:T(8,128)(2,1)S(1)} %get-tuple-element.10), channel_id=1, source_target_pairs={{0,16},{4,20},{8,24},{12,28},{16,0},{20,4},{24,8},{28,12},{1,17},{... | collective-permute-start | bytes 3145736 | tf_op jit(solution)/shard_map/ppermute | solution.py:305
  246.6 38.0 %copy-start.4 = (bf16[2,512,1024]{2,1,0:T(8,128)(2,1)}, bf16[2,512,1024]{2,1,0:T(8,128)(2,1)S(1)}, u32[]{:S(2)}) copy-start(bf16[2,512,1024]{2,1,0:T(8,128)(2,1)S(1)} %collective-permute-done.10) | copy-start | bytes 6291460
  248.9 48.9 %collective-permute-start.11 = (bf16[512,1024]{1,0:T(8,128)(2,1)S(1)}, bf16[512,1024]{1,0:T(8,128)(2,1)}, u32[]{:S(2)}, u32[]{:S(2)}) collective-permute-start(bf16[512,1024]{1,0:T(8,128)(2,1)S(1)} %fusion.2), channel_id=1, source_target_pairs={{0,8},{4,12},{8,0},{12,4},{16,24},{20,28},{24,16},{28,20},{1,9},{5... | collective-permute-start | bytes 3145736 | tf_op jit(solution)/shard_map/ppermute | solution.py:308
  284.5 19.0 %all-to-all-start = ((bf16[4,128,1024]{2,1,0:T(8,128)(2,1)}), bf16[4,128,1024]{2,1,0:T(8,128)(2,1)S(1)}, u32[]{:S(2)}, u32[]{:S(2)}) async-start(bf16[4,128,1024]{2,1,0:T(8,128)(2,1)} %bitcast.13), calls=%async_computation | async-start | bytes 2097152 | tf_op jit(solution)/shard_map/all_to_all | solution.py:417
  289.1 8.7 %copy-start.3 = (bf16[2,512,1024]{2,1,0:T(8,128)(2,1)S(1)}, bf16[2,512,1024]{2,1,0:T(8,128)(2,1)}, u32[]{:S(2)}) copy-start(bf16[2,512,1024]{2,1,0:T(8,128)(2,1)} %get-tuple-element.11) | copy-start | bytes 6291460
  292.1 25.9 %collective-permute-start.13 = (bf16[512,1024]{1,0:T(8,128)(2,1)}, bf16[512,1024]{1,0:T(8,128)(2,1)}, u32[]{:S(2)}, u32[]{:S(2)}) collective-permute-start(bf16[512,1024]{1,0:T(8,128)(2,1)} %fusion.3), channel_id=1, source_target_pairs={{0,4},{4,0},{8,12},{12,8},{16,20},{20,16},{24,28},{28,24},{1,5},{5... | collective-permute-start | bytes 3145736 | tf_op jit(solution)/shard_map/ppermute | solution.py:308
  303.5 18.0 %all-to-all-start.1 = ((bf16[4,128,1024]{2,1,0:T(8,128)(2,1)}), bf16[4,128,1024]{2,1,0:T(8,128)(2,1)S(1)}, u32[]{:S(2)}, u32[]{:S(2)}) async-start(bf16[4,128,1024]{2,1,0:T(8,128)(2,1)} %bitcast.17), calls=%async_computation.1 | async-start | bytes 2097152 | tf_op jit(solution)/shard_map/all_to_all | solution.py:417
  321.5 18.0 %all-to-all-start.2 = ((bf16[4,128,1024]{2,1,0:T(8,128)(2,1)}), bf16[4,128,1024]{2,1,0:T(8,128)(2,1)S(1)}, u32[]{:S(2)}, u32[]{:S(2)}) async-start(bf16[4,128,1024]{2,1,0:T(8,128)(2,1)} %bitcast.60), calls=%async_computation.2 | async-start | bytes 2097152 | tf_op jit(solution)/shard_map/all_to_all | solution.py:417

commit v2 on v1

--- a/solution.py
+++ b/solution.py
@@ -12,6 +12,8 @@
 BS = 64
 GROUP = 4
 BATCH = 8
+CHUNKS = 2
+JOINED = 4
 LOG2E = math.log2(math.e)
 SCALE = DH**-0.5
 OFF = 1e30
@@ -159,7 +161,8 @@
     count = jnp.int32(0)
 
     def note(count, item, place, inside):
-        listed[count] = item * group_blocks + place
+        listed[0, count] = item
+        listed[1, count] = place
         return count + inside.astype(jnp.int32)
 
     for r in range(sources):
@@ -174,13 +177,8 @@
                 if found is not None:
                     count = note(count, item, *found)
     for u in range(BATCH):
-        listed[count + u] = 0
-
-    def terms(q, g, k, v, norm, rdot):
-        w = jnp.exp2(dot(k, q, NT) * c2 - norm)
-        ds = w * (dot(v, g, NT) - rdot)
-        wb, dsb = w.astype(jnp.bfloat16), ds.astype(jnp.bfloat16)
-        return dot(dsb, k, TN), dot(dsb, q), dot(wb, g)
+        listed[0, count + u] = 0
+        listed[1, count + u] = 0
 
     lane = lax.broadcasted_iota(jnp.int32, (1, 2 * BS), 1)
     pairs = blocks // 2
@@ -245,29 +243,49 @@
             dv_sum[span, :] += dv[j * BS : (j + 1) * BS]
 
     def batch(step, carry):
-        found = []
-        for u in range(BATCH):
-            i = step * BATCH + u
-            code = listed[i]
-            item = code // group_blocks
-            place = code - item * group_blocks
-            rows = pl.ds(aligned(item * BS), BS)
-            span = pl.ds(aligned(BS + place * BS), BS)
-            norm = norm_ref[0, pl.ds(item, 1), :] + jnp.where(i < count, 0.0, OFF)
-            rdot = dot_ref[0, pl.ds(item, 1), :]
-            found.append(
-                (
-                    rows,
-                    span,
-                    terms(
-                        q_rows[rows, :], g_rows[rows, :], k_rows[span, :], v_rows[span, :], norm, rdot
-                    ),
+        done = []
+        for first in range(0, BATCH, JOINED):
+            rows, spans, norms, dots = [], [], [], []
+            for u in range(first, first + JOINED):
+                i = step * BATCH + u
+                item = listed[0, i]
+                rows.append(pl.ds(aligned(item * BS), BS))
+                spans.append(pl.ds(aligned(BS + listed[1, i] * BS), BS))
+                norms.append(norm_ref[0, pl.ds(item, 1), :] + jnp.where(i < count, 0.0, OFF))
+                dots.append(dot_ref[0, pl.ds(item, 1), :])
+            q = jnp.concatenate([q_rows[x, :] for x in rows], axis=0)
+            g = jnp.concatenate([g_rows[x, :] for x in rows], axis=0)
+            k = jnp.concatenate([k_rows[x, :] for x in spans], axis=0)
+            v = jnp.concatenate([v_rows[x, :] for x in spans], axis=0)
+            s, dw = dot(k, q, NT), dot(v, g, NT)
+            w_diag, ds_diag = [], []
+            for t in range(JOINED // 2):
+                part = slice(t * 2 * BS, (t + 1) * 2 * BS)
+                both = s[part, part] * c2
+                w = jnp.concatenate(
+                    [
+                        jnp.exp2(both[:BS] - jnp.where(lane < BS, norms[2 * t], OFF)),
+                        jnp.exp2(both[BS:] - jnp.where(lane < BS, OFF, norms[2 * t + 1])),
+                    ],
+                    axis=0,
                 )
-            )
-        for rows, span, (dq, dk, dv) in found:
-            dq_sum[rows, :] += dq
-            dk_sum[span, :] += dk
-            dv_sum[span, :] += dv
+                ds = w * (dw[part, part] - jnp.where(lane < BS, dots[2 * t], dots[2 * t + 1]))
+                w_diag.append(w.astype(jnp.bfloat16))
+                ds_diag.append(ds.astype(jnp.bfloat16))
+
+            def each(left, right, dims=(((1,), (0,)), ((), ()))):
+                pieces = [
+                    dot(x, right[t * 2 * BS : (t + 1) * 2 * BS], dims) for t, x in enumerate(left)
+                ]
+                return jnp.concatenate(pieces, axis=0)
+
+            done.append((rows, spans, each(ds_diag, k, TN), each(ds_diag, q), each(w_diag, g)))
+        for rows, spans, dq, dk, dv in done:
+            for u in range(JOINED):
+                part = slice(u * BS, (u + 1) * BS)
+                dq_sum[rows[u], :] += dq[part]
+                dk_sum[spans[u], :] += dk[part]
+                dv_sum[spans[u], :] += dv[part]
         return carry
 
     lax.fori_loop(0, (count + BATCH - 1) // BATCH, batch, 0)
@@ -355,14 +373,15 @@
     norms, dots = jnp.stack(norms), jnp.stack(dots)
 
     def by_item(array):
-        return array.transpose(1, 0, 2, 3).reshape(heads, sources * blocks, BS)
+        array = array.transpose(1, 0, 2, 3).reshape(heads, sources * blocks, BS)
+        return jnp.concatenate([array, array], axis=-1)
 
     def flat(array):
         return array.reshape(sources, heads, 1, tokens)
 
     def gradients(head0, count):
         width = count * DH
-        item_spec = pl.BlockSpec((1, sources * blocks, BS), lambda h, *_: (h + head0, 0, 0))
+        item_spec = pl.BlockSpec((1, sources * blocks, 2 * BS), lambda h, *_: (h + head0, 0, 0))
         flat_spec = pl.BlockSpec((sources, 1, 1, tokens), lambda h, *_: (0, h + head0, 0, 0))
         out_column = pl.BlockSpec((tokens, DH), lambda h, *_: (0, h))
         half_spec = pl.BlockSpec((GROUP // 2, tokens, DH), lambda h, *_: (0, 0, h))
@@ -384,7 +403,7 @@
                     pltpu.VMEM((sources * tokens, DH), jnp.float32),
                     pltpu.VMEM(padded_rows, jnp.float32),
                     pltpu.VMEM(padded_rows, jnp.float32),
-                    pltpu.SMEM((sources * (3 * blocks + 2) + BATCH,), jnp.int32),
+                    pltpu.SMEM((2, sources * (3 * blocks + 2) + BATCH), jnp.int32),
                 ],
             ),
             out_shape=[jax.ShapeDtypeStruct((tokens, width), jnp.float32)]
@@ -416,15 +435,20 @@
     def to_tokens(array):
         return lax.all_to_all(array, "head", split_axis=0, concat_axis=1, tiled=True)
 
-    outs = gradients(0, heads)
-    dq_own, dq_far = outs[0], outs[1:sources]
-    dk_keep, dk_send, dv_keep, dv_send = outs[sources:]
-    dk = to_tokens(reduced(dk_keep, dk_send, 1, 2))
-    dv = to_tokens(reduced(dv_keep, dv_send, 2, 1))
-    dq = dq_own
-    for r in range(1, sources):
-        dq = dq + wide(shift(dq_far[r - 1], -r))
-    dq = to_tokens(dq.astype(jnp.bfloat16))
+    count = heads // CHUNKS
+    dq_parts, dk_parts, dv_parts = [], [], []
+    for c in range(CHUNKS):
+        outs = gradients(c * count, count)
+        dq, dq_far = outs[0], outs[1:sources]
+        dk_keep, dk_send, dv_keep, dv_send = outs[sources:]
+        for r in range(1, sources):
+            dq = dq + wide(shift(dq_far[r - 1], -r))
+        dq_parts.append(dq.astype(jnp.bfloat16))
+        dk_parts.append(reduced(dk_keep, dk_send, 1, 2))
+        dv_parts.append(reduced(dv_keep, dv_send, 2, 1))
+    dq, dk, dv = (
+        to_tokens(jnp.concatenate(parts, axis=1)) for parts in (dq_parts, dk_parts, dv_parts)
+    )
     return dq, dk, dv
 
 

time: 344 us -> 286 us (0.83)
  waiting for transfers between devices: 187 us -> 152 us
  Pallas kernels: 81 us -> 54.8 us
    ppermute x4 -> x5, waiting for transfers between devices: 70.8 us -> 21 us  [shift(): return lax.ppermute(array, 'seq', pairs)]
    pallas_call x1 -> x2, Pallas kernels: 68.9 us -> 42.8 us  [gradients(): pl.pallas_call(partial(grads_kernel, sizes, head0), grid_spec=pltpu.Prefe...]
    ppermute x10 -> x14, waiting for transfers between devices: 101 us -> 109 us  [flip(): return lax.ppermute(array, 'seq', [(i, i ^ j) for i in range(seq_count)])]
    ppermute x10 -> x14, starting transfers between devices: 21.6 us -> 14.1 us  [flip(): return lax.ppermute(array, 'seq', [(i, i ^ j) for i in range(seq_count)])]
    ppermute x4 -> x5, starting transfers between devices: 13.9 us -> 21 us  [shift(): return lax.ppermute(array, 'seq', pairs)]
    all_to_all x3, waiting for transfers between devices: 15.1 us -> 21.6 us  [to_tokens(): lax.all_to_all(array, 'head', split_axis=0, concat_axis=1, tiled=True)]
    concatenate x0 -> x5, other arithmetic: none -> 3.49 us  [the longest x3 3.32 us: on_device(): jnp.concatenate(parts, axis=1)]
  transfers between devices with their start and end apart: 17 -> 22, of which waited for: 11 -> 12; matrix products, arithmetic and copies ran while one was open for 7% -> 9% of each run, Pallas kernels for 4% -> 12%
where the time goes in v2:
time: 286 us; the launch traced here: 284 us
  waiting for transfers between devices  152 us (53%)
  Pallas kernels  54.8 us (19%)
  starting transfers between devices  47.8 us (17%)
  other arithmetic  20 us (7%)
  local copies, waits for them, and re-layouts  8.79 us (3%)
    ppermute x14, waiting for transfers between devices, flip(): return lax.ppermute(array, 'seq', [(i, i ^ j) for i in range(seq_count)])  109 us
    pallas_call x2, Pallas kernels, gradients(): pl.pallas_call(partial(grads_kernel, sizes, head0), grid_spec=pltpu.Prefe...  42.8 us
    all_to_all x3, waiting for transfers between devices, to_tokens(): lax.all_to_all(array, 'head', split_axis=0, concat_axis=1, tiled=True)  21.6 us
    ppermute x5, waiting for transfers between devices, shift(): return lax.ppermute(array, 'seq', pairs)  21 us
    ppermute x5, starting transfers between devices, shift(): return lax.ppermute(array, 'seq', pairs)  21 us
    ppermute x14, starting transfers between devices, flip(): return lax.ppermute(array, 'seq', [(i, i ^ j) for i in range(seq_count)])  14.1 us
    all_to_all x3, starting transfers between devices, to_tokens(): lax.all_to_all(array, 'head', split_axis=0, concat_axis=1, tiled=True)  12.7 us
    pallas_call x1, Pallas kernels, on_device(): pl.pallas_call(partial(norm_kernel, sizes), grid_spec=pltpu.PrefetchScala...  12 us
  transfers between devices with their start and end apart: 22, of which 12 were waited for; matrix products, arithmetic and copies ran while one was open for 9% of the time, Pallas kernels for 12%

profile of v2, /device:TPU:8, one launch (start us, length us, event | category | flops | bytes accessed | tf_op | source)
XLA Modules:
  0.0 284.2 jit_solution(14850929889904146487)
XLA Ops:
  0.7 3.0 %collective-permute-start = (bf16[512,1024]{1,0:T(8,128)(2,1)}, bf16[512,1024]{1,0:T(8,128)(2,1)}, u32[]{:S(2)}, u32[]{:S(2)}) collective-permute-start(bf16[512,1024]{1,0:T(8,128)(2,1)} %refs_0_.5), channel_id=1, source_target_pairs={{0,16},{4,20},{8,24},{12,28},{16,0},{20,4},{24,8},{28,12},{1,17},{... | collective-permute-start | bytes 3145736 | tf_op jit(solution)/shard_map/ppermute | solution.py:323
  5.2 40.8 %collective-permute-done.3.refs_4_.refs_6_ = bf16[512,1024]{1,0:T(8,128)(2,1)S(1)} collective-permute-done((bf16[512,1024]{1,0:T(8,128)(2,1)}, bf16[512,1024]{1,0:T(8,128)(2,1)S(1)}, u32[]{:S(2)}, u32[]{:S(2)}) %collective-permute-start.3) | collective-permute-done | bytes 1048608 | tf_op jit(solution)/shard_map/ppermute | solution.py:326
  46.1 1.7 collective-permute-start.4
  47.7 2.4 collective-permute-start.6
  52.2 1.9 multiply_bitcast_fusion
  54.1 1.8 copy.32
  56.0 2.4 reduce_sum.27
  59.2 13.1 %collective-permute-done.4.refs_5_.refs_7_ = bf16[512,1024]{1,0:T(8,128)(2,1)} collective-permute-done((bf16[512,1024]{1,0:T(8,128)(2,1)S(1)}, bf16[512,1024]{1,0:T(8,128)(2,1)}, u32[]{:S(2)}, u32[]{:S(2)}) %collective-permute-start.4) | collective-permute-done | bytes 1048608 | tf_op jit(solution)/shard_map/ppermute | solution.py:326
  72.3 12.0 %partial_norms.1 = f32[2,8,8,64]{3,2,1,0:T(8,128)S(1)} custom-call(s32[3]{0:T(128)S(1)} %pad_add_fusion.meta, s32[1536]{0:T(1024)S(1)} %reshape.99.table, bf16[512,1024]{1,0:T(8,128)(2,1)S(1)} %copy-done, bf16[512,1024]{1,0:T(8,128)(2,1)} %collective-permute-done.refs_1_, bf16[512,1024]{1,0:T(8,128)(2,1)S(1)} %copy-done.1, ...), custom_call_target="tpu_custom_call" | custom-call | tf_op jit(solution)/shard_map/partial_norms/pallas_call | solution.py:344
  84.3 3.6 %collective-permute-start.8 = (f32[3,8,8,64]{3,2,1,0:T(8,128)S(1)}, f32[3,8,8,64]{3,2,1,0:T(8,128)S(1)}, u32[]{:S(2)}, u32[]{:S(2)}) collective-permute-start(f32[3,8,8,64]{3,2,1,0:T(8,128)S(1)} %pad_maximum_fusion.3), channel_id=1, source_target_pairs={{0,16},{4,20},{8,24},{12,28},{16,0},{20,4},{24,8},{28,12},{1,17},{... | collective-permute-start | bytes 147464 | tf_op jit(solution)/shard_map/ppermute | solution.py:323
  87.9 6.1 %collective-permute-done.6.refs_10_ = bf16[512,1024]{1,0:T(8,128)(2,1)} collective-permute-done((bf16[512,1024]{1,0:T(8,128)(2,1)}, bf16[512,1024]{1,0:T(8,128)(2,1)}, u32[]{:S(2)}, u32[]{:S(2)}) %collective-permute-start.6) | collective-permute-done | bytes 1048608 | tf_op jit(solution)/shard_map/ppermute | solution.py:326
  94.8 4.7 %collective-permute-done.8 = f32[3,8,8,64]{3,2,1,0:T(8,128)S(1)} collective-permute-done((f32[3,8,8,64]{3,2,1,0:T(8,128)S(1)}, f32[3,8,8,64]{3,2,1,0:T(8,128)S(1)}, u32[]{:S(2)}, u32[]{:S(2)}) %collective-permute-start.8) | collective-permute-done | bytes 49184 | tf_op jit(solution)/shard_map/ppermute | solution.py:323
  100.1 18.1 %collective-permute-done.7.refs_11_ = bf16[512,1024]{1,0:T(8,128)(2,1)S(1)} collective-permute-done((bf16[512,1024]{1,0:T(8,128)(2,1)}, bf16[512,1024]{1,0:T(8,128)(2,1)S(1)}, u32[]{:S(2)}, u32[]{:S(2)}) %collective-permute-start.7) | collective-permute-done | bytes 1048608 | tf_op jit(solution)/shard_map/ppermute | solution.py:326
  119.2 21.0 %gradients.2 = (f32[512,512]{1,0:T(8,128)S(1)}, bf16[512,512]{1,0:T(8,128)(2,1)S(1)}, bf16[2,512,512]{2,1,0:T(8,128)(2,1)S(1)}, bf16[2,512,512]{2,1,0:T(8,128)(2...) custom-call(s32[3]{0:T(128)S(1)} %pad_add_fusion.meta, s32[1536]{0:T(1024)S(1)} %reshape.99.table, ...), custom_call_target="tpu_custom_call" | custom-call | tf_op jit(solution)/shard_map/gradients/pallas_call | solution.py:389
  140.2 9.1 %collective-permute-start.9 = (bf16[512,512]{1,0:T(8,128)(2,1)S(1)}, bf16[512,512]{1,0:T(8,128)(2,1)S(1)}, u32[]{:S(2)}, u32[]{:S(2)}) collective-permute-start(bf16[512,512]{1,0:T(8,128)(2,1)S(1)} %get-tuple-element.16), channel_id=1, source_target_pairs={{0,16},{4,20},{8,24},{12,28},{16,0},{20,4},{24,8},{28,12},{1,17},{... | collective-permute-start | bytes 1572872 | tf_op jit(solution)/shard_map/ppermute | solution.py:323
  149.3 21.8 %gradients.3 = (f32[512,512]{1,0:T(8,128)S(1)}, bf16[512,512]{1,0:T(8,128)(2,1)S(1)}, bf16[2,512,512]{2,1,0:T(8,128)(2,1)S(1)}, bf16[2,512,512]{2,1,0:T(8,128)(2...) custom-call(s32[3]{0:T(128)S(1)} %pad_add_fusion.meta, s32[1536]{0:T(1024)S(1)} %reshape.99.table, ...), custom_call_target="tpu_custom_call" | custom-call | tf_op jit(solution)/shard_map/gradients/pallas_call | solution.py:389
  171.1 4.3 %collective-permute-start.10 = (bf16[512,512]{1,0:T(8,128)(2,1)S(1)}, bf16[512,512]{1,0:T(8,128)(2,1)S(1)}, u32[]{:S(2)}, u32[]{:S(2)}) collective-permute-start(bf16[512,512]{1,0:T(8,128)(2,1)S(1)} %get-tuple-element.18), channel_id=1, source_target_pairs={{0,16},{4,20},{8,24},{12,28},{16,0},{20,4},{24,8},{28,12},{1,17},{... | collective-permute-start | bytes 1572872 | tf_op jit(solution)/shard_map/ppermute | solution.py:323
  175.4 2.0 collective-permute-start.17
  177.5 1.9 collective-permute-start.13
  179.5 16.4 %collective-permute-done.10 = bf16[512,512]{1,0:T(8,128)(2,1)S(1)} collective-permute-done((bf16[512,512]{1,0:T(8,128)(2,1)S(1)}, bf16[512,512]{1,0:T(8,128)(2,1)S(1)}, u32[]{:S(2)}, u32[]{:S(2)}) %collective-permute-start.10) | collective-permute-done | bytes 524320 | tf_op jit(solution)/shard_map/ppermute | solution.py:323
  197.2 4.4 %all-to-all-start = ((bf16[4,128,1024]{2,1,0:T(8,128)(2,1)}), bf16[4,128,1024]{2,1,0:T(8,128)(2,1)}, u32[]{:S(2)}, u32[]{:S(2)}) async-start(bf16[4,128,1024]{2,1,0:T(8,128)(2,1)} %bitcast.69), calls=%async_computation | async-start | bytes 2097152 | tf_op jit(solution)/shard_map/all_to_all | solution.py:436
  204.4 9.9 %collective-permute-done.17 = bf16[2,512,512]{2,1,0:T(8,128)(2,1)} collective-permute-done((bf16[2,512,512]{2,1,0:T(8,128)(2,1)}, bf16[2,512,512]{2,1,0:T(8,128)(2,1)}, u32[]{:S(2)}, u32[]{:S(2)}) %collective-permute-start.17) | collective-permute-done | bytes 1048608 | tf_op jit(solution)/shard_map/ppermute | solution.py:326
  216.3 2.0 fusion.4
  219.1 7.1 %collective-permute-done.13 = bf16[2,512,512]{2,1,0:T(8,128)(2,1)} collective-permute-done((bf16[2,512,512]{2,1,0:T(8,128)(2,1)}, bf16[2,512,512]{2,1,0:T(8,128)(2,1)}, u32[]{:S(2)}, u32[]{:S(2)}) %collective-permute-start.13) | collective-permute-done | bytes 1048608 | tf_op jit(solution)/shard_map/ppermute | solution.py:326
  226.2 2.0 fusion.5
  228.3 9.0 %collective-permute-done.16 = bf16[512,512]{1,0:T(8,128)(2,1)S(1)} collective-permute-done((bf16[512,512]{1,0:T(8,128)(2,1)S(1)}, bf16[512,512]{1,0:T(8,128)(2,1)S(1)}, u32[]{:S(2)}, u32[]{:S(2)}) %collective-permute-start.16) | collective-permute-done | bytes 524320 | tf_op jit(solution)/shard_map/ppermute | solution.py:326
  238.6 5.0 %collective-permute-done.18 = bf16[512,512]{1,0:T(8,128)(2,1)S(1)} collective-permute-done((bf16[512,512]{1,0:T(8,128)(2,1)S(1)}, bf16[512,512]{1,0:T(8,128)(2,1)S(1)}, u32[]{:S(2)}, u32[]{:S(2)}) %collective-permute-start.18) | collective-permute-done | bytes 524320 | tf_op jit(solution)/shard_map/ppermute | solution.py:326
  246.0 4.8 %all-to-all-start.2 = ((bf16[4,128,1024]{2,1,0:T(8,128)(2,1)}), bf16[4,128,1024]{2,1,0:T(8,128)(2,1)S(1)}, u32[]{:S(2)}, u32[]{:S(2)}) async-start(bf16[4,128,1024]{2,1,0:T(8,128)(2,1)} %bitcast.71), calls=%async_computation.2 | async-start | bytes 2097152 | tf_op jit(solution)/shard_map/all_to_all | solution.py:436
  254.7 10.5 %all-to-all-done.2 = bf16[4,128,1024]{2,1,0:T(8,128)(2,1)S(1)} async-done(((bf16[4,128,1024]{2,1,0:T(8,128)(2,1)}), bf16[4,128,1024]{2,1,0:T(8,128)(2,1)S(1)}, u32[]{:S(2)}, u32[]{:S(2)}) %all-to-all-start.2) | async-done | bytes 1048608 | tf_op jit(solution)/shard_map/all_to_all | solution.py:436
  265.2 3.5 %all-to-all-start.1 = ((bf16[4,128,1024]{2,1,0:T(8,128)(2,1)}), bf16[4,128,1024]{2,1,0:T(8,128)(2,1)S(1)}, u32[]{:S(2)}, u32[]{:S(2)}) async-start(bf16[4,128,1024]{2,1,0:T(8,128)(2,1)} %bitcast.19), calls=%async_computation.1 | async-start | bytes 2097152 | tf_op jit(solution)/shard_map/all_to_all | solution.py:436
  268.7 2.3 copy.29
  272.1 11.1 %all-to-all-done.1 = bf16[4,128,1024]{2,1,0:T(8,128)(2,1)S(1)} async-done(((bf16[4,128,1024]{2,1,0:T(8,128)(2,1)}), bf16[4,128,1024]{2,1,0:T(8,128)(2,1)S(1)}, u32[]{:S(2)}, u32[]{:S(2)}) %all-to-all-start.1) | async-done | bytes 1048608 | tf_op jit(solution)/shard_map/all_to_all | solution.py:436
  (68 shorter events, 23.7 us)
Async XLA Ops:
  0.6 45.4 %collective-permute-start.3 = (bf16[512,1024]{1,0:T(8,128)(2,1)}, bf16[512,1024]{1,0:T(8,128)(2,1)S(1)}, u32[]{:S(2)}, u32[]{:S(2)}) collective-permute-start(bf16[512,1024]{1,0:T(8,128)(2,1)} %refs_4_.3), channel_id=1, source_target_pairs={{0,8},{4,12},{8,0},{12,4},{16,24},{20,28},{24,16},{28,20},{1,9},{5... | collective-permute-start | bytes 3145736 | tf_op jit(solution)/shard_map/ppermute | solution.py:326
  0.7 57.9 %collective-permute-start = (bf16[512,1024]{1,0:T(8,128)(2,1)}, bf16[512,1024]{1,0:T(8,128)(2,1)}, u32[]{:S(2)}, u32[]{:S(2)}) collective-permute-start(bf16[512,1024]{1,0:T(8,128)(2,1)} %refs_0_.5), channel_id=1, source_target_pairs={{0,16},{4,20},{8,24},{12,28},{16,0},{20,4},{24,8},{28,12},{1,17},{... | collective-permute-start | bytes 3145736 | tf_op jit(solution)/shard_map/ppermute | solution.py:323
  3.7 55.5 %collective-permute-start.2 = (bf16[512,1024]{1,0:T(8,128)(2,1)}, bf16[512,1024]{1,0:T(8,128)(2,1)}, u32[]{:S(2)}, u32[]{:S(2)}) collective-permute-start(bf16[512,1024]{1,0:T(8,128)(2,1)} %refs_4_.3), channel_id=1, source_target_pairs={{0,4},{4,0},{8,12},{12,8},{16,20},{20,16},{24,28},{28,24},{1,5},{5... | collective-permute-start | bytes 3145736 | tf_op jit(solution)/shard_map/ppermute | solution.py:326
  46.1 26.2 %copy-start.2 = (bf16[512,1024]{1,0:T(8,128)(2,1)}, bf16[512,1024]{1,0:T(8,128)(2,1)S(1)}, u32[]{:S(2)}) copy-start(bf16[512,1024]{1,0:T(8,128)(2,1)S(1)} %collective-permute-done.3.refs_4_.refs_6_) | copy-start | bytes 3145732
  46.1 26.2 %collective-permute-start.4 = (bf16[512,1024]{1,0:T(8,128)(2,1)S(1)}, bf16[512,1024]{1,0:T(8,128)(2,1)}, u32[]{:S(2)}, u32[]{:S(2)}) collective-permute-start(bf16[512,1024]{1,0:T(8,128)(2,1)S(1)} %collective-permute-done.3.refs_4_.refs_6_), channel_id=1, source_target_pairs={{0,4},{4,0},{8,12},{12,8},{16,20},{20,16},{24,28},{28,24},{1,5},{5... | collective-permute-start | bytes 3145736 | tf_op jit(solution)/shard_map/ppermute | solution.py:326
  47.7 46.3 %collective-permute-start.6 = (bf16[512,1024]{1,0:T(8,128)(2,1)}, bf16[512,1024]{1,0:T(8,128)(2,1)}, u32[]{:S(2)}, u32[]{:S(2)}) collective-permute-start(bf16[512,1024]{1,0:T(8,128)(2,1)} %refs_8_.3), channel_id=1, source_target_pairs={{0,8},{4,12},{8,0},{12,4},{16,24},{20,28},{24,16},{28,20},{1,9},{5... | collective-permute-start | bytes 3145736 | tf_op jit(solution)/shard_map/ppermute | solution.py:326
  50.1 50.0 %collective-permute-start.1 = (bf16[512,1024]{1,0:T(8,128)(2,1)}, bf16[512,1024]{1,0:T(8,128)(2,1)}, u32[]{:S(2)}, u32[]{:S(2)}) collective-permute-start(bf16[512,1024]{1,0:T(8,128)(2,1)} %refs_2_.5), channel_id=1, source_target_pairs={{0,16},{4,20},{8,24},{12,28},{16,0},{20,4},{24,8},{28,12},{1,17},{... | collective-permute-start | bytes 3145736 | tf_op jit(solution)/shard_map/ppermute | solution.py:323
  56.0 2.6 copy-start.6
  56.0 16.3 %copy-start = (bf16[512,1024]{1,0:T(8,128)(2,1)S(1)}, bf16[512,1024]{1,0:T(8,128)(2,1)}, u32[]{:S(2)}) copy-start(bf16[512,1024]{1,0:T(8,128)(2,1)} %refs_0_.5) | copy-start | bytes 3145732
  56.0 16.3 %copy-start.1 = (bf16[512,1024]{1,0:T(8,128)(2,1)S(1)}, bf16[512,1024]{1,0:T(8,128)(2,1)}, u32[]{:S(2)}) copy-start(bf16[512,1024]{1,0:T(8,128)(2,1)} %refs_4_.3) | copy-start | bytes 3145732
  58.6 41.4 %collective-permute-start.5 = (bf16[512,1024]{1,0:T(8,128)(2,1)}, bf16[512,1024]{1,0:T(8,128)(2,1)}, u32[]{:S(2)}, u32[]{:S(2)}) collective-permute-start(bf16[512,1024]{1,0:T(8,128)(2,1)} %refs_8_.3), channel_id=1, source_target_pairs={{0,4},{4,0},{8,12},{12,8},{16,20},{20,16},{24,28},{28,24},{1,5},{5... | collective-permute-start | bytes 3145736 | tf_op jit(solution)/shard_map/ppermute | solution.py:326
  84.3 15.1 %collective-permute-start.8 = (f32[3,8,8,64]{3,2,1,0:T(8,128)S(1)}, f32[3,8,8,64]{3,2,1,0:T(8,128)S(1)}, u32[]{:S(2)}, u32[]{:S(2)}) collective-permute-start(f32[3,8,8,64]{3,2,1,0:T(8,128)S(1)} %pad_maximum_fusion.3), channel_id=1, source_target_pairs={{0,16},{4,20},{8,24},{12,28},{16,0},{20,4},{24,8},{28,12},{1,17},{... | collective-permute-start | bytes 147464 | tf_op jit(solution)/shard_map/ppermute | solution.py:323
  94.0 24.2 %collective-permute-start.7 = (bf16[512,1024]{1,0:T(8,128)(2,1)}, bf16[512,1024]{1,0:T(8,128)(2,1)S(1)}, u32[]{:S(2)}, u32[]{:S(2)}) collective-permute-start(bf16[512,1024]{1,0:T(8,128)(2,1)} %collective-permute-done.6.refs_10_), channel_id=1, source_target_pairs={{0,4},{4,0},{8,12},{12,8},{16,20},{20,16},{24,28},{28,24},{1,5},{5... | collective-permute-start | bytes 3145736 | tf_op jit(solution)/shard_map/ppermute | solution.py:326
  118.2 1.0 copy-start.5
  140.2 37.3 %collective-permute-start.9 = (bf16[512,512]{1,0:T(8,128)(2,1)S(1)}, bf16[512,512]{1,0:T(8,128)(2,1)S(1)}, u32[]{:S(2)}, u32[]{:S(2)}) collective-permute-start(bf16[512,512]{1,0:T(8,128)(2,1)S(1)} %get-tuple-element.16), channel_id=1, source_target_pairs={{0,16},{4,20},{8,24},{12,28},{16,0},{20,4},{24,8},{28,12},{1,17},{... | collective-permute-start | bytes 1572872 | tf_op jit(solution)/shard_map/ppermute | solution.py:323
  149.3 52.3 %collective-permute-start.15 = (bf16[2,512,512]{2,1,0:T(8,128)(2,1)}, bf16[2,512,512]{2,1,0:T(8,128)(2,1)}, u32[]{:S(2)}, u32[]{:S(2)}) collective-permute-start(bf16[2,512,512]{2,1,0:T(8,128)(2,1)} %get-tuple-element.24), channel_id=1, source_target_pairs={{0,8},{4,12},{8,0},{12,4},{16,24},{20,28},{24,16},{28,20},{1,9},{5... | collective-permute-start | bytes 3145736 | tf_op jit(solution)/shard_map/ppermute | solution.py:326
  171.1 25.0 %copy-start.3 = (bf16[2,512,512]{2,1,0:T(8,128)(2,1)}, bf16[2,512,512]{2,1,0:T(8,128)(2,1)S(1)}, u32[]{:S(2)}) copy-start(bf16[2,512,512]{2,1,0:T(8,128)(2,1)S(1)} %get-tuple-element.25) | copy-start | bytes 3145732
  171.1 24.8 %collective-permute-start.10 = (bf16[512,512]{1,0:T(8,128)(2,1)S(1)}, bf16[512,512]{1,0:T(8,128)(2,1)S(1)}, u32[]{:S(2)}, u32[]{:S(2)}) collective-permute-start(bf16[512,512]{1,0:T(8,128)(2,1)S(1)} %get-tuple-element.18), channel_id=1, source_target_pairs={{0,16},{4,20},{8,24},{12,28},{16,0},{20,4},{24,8},{28,12},{1,17},{... | collective-permute-start | bytes 1572872 | tf_op jit(solution)/shard_map/ppermute | solution.py:323
  175.4 39.0 %collective-permute-start.17 = (bf16[2,512,512]{2,1,0:T(8,128)(2,1)}, bf16[2,512,512]{2,1,0:T(8,128)(2,1)}, u32[]{:S(2)}, u32[]{:S(2)}) collective-permute-start(bf16[2,512,512]{2,1,0:T(8,128)(2,1)} %get-tuple-element.26), channel_id=1, source_target_pairs={{0,8},{4,12},{8,0},{12,4},{16,24},{20,28},{24,16},{28,20},{1,9},{5... | collective-permute-start | bytes 3145736 | tf_op jit(solution)/shard_map/ppermute | solution.py:326
  177.3 39.0 %collective-permute-start.11 = (bf16[2,512,512]{2,1,0:T(8,128)(2,1)}, bf16[2,512,512]{2,1,0:T(8,128)(2,1)}, u32[]{:S(2)}, u32[]{:S(2)}) collective-permute-start(bf16[2,512,512]{2,1,0:T(8,128)(2,1)} %get-tuple-element.20), channel_id=1, source_target_pairs={{0,4},{4,0},{8,12},{12,8},{16,20},{20,16},{24,28},{28,24},{1,5},{5... | collective-permute-start | bytes 3145736 | tf_op jit(solution)/shard_map/ppermute | solution.py:326
  177.5 48.7 %collective-permute-start.13 = (bf16[2,512,512]{2,1,0:T(8,128)(2,1)}, bf16[2,512,512]{2,1,0:T(8,128)(2,1)}, u32[]{:S(2)}, u32[]{:S(2)}) collective-permute-start(bf16[2,512,512]{2,1,0:T(8,128)(2,1)} %get-tuple-element.22), channel_id=1, source_target_pairs={{0,4},{4,0},{8,12},{12,8},{16,20},{20,16},{24,28},{28,24},{1,5},{5... | collective-permute-start | bytes 3145736 | tf_op jit(solution)/shard_map/ppermute | solution.py:326
  197.2 48.8 %all-to-all-start = ((bf16[4,128,1024]{2,1,0:T(8,128)(2,1)}), bf16[4,128,1024]{2,1,0:T(8,128)(2,1)}, u32[]{:S(2)}, u32[]{:S(2)}) async-start(bf16[4,128,1024]{2,1,0:T(8,128)(2,1)} %bitcast.69), calls=%async_computation | async-start | bytes 2097152 | tf_op jit(solution)/shard_map/all_to_all | solution.py:436
  202.8 34.5 %collective-permute-start.16 = (bf16[512,512]{1,0:T(8,128)(2,1)S(1)}, bf16[512,512]{1,0:T(8,128)(2,1)S(1)}, u32[]{:S(2)}, u32[]{:S(2)}) collective-permute-start(bf16[512,512]{1,0:T(8,128)(2,1)S(1)} %fusion.6), channel_id=1, source_target_pairs={{0,4},{4,0},{8,12},{12,8},{16,20},{20,16},{24,28},{28,24},{1,5},{5... | collective-permute-start | bytes 1572872 | tf_op jit(solution)/shard_map/ppermute | solution.py:326
  215.7 27.9 %collective-permute-start.18 = (bf16[512,512]{1,0:T(8,128)(2,1)S(1)}, bf16[512,512]{1,0:T(8,128)(2,1)S(1)}, u32[]{:S(2)}, u32[]{:S(2)}) collective-permute-start(bf16[512,512]{1,0:T(8,128)(2,1)S(1)} %fusion.7), channel_id=1, source_target_pairs={{0,4},{4,0},{8,12},{12,8},{16,20},{20,16},{24,28},{28,24},{1,5},{5... | collective-permute-start | bytes 1572872 | tf_op jit(solution)/shard_map/ppermute | solution.py:326
  218.3 25.3 %copy-start.4 = (bf16[2,512,512]{2,1,0:T(8,128)(2,1)S(1)}, bf16[2,512,512]{2,1,0:T(8,128)(2,1)}, u32[]{:S(2)}) copy-start(bf16[2,512,512]{2,1,0:T(8,128)(2,1)} %copy-done.3) | copy-start | bytes 3145732
  218.3 32.4 %collective-permute-start.12 = (bf16[512,512]{1,0:T(8,128)(2,1)}, bf16[512,512]{1,0:T(8,128)(2,1)}, u32[]{:S(2)}, u32[]{:S(2)}) collective-permute-start(bf16[512,512]{1,0:T(8,128)(2,1)} %fusion.4), channel_id=1, source_target_pairs={{0,8},{4,12},{8,0},{12,4},{16,24},{20,28},{24,16},{28,20},{1,9},{5... | collective-permute-start | bytes 1572872 | tf_op jit(solution)/shard_map/ppermute | solution.py:326
  228.2 23.9 %collective-permute-start.14 = (bf16[512,512]{1,0:T(8,128)(2,1)}, bf16[512,512]{1,0:T(8,128)(2,1)}, u32[]{:S(2)}, u32[]{:S(2)}) collective-permute-start(bf16[512,512]{1,0:T(8,128)(2,1)} %fusion.5), channel_id=1, source_target_pairs={{0,8},{4,12},{8,0},{12,4},{16,24},{20,28},{24,16},{28,20},{1,9},{5... | collective-permute-start | bytes 1572872 | tf_op jit(solution)/shard_map/ppermute | solution.py:326
  246.0 19.2 %all-to-all-start.2 = ((bf16[4,128,1024]{2,1,0:T(8,128)(2,1)}), bf16[4,128,1024]{2,1,0:T(8,128)(2,1)S(1)}, u32[]{:S(2)}, u32[]{:S(2)}) async-start(bf16[4,128,1024]{2,1,0:T(8,128)(2,1)} %bitcast.71), calls=%async_computation.2 | async-start | bytes 2097152 | tf_op jit(solution)/shard_map/all_to_all | solution.py:436
  265.2 18.0 %all-to-all-start.1 = ((bf16[4,128,1024]{2,1,0:T(8,128)(2,1)}), bf16[4,128,1024]{2,1,0:T(8,128)(2,1)S(1)}, u32[]{:S(2)}, u32[]{:S(2)}) async-start(bf16[4,128,1024]{2,1,0:T(8,128)(2,1)} %bitcast.19), calls=%async_computation.1 | async-start | bytes 2097152 | tf_op jit(solution)/shard_map/all_to_all | solution.py:436

commit v3 on v2

--- a/solution.py
+++ b/solution.py
@@ -325,20 +325,49 @@
     def flip(array, j):
         return lax.ppermute(array, "seq", [(i, i ^ j) for i in range(seq_count)])
 
-    def collect(array):
-        across = flip(array, 2)
-        return [array, flip(array, 1), across, flip(across, 1)]
-
-    k_group = collect(key_states)
-    q_all = [queries] + [shift(queries, r) for r in range(1, sources)]
-    v_group = collect(value_states)
-    g_all = [grad_out] + [shift(grad_out, r) for r in range(1, sources)]
+    def after(array, other):
+        return lax.optimization_barrier((array, other))[0]
+
+    def whole(array, place=None):
+        return [(array, place, 0)]
+
+    count = heads // CHUNKS
+    k_z = flip(key_states, 2)
+    q_all = whole(queries)
+    for r in range(1, sources):
+        q_all += whole(shift(queries, r))
+    kv_x = flip(jnp.stack([key_states, value_states]), 1)
+    k_all = whole(key_states) + whole(kv_x, 0) + whole(k_z) + whole(flip(k_z, 1))
+
+    v_chunks, previous = [], k_z
+    g_all = whole(grad_out)
+    for r in range(1, sources):
+        g_all += whole(shift(after(grad_out, k_z), r))
+    for c in range(CHUNKS):
+        cut = slice(c * count * DH, (c + 1) * count * DH)
+        v = after(value_states[:, cut], previous)
+        own = [(value_states, None, c * count), (kv_x, 1, c * count)]
+        if c == 0:
+            v_z = flip(v, 2)
+            v_all = own + [(v_z, None, 0), (flip(v_z, 1), None, 0)]
+            previous = v_z
+        else:
+            v_z = flip(jnp.stack([v, kv_x[1][:, cut]]), 2)
+            v_all = own + [(v_z, 0, 0), (v_z, 1, 0)]
+            previous = v_z
+        v_chunks.append(v_all)
 
     meta = jnp.concatenate([me.astype(jnp.int32)[None], global_blocks.astype(jnp.int32)])
     table = random_blocks.reshape(-1)
 
-    def column(offset):
-        return pl.BlockSpec((tokens, DH), lambda h, *_: (0, h + offset))
+    def spec(operand, head0):
+        _, place, first = operand
+        if place is None:
+            return pl.BlockSpec((tokens, DH), lambda h, *_: (0, h + head0 + first))
+        return pl.BlockSpec((None, tokens, DH), lambda h, *_: (place, 0, h + head0 + first))
+
+    def arrays(operands):
+        return [array for array, _, _ in operands]
 
     padded_rows = (GROUP * tokens + 2 * BS, DH)
     partial_norms = pl.pallas_call(
@@ -346,14 +375,14 @@
         grid_spec=pltpu.PrefetchScalarGridSpec(
             num_scalar_prefetch=2,
             grid=(heads,),
-            in_specs=[column(0)] * (sources + GROUP),
+            in_specs=[spec(x, 0) for x in q_all + k_all],
             out_specs=pl.BlockSpec((sources, 1, blocks, BS), lambda h, *_: (0, h, 0, 0)),
             scratch_shapes=[pltpu.VMEM(padded_rows, jnp.bfloat16)],
         ),
         out_shape=jax.ShapeDtypeStruct((sources, heads, blocks, BS), jnp.float32),
         compiler_params=pltpu.CompilerParams(vmem_limit_bytes=48 * 2**20),
         name="partial_norms",
-    )(meta, table, *q_all, *k_group)
+    )(meta, table, *arrays(q_all + k_all))
 
     row_dot = jnp.sum(
         grad_out.astype(jnp.float32).reshape(tokens, heads, DH)
@@ -379,7 +408,8 @@
     def flat(array):
         return array.reshape(sources, heads, 1, tokens)
 
-    def gradients(head0, count):
+    def gradients(c):
+        head0 = c * count
         width = count * DH
         item_spec = pl.BlockSpec((1, sources * blocks, 2 * BS), lambda h, *_: (h + head0, 0, 0))
         flat_spec = pl.BlockSpec((sources, 1, 1, tokens), lambda h, *_: (0, h + head0, 0, 0))
@@ -391,7 +421,10 @@
             grid_spec=pltpu.PrefetchScalarGridSpec(
                 num_scalar_prefetch=2,
                 grid=(count,),
-                in_specs=[column(head0)] * (2 * sources + 2 * GROUP)
+                in_specs=[spec(x, head0) for x in q_all]
+                + [spec(x, head0) for x in g_all]
+                + [spec(x, head0) for x in k_all]
+                + [spec(x, 0) for x in v_chunks[c]]
                 + [item_spec] * 2
                 + [flat_spec] * 2,
                 out_specs=[out_column] * sources + [half_spec] * 4,
@@ -414,10 +447,7 @@
         )(
             meta,
             table,
-            *q_all,
-            *g_all,
-            *k_group,
-            *v_group,
+            *arrays(q_all + g_all + k_all + v_chunks[c]),
             by_item(norms),
             by_item(dots),
             flat(norms),
@@ -435,10 +465,9 @@
     def to_tokens(array):
         return lax.all_to_all(array, "head", split_axis=0, concat_axis=1, tiled=True)
 
-    count = heads // CHUNKS
     dq_parts, dk_parts, dv_parts = [], [], []
     for c in range(CHUNKS):
-        outs = gradients(c * count, count)
+        outs = gradients(c)
         dq, dq_far = outs[0], outs[1:sources]
         dk_keep, dk_send, dv_keep, dv_send = outs[sources:]
         for r in range(1, sources):

time: 286 us -> 265 us (0.927)
  waiting for transfers between devices: 152 us -> 129 us
  Pallas kernels: 54.8 us -> 64.8 us
  starting transfers between devices: 47.8 us -> 39.1 us
    ppermute x14, waiting for transfers between devices: 109 us -> 63.9 us  [flip(): return lax.ppermute(array, 'seq', [(i, i ^ j) for i in range(seq_count)])]
    ppermute x5, waiting for transfers between devices: 21 us -> 43.1 us  [shift(): return lax.ppermute(array, 'seq', pairs)]
    ppermute x5, starting transfers between devices: 21 us -> 9.51 us  [shift(): return lax.ppermute(array, 'seq', pairs)]
    pallas_call x2, Pallas kernels: 42.8 us -> 52.7 us  [gradients(): pl.pallas_call(partial(grads_kernel, sizes, head0), grid_spec=pltpu.Prefe...]
    another operation x0 -> x2, other arithmetic: none -> 4.27 us  [the longest x1 3.21 us: on_device(): kv_x = flip(jnp.stack([key_states, value_states]), 1)]
    ppermute x14, starting transfers between devices: 14.1 us -> 18.3 us  [flip(): return lax.ppermute(array, 'seq', [(i, i ^ j) for i in range(seq_count)])]
  transfers between devices with their start and end apart: 22 -> 22, of which waited for: 12 -> 9; matrix products, arithmetic and copies ran while one was open for 9% -> 11% of each run, Pallas kernels for 12% -> 24%
where the time goes in v3:
time: 265 us
  waiting for transfers between devices  129 us (49%)
  Pallas kernels  64.8 us (24%)
  starting transfers between devices  39.1 us (15%)
  other arithmetic  21.9 us (8%)
  local copies, waits for them, and re-layouts  9.55 us (4%)
    ppermute x14, waiting for transfers between devices, flip(): return lax.ppermute(array, 'seq', [(i, i ^ j) for i in range(seq_count)])  63.9 us
    pallas_call x2, Pallas kernels, gradients(): pl.pallas_call(partial(grads_kernel, sizes, head0), grid_spec=pltpu.Prefe...  52.7 us
    ppermute x5, waiting for transfers between devices, shift(): return lax.ppermute(array, 'seq', pairs)  43.1 us
    all_to_all x3, waiting for transfers between devices, to_tokens(): lax.all_to_all(array, 'head', split_axis=0, concat_axis=1, tiled=True)  21.6 us
    ppermute x14, starting transfers between devices, flip(): return lax.ppermute(array, 'seq', [(i, i ^ j) for i in range(seq_count)])  18.3 us
    pallas_call x1, Pallas kernels, on_device(): pl.pallas_call(partial(norm_kernel, sizes), grid_spec=pltpu.PrefetchScala...  12.2 us
    all_to_all x3, starting transfers between devices, to_tokens(): lax.all_to_all(array, 'head', split_axis=0, concat_axis=1, tiled=True)  11.3 us
    ppermute x5, starting transfers between devices, shift(): return lax.ppermute(array, 'seq', pairs)  9.51 us
  transfers between devices with their start and end apart: 22, of which 9 were waited for; matrix products, arithmetic and copies ran while one was open for 11% of the time, Pallas kernels for 24%

profile of v3, /device:TPU:8, one launch (start us, length us, event | category | flops | bytes accessed | tf_op | source)
XLA Modules:
  0.0 264.9 jit_solution(16650912193164219108)
XLA Ops:
  0.7 3.2 %pad_maximum_fusion = bf16[2,512,1024]{2,1,0:T(8,128)(2,1)} fusion(bf16[1,512,1024]{2,1,0:T(8,128)(2,1)} %bitcast.76, bf16[1,512,1024]{2,1,0:T(8,128)(2,1)} %bitcast.75), kind=kLoop, calls=%fused_computation | loop fusion | flops 1048576 | bytes 4194304 | tf_op jit(solution)/shard_map/stack | solution.py:339
  4.0 1.9 collective-permute-start.3
  5.9 2.6 collective-permute-start
  8.4 33.4 %collective-permute-done.1.refs_4_.refs_6_ = bf16[512,1024]{1,0:T(8,128)(2,1)S(1)} collective-permute-done((bf16[512,1024]{1,0:T(8,128)(2,1)}, bf16[512,1024]{1,0:T(8,128)(2,1)S(1)}, u32[]{:S(2)}, u32[]{:S(2)}) %collective-permute-start.1) | collective-permute-done | bytes 1048608 | tf_op jit(solution)/shard_map/ppermute | solution.py:326
  41.9 2.6 collective-permute-start.4
  45.9 2.4 collective-permute-start.5
  48.7 1.8 copy.32
  50.5 2.3 reduce_sum.27
  53.2 1.9 collective-permute-start.2
  55.0 13.6 %collective-permute-done.5.refs_10_ = bf16[512,512]{1,0:T(8,128)(2,1)} collective-permute-done((bf16[512,512]{1,0:T(8,128)(2,1)}, bf16[512,512]{1,0:T(8,128)(2,1)}, u32[]{:S(2)}, u32[]{:S(2)}) %collective-permute-start.5) | collective-permute-done | bytes 524320 | tf_op jit(solution)/shard_map/ppermute | solution.py:326
  69.2 6.1 %collective-permute-done.4.refs_5_.refs_7_ = bf16[512,1024]{1,0:T(8,128)(2,1)} collective-permute-done((bf16[512,1024]{1,0:T(8,128)(2,1)S(1)}, bf16[512,1024]{1,0:T(8,128)(2,1)}, u32[]{:S(2)}, u32[]{:S(2)}) %collective-permute-start.4) | collective-permute-done | bytes 1048608 | tf_op jit(solution)/shard_map/ppermute | solution.py:326
  75.3 12.2 %partial_norms.1 = f32[2,8,8,64]{3,2,1,0:T(8,128)S(1)} custom-call(s32[3]{0:T(128)S(1)} %pad_add_fusion.meta, s32[1536]{0:T(1024)S(1)} %reshape.99.table, bf16[512,1024]{1,0:T(8,128)(2,1)S(1)} %copy-done.1, bf16[512,1024]{1,0:T(8,128)(2,1)} %collective-permute-done.refs_1_, bf16[512,1024]{1,0:T(8,128)(2,1)S(1)} %copy-done, ...), custom_call_target="tpu_custom_call" | custom-call | tf_op jit(solution)/shard_map/partial_norms/pallas_call | solution.py:373
  87.5 3.1 %collective-permute-start.7 = (f32[3,8,8,64]{3,2,1,0:T(8,128)S(1)}, f32[3,8,8,64]{3,2,1,0:T(8,128)S(1)}, u32[]{:S(2)}, u32[]{:S(2)}) collective-permute-start(f32[3,8,8,64]{3,2,1,0:T(8,128)S(1)} %pad_maximum_fusion.5), channel_id=1, source_target_pairs={{0,16},{4,20},{8,24},{12,28},{16,0},{20,4},{24,8},{28,12},{1,17},{... | collective-permute-start | bytes 147464 | tf_op jit(solution)/shard_map/ppermute | solution.py:323
  93.0 1.6 collective-permute-start.9
  94.5 8.9 %collective-permute-done.7 = f32[3,8,8,64]{3,2,1,0:T(8,128)S(1)} collective-permute-done((f32[3,8,8,64]{3,2,1,0:T(8,128)S(1)}, f32[3,8,8,64]{3,2,1,0:T(8,128)S(1)}, u32[]{:S(2)}, u32[]{:S(2)}) %collective-permute-start.7) | collective-permute-done | bytes 49184 | tf_op jit(solution)/shard_map/ppermute | solution.py:323
  104.0 26.0 %gradients.2 = (f32[512,512]{1,0:T(8,128)S(1)}, bf16[512,512]{1,0:T(8,128)(2,1)S(1)}, bf16[2,512,512]{2,1,0:T(8,128)(2,1)S(1)}, bf16[2,512,512]{2,1,0:T(8,128)(2...) custom-call(s32[3]{0:T(128)S(1)} %pad_add_fusion.meta, s32[1536]{0:T(1024)S(1)} %reshape.99.table, ...), custom_call_target="tpu_custom_call" | custom-call | tf_op jit(solution)/shard_map/gradients/pallas_call | solution.py:419
  130.1 3.2 %collective-permute-start.15 = (bf16[2,512,512]{2,1,0:T(8,128)(2,1)}, bf16[2,512,512]{2,1,0:T(8,128)(2,1)S(1)}, u32[]{:S(2)}, u32[]{:S(2)}) collective-permute-start(bf16[2,512,512]{2,1,0:T(8,128)(2,1)} %get-tuple-element.30), channel_id=1, source_target_pairs={{0,8},{4,12},{8,0},{12,4},{16,24},{20,28},{24,16},{28,20},{1,9},{5... | collective-permute-start | bytes 3145736 | tf_op jit(solution)/shard_map/ppermute | solution.py:326
  133.3 1.9 collective-permute-start.8
  135.2 26.6 %gradients.3 = (f32[512,512]{1,0:T(8,128)S(1)}, bf16[512,512]{1,0:T(8,128)(2,1)S(1)}, bf16[2,512,512]{2,1,0:T(8,128)(2,1)S(1)}, bf16[2,512,512]{2,1,0:T(8,128)(2...) custom-call(s32[3]{0:T(128)S(1)} %pad_add_fusion.meta, s32[1536]{0:T(1024)S(1)} %reshape.99.table, ...), custom_call_target="tpu_custom_call" | custom-call | tf_op jit(solution)/shard_map/gradients/pallas_call | solution.py:419
  161.8 2.8 %collective-permute-start.17 = (bf16[2,512,512]{2,1,0:T(8,128)(2,1)}, bf16[2,512,512]{2,1,0:T(8,128)(2,1)}, u32[]{:S(2)}, u32[]{:S(2)}) collective-permute-start(bf16[2,512,512]{2,1,0:T(8,128)(2,1)} %get-tuple-element.32), channel_id=1, source_target_pairs={{0,8},{4,12},{8,0},{12,4},{16,24},{20,28},{24,16},{28,20},{1,9},{5... | collective-permute-start | bytes 3145736 | tf_op jit(solution)/shard_map/ppermute | solution.py:326
  164.6 6.0 %collective-permute-done.8 = bf16[512,512]{1,0:T(8,128)(2,1)S(1)} collective-permute-done((bf16[512,512]{1,0:T(8,128)(2,1)S(1)}, bf16[512,512]{1,0:T(8,128)(2,1)S(1)}, u32[]{:S(2)}, u32[]{:S(2)}) %collective-permute-start.8) | collective-permute-done | bytes 524320 | tf_op jit(solution)/shard_map/ppermute | solution.py:323
  172.1 1.9 collective-permute-start.16
  176.2 28.2 %collective-permute-done.10 = bf16[512,512]{1,0:T(8,128)(2,1)S(1)} collective-permute-done((bf16[512,512]{1,0:T(8,128)(2,1)S(1)}, bf16[512,512]{1,0:T(8,128)(2,1)S(1)}, u32[]{:S(2)}, u32[]{:S(2)}) %collective-permute-start.10) | collective-permute-done | bytes 524320 | tf_op jit(solution)/shard_map/ppermute | solution.py:323
  205.7 4.2 %all-to-all-start = ((bf16[4,128,1024]{2,1,0:T(8,128)(2,1)}), bf16[4,128,1024]{2,1,0:T(8,128)(2,1)}, u32[]{:S(2)}, u32[]{:S(2)}) async-start(bf16[4,128,1024]{2,1,0:T(8,128)(2,1)} %bitcast.78), calls=%async_computation | async-start | bytes 2097152 | tf_op jit(solution)/shard_map/all_to_all | solution.py:466
  211.4 1.5 fusion.1
  212.8 2.0 fusion.5
  214.8 10.8 %collective-permute-done.18 = bf16[512,512]{1,0:T(8,128)(2,1)S(1)} collective-permute-done((bf16[512,512]{1,0:T(8,128)(2,1)S(1)}, bf16[512,512]{1,0:T(8,128)(2,1)S(1)}, u32[]{:S(2)}, u32[]{:S(2)}) %collective-permute-start.18) | collective-permute-done | bytes 524320 | tf_op jit(solution)/shard_map/ppermute | solution.py:326
  228.0 3.5 %all-to-all-start.2 = ((bf16[4,128,1024]{2,1,0:T(8,128)(2,1)}), bf16[4,128,1024]{2,1,0:T(8,128)(2,1)S(1)}, u32[]{:S(2)}, u32[]{:S(2)}) async-start(bf16[4,128,1024]{2,1,0:T(8,128)(2,1)} %bitcast.80), calls=%async_computation.2 | async-start | bytes 2097152 | tf_op jit(solution)/shard_map/all_to_all | solution.py:466
  235.4 10.5 %all-to-all-done.2 = bf16[4,128,1024]{2,1,0:T(8,128)(2,1)S(1)} async-done(((bf16[4,128,1024]{2,1,0:T(8,128)(2,1)}), bf16[4,128,1024]{2,1,0:T(8,128)(2,1)S(1)}, u32[]{:S(2)}, u32[]{:S(2)}) %all-to-all-start.2) | async-done | bytes 1048608 | tf_op jit(solution)/shard_map/all_to_all | solution.py:466
  245.9 3.5 %all-to-all-start.1 = ((bf16[4,128,1024]{2,1,0:T(8,128)(2,1)}), bf16[4,128,1024]{2,1,0:T(8,128)(2,1)S(1)}, u32[]{:S(2)}, u32[]{:S(2)}) async-start(bf16[4,128,1024]{2,1,0:T(8,128)(2,1)} %bitcast.24), calls=%async_computation.1 | async-start | bytes 2097152 | tf_op jit(solution)/shard_map/all_to_all | solution.py:466
  249.4 2.3 copy.29
  252.8 11.1 %all-to-all-done.1 = bf16[4,128,1024]{2,1,0:T(8,128)(2,1)S(1)} async-done(((bf16[4,128,1024]{2,1,0:T(8,128)(2,1)}), bf16[4,128,1024]{2,1,0:T(8,128)(2,1)S(1)}, u32[]{:S(2)}, u32[]{:S(2)}) %all-to-all-start.1) | async-done | bytes 1048608 | tf_op jit(solution)/shard_map/all_to_all | solution.py:466
  (85 shorter events, 20.4 us)
Async XLA Ops:
  0.6 41.2 %collective-permute-start.1 = (bf16[512,1024]{1,0:T(8,128)(2,1)}, bf16[512,1024]{1,0:T(8,128)(2,1)S(1)}, u32[]{:S(2)}, u32[]{:S(2)}) collective-permute-start(bf16[512,1024]{1,0:T(8,128)(2,1)} %refs_4_.3), channel_id=1, source_target_pairs={{0,8},{4,12},{8,0},{12,4},{16,24},{20,28},{24,16},{28,20},{1,9},{5... | collective-permute-start | bytes 3145736 | tf_op jit(solution)/shard_map/ppermute | solution.py:326
  0.7 5.1 %copy-start.1 = (bf16[512,1024]{1,0:T(8,128)(2,1)S(1)}, bf16[512,1024]{1,0:T(8,128)(2,1)}, u32[]{:S(2)}) copy-start(bf16[512,1024]{1,0:T(8,128)(2,1)} %refs_0_.5) | copy-start | bytes 3145732
  0.7 43.7 %copy-start.11 = (s32[64,8,3]{0,1,2:T(8,128)S(1)}, s32[64,8,3]{0,1,2:T(8,128)}, u32[]{:S(2)}) copy-start(s32[64,8,3]{0,1,2:T(8,128)} %param.12) | copy-start | bytes 18436
  0.7 44.1 %copy-start.5 = (bf16[512,1024]{1,0:T(8,128)(2,1)S(1)}, bf16[512,1024]{1,0:T(8,128)(2,1)}, u32[]{:S(2)}) copy-start(bf16[512,1024]{1,0:T(8,128)(2,1)} %refs_8_.3) | copy-start | bytes 3145732
  4.0 71.3 %collective-permute-start.3 = (bf16[2,512,1024]{2,1,0:T(8,128)(2,1)}, bf16[2,512,1024]{2,1,0:T(8,128)(2,1)}, u32[]{:S(2)}, u32[]{:S(2)}) collective-permute-start(bf16[2,512,1024]{2,1,0:T(8,128)(2,1)} %pad_maximum_fusion), channel_id=1, source_target_pairs={{0,4},{4,0},{8,12},{12,8},{16,20},{20,16},{24,28},{28,24},{1,5},{5... | collective-permute-start | bytes 6291464 | tf_op jit(solution)/shard_map/ppermute | solution.py:326
  5.9 63.3 %collective-permute-start = (bf16[512,1024]{1,0:T(8,128)(2,1)S(1)}, bf16[512,1024]{1,0:T(8,128)(2,1)}, u32[]{:S(2)}, u32[]{:S(2)}) collective-permute-start(bf16[512,1024]{1,0:T(8,128)(2,1)S(1)} %copy-done.1), channel_id=1, source_target_pairs={{0,16},{4,20},{8,24},{12,28},{16,0},{20,4},{24,8},{28,12},{1,17},{... | collective-permute-start | bytes 3145736 | tf_op jit(solution)/shard_map/ppermute | solution.py:323
  41.9 33.4 %copy-start.2 = (bf16[512,1024]{1,0:T(8,128)(2,1)}, bf16[512,1024]{1,0:T(8,128)(2,1)S(1)}, u32[]{:S(2)}) copy-start(bf16[512,1024]{1,0:T(8,128)(2,1)S(1)} %collective-permute-done.1.refs_4_.refs_6_) | copy-start | bytes 3145732
  41.9 33.4 %collective-permute-start.4 = (bf16[512,1024]{1,0:T(8,128)(2,1)S(1)}, bf16[512,1024]{1,0:T(8,128)(2,1)}, u32[]{:S(2)}, u32[]{:S(2)}) collective-permute-start(bf16[512,1024]{1,0:T(8,128)(2,1)S(1)} %collective-permute-done.1.refs_4_.refs_6_), channel_id=1, source_target_pairs={{0,4},{4,0},{8,12},{12,8},{16,20},{20,16},{24,28},{28,24},{1,5},{5... | collective-permute-start | bytes 3145736 | tf_op jit(solution)/shard_map/ppermute | solution.py:326
  45.9 22.7 %collective-permute-start.5 = (bf16[512,512]{1,0:T(8,128)(2,1)}, bf16[512,512]{1,0:T(8,128)(2,1)}, u32[]{:S(2)}, u32[]{:S(2)}) collective-permute-start(bf16[512,512]{1,0:T(8,128)(2,1)} %get-tuple-element.19), channel_id=1, source_target_pairs={{0,8},{4,12},{8,0},{12,4},{16,24},{20,28},{24,16},{28,20},{1,9},{5... | collective-permute-start | bytes 1572872 | tf_op jit(solution)/shard_map/ppermute | solution.py:326
  50.5 24.7 %copy-start = (bf16[512,1024]{1,0:T(8,128)(2,1)S(1)}, bf16[512,1024]{1,0:T(8,128)(2,1)}, u32[]{:S(2)}) copy-start(bf16[512,1024]{1,0:T(8,128)(2,1)} %refs_4_.3) | copy-start | bytes 3145732
  53.2 50.9 %collective-permute-start.2 = (bf16[512,1024]{1,0:T(8,128)(2,1)}, bf16[512,1024]{1,0:T(8,128)(2,1)}, u32[]{:S(2)}, u32[]{:S(2)}) collective-permute-start(bf16[512,1024]{1,0:T(8,128)(2,1)} %refs_2_.5), channel_id=1, source_target_pairs={{0,16},{4,20},{8,24},{12,28},{16,0},{20,4},{24,8},{28,12},{1,17},{... | collective-permute-start | bytes 3145736 | tf_op jit(solution)/shard_map/ppermute | solution.py:323
  68.6 35.4 %collective-permute-start.6 = (bf16[512,512]{1,0:T(8,128)(2,1)}, bf16[512,512]{1,0:T(8,128)(2,1)}, u32[]{:S(2)}, u32[]{:S(2)}) collective-permute-start(bf16[512,512]{1,0:T(8,128)(2,1)} %collective-permute-done.5.refs_10_), channel_id=1, source_target_pairs={{0,4},{4,0},{8,12},{12,8},{16,20},{20,16},{24,28},{28,24},{1,5},{5... | collective-permute-start | bytes 1572872 | tf_op jit(solution)/shard_map/ppermute | solution.py:326
  87.4 4.5 %copy-start.7 = (bf16[512,512]{1,0:T(8,128)(2,1)S(1)}, bf16[512,512]{1,0:T(8,128)(2,1)}, u32[]{:S(2)}) copy-start(bf16[512,512]{1,0:T(8,128)(2,1)} %get-tuple-element.22) | copy-start | bytes 1572868
  87.5 15.9 %collective-permute-start.7 = (f32[3,8,8,64]{3,2,1,0:T(8,128)S(1)}, f32[3,8,8,64]{3,2,1,0:T(8,128)S(1)}, u32[]{:S(2)}, u32[]{:S(2)}) collective-permute-start(f32[3,8,8,64]{3,2,1,0:T(8,128)S(1)} %pad_maximum_fusion.5), channel_id=1, source_target_pairs={{0,16},{4,20},{8,24},{12,28},{16,0},{20,4},{24,8},{28,12},{1,17},{... | collective-permute-start | bytes 147464 | tf_op jit(solution)/shard_map/ppermute | solution.py:323
  93.0 42.2 %collective-permute-start.9 = (bf16[2,512,512]{2,1,0:T(8,128)(2,1)}, bf16[2,512,512]{2,1,0:T(8,128)(2,1)}, u32[]{:S(2)}, u32[]{:S(2)}) collective-permute-start(bf16[2,512,512]{2,1,0:T(8,128)(2,1)} %pad_maximum_fusion.1), channel_id=1, source_target_pairs={{0,8},{4,12},{8,0},{12,4},{16,24},{20,28},{24,16},{28,20},{1,9},{5... | collective-permute-start | bytes 3145736 | tf_op jit(solution)/shard_map/ppermute | solution.py:326
  130.1 40.9 %collective-permute-start.15 = (bf16[2,512,512]{2,1,0:T(8,128)(2,1)}, bf16[2,512,512]{2,1,0:T(8,128)(2,1)S(1)}, u32[]{:S(2)}, u32[]{:S(2)}) collective-permute-start(bf16[2,512,512]{2,1,0:T(8,128)(2,1)} %get-tuple-element.30), channel_id=1, source_target_pairs={{0,8},{4,12},{8,0},{12,4},{16,24},{20,28},{24,16},{28,20},{1,9},{5... | collective-permute-start | bytes 3145736 | tf_op jit(solution)/shard_map/ppermute | solution.py:326
  133.3 37.3 %collective-permute-start.8 = (bf16[512,512]{1,0:T(8,128)(2,1)S(1)}, bf16[512,512]{1,0:T(8,128)(2,1)S(1)}, u32[]{:S(2)}, u32[]{:S(2)}) collective-permute-start(bf16[512,512]{1,0:T(8,128)(2,1)S(1)} %get-tuple-element.21), channel_id=1, source_target_pairs={{0,16},{4,20},{8,24},{12,28},{16,0},{20,4},{24,8},{28,12},{1,17},{... | collective-permute-start | bytes 1572872 | tf_op jit(solution)/shard_map/ppermute | solution.py:323
  135.2 38.8 %collective-permute-start.11 = (bf16[2,512,512]{2,1,0:T(8,128)(2,1)S(1)}, bf16[2,512,512]{2,1,0:T(8,128)(2,1)S(1)}, u32[]{:S(2)}, u32[]{:S(2)}) collective-permute-start(bf16[2,512,512]{2,1,0:T(8,128)(2,1)S(1)} %get-tuple-element.26), channel_id=1, source_target_pairs={{0,4},{4,0},{8,12},{12,8},{16,20},{20,16},{24,28},{28,24},{1,5},{5... | collective-permute-start | bytes 3145736 | tf_op jit(solution)/shard_map/ppermute | solution.py:326
  161.8 13.2 %copy-start.3 = (bf16[2,512,512]{2,1,0:T(8,128)(2,1)}, bf16[2,512,512]{2,1,0:T(8,128)(2,1)S(1)}, u32[]{:S(2)}) copy-start(bf16[2,512,512]{2,1,0:T(8,128)(2,1)S(1)} %get-tuple-element.31) | copy-start | bytes 3145732
  161.8 48.1 %collective-permute-start.17 = (bf16[2,512,512]{2,1,0:T(8,128)(2,1)}, bf16[2,512,512]{2,1,0:T(8,128)(2,1)}, u32[]{:S(2)}, u32[]{:S(2)}) collective-permute-start(bf16[2,512,512]{2,1,0:T(8,128)(2,1)} %get-tuple-element.32), channel_id=1, source_target_pairs={{0,8},{4,12},{8,0},{12,4},{16,24},{20,28},{24,16},{28,20},{1,9},{5... | collective-permute-start | bytes 3145736 | tf_op jit(solution)/shard_map/ppermute | solution.py:326
  170.8 42.0 %collective-permute-start.13 = (bf16[2,512,512]{2,1,0:T(8,128)(2,1)}, bf16[2,512,512]{2,1,0:T(8,128)(2,1)}, u32[]{:S(2)}, u32[]{:S(2)}) collective-permute-start(bf16[2,512,512]{2,1,0:T(8,128)(2,1)} %get-tuple-element.28), channel_id=1, source_target_pairs={{0,4},{4,0},{8,12},{12,8},{16,20},{20,16},{24,28},{28,24},{1,5},{5... | collective-permute-start | bytes 3145736 | tf_op jit(solution)/shard_map/ppermute | solution.py:326
  170.9 33.5 %collective-permute-start.10 = (bf16[512,512]{1,0:T(8,128)(2,1)S(1)}, bf16[512,512]{1,0:T(8,128)(2,1)S(1)}, u32[]{:S(2)}, u32[]{:S(2)}) collective-permute-start(bf16[512,512]{1,0:T(8,128)(2,1)S(1)} %get-tuple-element.24), channel_id=1, source_target_pairs={{0,16},{4,20},{8,24},{12,28},{16,0},{20,4},{24,8},{28,12},{1,17},{... | collective-permute-start | bytes 1572872 | tf_op jit(solution)/shard_map/ppermute | solution.py:323
  171.0 33.5 %copy-start.9 = (bf16[2,512,512]{2,1,0:T(8,128)(2,1)}, bf16[2,512,512]{2,1,0:T(8,128)(2,1)S(1)}, u32[]{:S(2)}) copy-start(bf16[2,512,512]{2,1,0:T(8,128)(2,1)S(1)} %collective-permute-done.15) | copy-start | bytes 3145732
  172.1 39.3 %collective-permute-start.16 = (bf16[512,512]{1,0:T(8,128)(2,1)}, bf16[512,512]{1,0:T(8,128)(2,1)}, u32[]{:S(2)}, u32[]{:S(2)}) collective-permute-start(bf16[512,512]{1,0:T(8,128)(2,1)} %fusion.6), channel_id=1, source_target_pairs={{0,4},{4,0},{8,12},{12,8},{16,20},{20,16},{24,28},{28,24},{1,5},{5... | collective-permute-start | bytes 1572872 | tf_op jit(solution)/shard_map/ppermute | solution.py:326
  174.0 31.6 %copy-start.8 = (bf16[2,512,512]{2,1,0:T(8,128)(2,1)}, bf16[2,512,512]{2,1,0:T(8,128)(2,1)S(1)}, u32[]{:S(2)}) copy-start(bf16[2,512,512]{2,1,0:T(8,128)(2,1)S(1)} %collective-permute-done.11) | copy-start | bytes 3145732
  175.1 56.4 %collective-permute-start.12 = (bf16[512,512]{1,0:T(8,128)(2,1)}, bf16[512,512]{1,0:T(8,128)(2,1)}, u32[]{:S(2)}, u32[]{:S(2)}) collective-permute-start(bf16[512,512]{1,0:T(8,128)(2,1)} %fusion.4), channel_id=1, source_target_pairs={{0,8},{4,12},{8,0},{12,4},{16,24},{20,28},{24,16},{28,20},{1,9},{5... | collective-permute-start | bytes 1572872 | tf_op jit(solution)/shard_map/ppermute | solution.py:326
  205.7 22.3 %all-to-all-start = ((bf16[4,128,1024]{2,1,0:T(8,128)(2,1)}), bf16[4,128,1024]{2,1,0:T(8,128)(2,1)}, u32[]{:S(2)}, u32[]{:S(2)}) async-start(bf16[4,128,1024]{2,1,0:T(8,128)(2,1)} %bitcast.78), calls=%async_computation | async-start | bytes 2097152 | tf_op jit(solution)/shard_map/all_to_all | solution.py:466
  211.3 14.4 %copy-start.4 = (bf16[2,512,512]{2,1,0:T(8,128)(2,1)S(1)}, bf16[2,512,512]{2,1,0:T(8,128)(2,1)}, u32[]{:S(2)}) copy-start(bf16[2,512,512]{2,1,0:T(8,128)(2,1)} %copy-done.3) | copy-start | bytes 3145732
  211.3 14.3 %collective-permute-start.18 = (bf16[512,512]{1,0:T(8,128)(2,1)S(1)}, bf16[512,512]{1,0:T(8,128)(2,1)S(1)}, u32[]{:S(2)}, u32[]{:S(2)}) collective-permute-start(bf16[512,512]{1,0:T(8,128)(2,1)S(1)} %fusion.7), channel_id=1, source_target_pairs={{0,4},{4,0},{8,12},{12,8},{16,20},{20,16},{24,28},{28,24},{1,5},{5... | collective-permute-start | bytes 1572872 | tf_op jit(solution)/shard_map/ppermute | solution.py:326
  214.8 18.1 %collective-permute-start.14 = (bf16[512,512]{1,0:T(8,128)(2,1)}, bf16[512,512]{1,0:T(8,128)(2,1)}, u32[]{:S(2)}, u32[]{:S(2)}) collective-permute-start(bf16[512,512]{1,0:T(8,128)(2,1)} %fusion.5), channel_id=1, source_target_pairs={{0,8},{4,12},{8,0},{12,4},{16,24},{20,28},{24,16},{28,20},{1,9},{5... | collective-permute-start | bytes 1572872 | tf_op jit(solution)/shard_map/ppermute | solution.py:326
  228.0 18.0 %all-to-all-start.2 = ((bf16[4,128,1024]{2,1,0:T(8,128)(2,1)}), bf16[4,128,1024]{2,1,0:T(8,128)(2,1)S(1)}, u32[]{:S(2)}, u32[]{:S(2)}) async-start(bf16[4,128,1024]{2,1,0:T(8,128)(2,1)} %bitcast.80), calls=%async_computation.2 | async-start | bytes 2097152 | tf_op jit(solution)/shard_map/all_to_all | solution.py:466
  245.9 18.0 %all-to-all-start.1 = ((bf16[4,128,1024]{2,1,0:T(8,128)(2,1)}), bf16[4,128,1024]{2,1,0:T(8,128)(2,1)S(1)}, u32[]{:S(2)}, u32[]{:S(2)}) async-start(bf16[4,128,1024]{2,1,0:T(8,128)(2,1)} %bitcast.24), calls=%async_computation.1 | async-start | bytes 2097152 | tf_op jit(solution)/shard_map/all_to_all | solution.py:466
  (3 other events, 9.4 us)

commit v4 on v3

--- a/solution.py
+++ b/solution.py
@@ -12,7 +12,7 @@
 BS = 64
 GROUP = 4
 BATCH = 8
-CHUNKS = 2
+CUTS = (0.0, 0.5, 1.0)
 JOINED = 4
 LOG2E = math.log2(math.e)
 SCALE = DH**-0.5
@@ -136,7 +136,7 @@
     (dq_own,) = take(1)
     dq_far = take(remote)
     dk_keep, dk_send, dv_keep, dv_send = take(4)
-    q_rows, g_rows, k_rows, v_rows, dq_sum, dk_sum, dv_sum, listed = refs
+    q_rows, g_rows, k_rows, v_rows, dq_sum, dk_sum, dv_sum, w_kept, ds_kept, listed = refs
     head = pl.program_id(0) + head0
     me = meta[0]
     pos = lax.rem(me, GROUP)
@@ -176,11 +176,103 @@
                 found = edge_block(src, b, blocks, seq_count, group, group_blocks)
                 if found is not None:
                     count = note(count, item, *found)
-    for u in range(BATCH):
+    for u in range(2 * BATCH):
         listed[0, count + u] = 0
         listed[1, count + u] = 0
 
     lane = lax.broadcasted_iota(jnp.int32, (1, 2 * BS), 1)
+
+    globs = [local_block(meta[1 + j], group, group_blocks) for j in range(2)]
+    wide = 4 * BS if blocks % 4 == 0 else 2 * BS
+
+    @pl.when(globs[0][1] | globs[1][1])
+    def _():
+        spans = [pl.ds(aligned(BS + p * BS), BS) for p, _ in globs]
+        k = jnp.concatenate([k_rows[s, :] for s in spans], axis=0)
+        v = jnp.concatenate([v_rows[s, :] for s in spans], axis=0)
+        off = [jnp.where(inside, 0.0, OFF) for _, inside in globs]
+        dk = jnp.zeros((2 * BS, DH), jnp.float32)
+        dv = jnp.zeros((2 * BS, DH), jnp.float32)
+        for r in range(sources):
+            for t in range(tokens // wide):
+                rows = pl.ds(r * tokens + t * wide, wide)
+                q, g = q_rows[rows, :], g_rows[rows, :]
+                norm = norm_flat[r, 0, :, t * wide : (t + 1) * wide]
+                rdot = dot_flat[r, 0, :, t * wide : (t + 1) * wide]
+                s = dot(k, q, NT) * c2
+                w = jnp.concatenate(
+                    [jnp.exp2(s[:BS] - (norm + off[0])), jnp.exp2(s[BS:] - (norm + off[1]))],
+                    axis=0,
+                )
+                ds = w * (dot(v, g, NT) - rdot)
+                wb, dsb = w.astype(jnp.bfloat16), ds.astype(jnp.bfloat16)
+                dq_sum[rows, :] += dot(dsb, k, TN)
+                dk = dk + dot(dsb, q)
+                dv = dv + dot(wb, g)
+        for j, span in enumerate(spans):
+            dk_sum[span, :] += dk[j * BS : (j + 1) * BS]
+            dv_sum[span, :] += dv[j * BS : (j + 1) * BS]
+
+    def places(step):
+        rows, spans = [], []
+        for u in range(BATCH):
+            rows.append(pl.ds(aligned(listed[0, step * BATCH + u] * BS), BS))
+            spans.append(pl.ds(aligned(BS + listed[1, step * BATCH + u] * BS), BS))
+        return rows, spans
+
+    def joined(ref, slices):
+        return jnp.concatenate([ref[x, :] for x in slices], axis=0)
+
+    def weigh(step):
+        rows, spans = places(step)
+        weighed = []
+        for first in range(0, BATCH, JOINED):
+            these = slice(first, first + JOINED)
+            s = dot(joined(k_rows, spans[these]), joined(q_rows, rows[these]), NT)
+            dw = dot(joined(v_rows, spans[these]), joined(g_rows, rows[these]), NT)
+            for t in range(JOINED // 2):
+                norms, dots = [], []
+                for u in (first + 2 * t, first + 2 * t + 1):
+                    item = listed[0, step * BATCH + u]
+                    off = jnp.where(step * BATCH + u < count, 0.0, OFF)
+                    norms.append(norm_ref[0, pl.ds(item, 1), :] + off)
+                    dots.append(dot_ref[0, pl.ds(item, 1), :])
+                part = slice(t * 2 * BS, (t + 1) * 2 * BS)
+                both = s[part, part] * c2
+                w = jnp.concatenate(
+                    [
+                        jnp.exp2(both[:BS] - jnp.where(lane < BS, norms[0], OFF)),
+                        jnp.exp2(both[BS:] - jnp.where(lane < BS, OFF, norms[1])),
+                    ],
+                    axis=0,
+                )
+                ds = w * (dw[part, part] - jnp.where(lane < BS, dots[0], dots[1]))
+                weighed.append((w.astype(jnp.bfloat16), ds.astype(jnp.bfloat16)))
+        return weighed
+
+    def keep_weighed(weighed):
+        for t, (w, ds) in enumerate(weighed):
+            w_kept[t], ds_kept[t] = w, ds
+
+    def batch(step, carry):
+        held = [(w_kept[t], ds_kept[t]) for t in range(BATCH // 2)]
+        following = weigh(step + 1)
+        rows, spans = places(step)
+        done = []
+        for t, (wb, dsb) in enumerate(held):
+            pair = slice(2 * t, 2 * t + 2)
+            q, g, k = joined(q_rows, rows[pair]), joined(g_rows, rows[pair]), joined(k_rows, spans[pair])
+            done.append((dot(dsb, k, TN), dot(dsb, q), dot(wb, g)))
+        keep_weighed(following)
+        for u in range(BATCH):
+            dq, dk, dv = done[u // 2]
+            part = slice((u % 2) * BS, (u % 2 + 1) * BS)
+            dq_sum[rows[u], :] += dq[part]
+            dk_sum[spans[u], :] += dk[part]
+            dv_sum[spans[u], :] += dv[part]
+        return carry
+
+    keep_weighed(weigh(0))
     pairs = blocks // 2
     for t in range(pairs):
         rows = pl.ds(t * 2 * BS, 2 * BS)
@@ -211,83 +303,6 @@
         dk_sum[span, :] += dot(dsb, q)
         dv_sum[span, :] += dot(wb, g)
 
-    globs = [local_block(meta[1 + j], group, group_blocks) for j in range(2)]
-    wide = 4 * BS if blocks % 4 == 0 else 2 * BS
-
-    @pl.when(globs[0][1] | globs[1][1])
-    def _():
-        spans = [pl.ds(aligned(BS + p * BS), BS) for p, _ in globs]
-        k = jnp.concatenate([k_rows[s, :] for s in spans], axis=0)
-        v = jnp.concatenate([v_rows[s, :] for s in spans], axis=0)
-        off = [jnp.where(inside, 0.0, OFF) for _, inside in globs]
-        dk = jnp.zeros((2 * BS, DH), jnp.float32)
-        dv = jnp.zeros((2 * BS, DH), jnp.float32)
-        for r in range(sources):
-            for t in range(tokens // wide):
-                rows = pl.ds(r * tokens + t * wide, wide)
-                q, g = q_rows[rows, :], g_rows[rows, :]
-                norm = norm_flat[r, 0, :, t * wide : (t + 1) * wide]
-                rdot = dot_flat[r, 0, :, t * wide : (t + 1) * wide]
-                s = dot(k, q, NT) * c2
-                w = jnp.concatenate(
-                    [jnp.exp2(s[:BS] - (norm + off[0])), jnp.exp2(s[BS:] - (norm + off[1]))],
-                    axis=0,
-                )
-                ds = w * (dot(v, g, NT) - rdot)
-                wb, dsb = w.astype(jnp.bfloat16), ds.astype(jnp.bfloat16)
-                dq_sum[rows, :] += dot(dsb, k, TN)
-                dk = dk + dot(dsb, q)
-                dv = dv + dot(wb, g)
-        for j, span in enumerate(spans):
-            dk_sum[span, :] += dk[j * BS : (j + 1) * BS]
-            dv_sum[span, :] += dv[j * BS : (j + 1) * BS]
-
-    def batch(step, carry):
-        done = []
-        for first in range(0, BATCH, JOINED):
-            rows, spans, norms, dots = [], [], [], []
-            for u in range(first, first + JOINED):
-                i = step * BATCH + u
-                item = listed[0, i]
-                rows.append(pl.ds(aligned(item * BS), BS))
-                spans.append(pl.ds(aligned(BS + listed[1, i] * BS), BS))
-                norms.append(norm_ref[0, pl.ds(item, 1), :] + jnp.where(i < count, 0.0, OFF))
-                dots.append(dot_ref[0, pl.ds(item, 1), :])
-            q = jnp.concatenate([q_rows[x, :] for x in rows], axis=0)
-            g = jnp.concatenate([g_rows[x, :] for x in rows], axis=0)
-            k = jnp.concatenate([k_rows[x, :] for x in spans], axis=0)
-            v = jnp.concatenate([v_rows[x, :] for x in spans], axis=0)
-            s, dw = dot(k, q, NT), dot(v, g, NT)
-            w_diag, ds_diag = [], []
-            for t in range(JOINED // 2):
-                part = slice(t * 2 * BS, (t + 1) * 2 * BS)
-                both = s[part, part] * c2
-                w = jnp.concatenate(
-                    [
-                        jnp.exp2(both[:BS] - jnp.where(lane < BS, norms[2 * t], OFF)),
-                        jnp.exp2(both[BS:] - jnp.where(lane < BS, OFF, norms[2 * t + 1])),
-                    ],
-                    axis=0,
-                )
-                ds = w * (dw[part, part] - jnp.where(lane < BS, dots[2 * t], dots[2 * t + 1]))
-                w_diag.append(w.astype(jnp.bfloat16))
-                ds_diag.append(ds.astype(jnp.bfloat16))
-
-            def each(left, right, dims=(((1,), (0,)), ((), ()))):
-                pieces = [
-                    dot(x, right[t * 2 * BS : (t + 1) * 2 * BS], dims) for t, x in enumerate(left)
-                ]
-                return jnp.concatenate(pieces, axis=0)
-
-            done.append((rows, spans, each(ds_diag, k, TN), each(ds_diag, q), each(w_diag, g)))
-        for rows, spans, dq, dk, dv in done:
-            for u in range(JOINED):
-                part = slice(u * BS, (u + 1) * BS)
-                dq_sum[rows[u], :] += dq[part]
-                dk_sum[spans[u], :] += dk[part]
-                dv_sum[spans[u], :] += dv[part]
-        return carry
-
     lax.fori_loop(0, (count + BATCH - 1) // BATCH, batch, 0)
 
     dq_own[...] = dq_sum[pl.ds(0, tokens), :] * SCALE
@@ -331,7 +346,8 @@
     def whole(array, place=None):
         return [(array, place, 0)]
 
-    count = heads // CHUNKS
+    cuts = [round(heads * x) for x in CUTS]
+    chunks = list(zip(cuts[:-1], cuts[1:]))
     k_z = flip(key_states, 2)
     q_all = whole(queries)
     for r in range(1, sources):
@@ -342,11 +358,11 @@
     v_chunks, previous = [], k_z
     g_all = whole(grad_out)
     for r in range(1, sources):
-        g_all += whole(shift(after(grad_out, k_z), r))
-    for c in range(CHUNKS):
-        cut = slice(c * count * DH, (c + 1) * count * DH)
+        g_all += whole(shift(grad_out, r))
+    for c, (low, high) in enumerate(chunks):
+        cut = slice(low * DH, high * DH)
         v = after(value_states[:, cut], previous)
-        own = [(value_states, None, c * count), (kv_x, 1, c * count)]
+        own = [(value_states, None, low), (kv_x, 1, low)]
         if c == 0:
             v_z = flip(v, 2)
             v_all = own + [(v_z, None, 0), (flip(v_z, 1), None, 0)]
@@ -409,7 +425,7 @@
         return array.reshape(sources, heads, 1, tokens)
 
     def gradients(c):
-        head0 = c * count
+        head0, count = chunks[c][0], chunks[c][1] - chunks[c][0]
         width = count * DH
         item_spec = pl.BlockSpec((1, sources * blocks, 2 * BS), lambda h, *_: (h + head0, 0, 0))
         flat_spec = pl.BlockSpec((sources, 1, 1, tokens), lambda h, *_: (0, h + head0, 0, 0))
@@ -436,7 +452,9 @@
                     pltpu.VMEM((sources * tokens, DH), jnp.float32),
                     pltpu.VMEM(padded_rows, jnp.float32),
                     pltpu.VMEM(padded_rows, jnp.float32),
-                    pltpu.SMEM((2, sources * (3 * blocks + 2) + BATCH), jnp.int32),
+                    pltpu.VMEM((BATCH // 2, 2 * BS, 2 * BS), jnp.bfloat16),
+                    pltpu.VMEM((BATCH // 2, 2 * BS, 2 * BS), jnp.bfloat16),
+                    pltpu.SMEM((2, sources * (3 * blocks + 2) + 2 * BATCH), jnp.int32),
                 ],
             ),
             out_shape=[jax.ShapeDtypeStruct((tokens, width), jnp.float32)]
@@ -466,7 +484,7 @@
         return lax.all_to_all(array, "head", split_axis=0, concat_axis=1, tiled=True)
 
     dq_parts, dk_parts, dv_parts = [], [], []
-    for c in range(CHUNKS):
+    for c in range(len(chunks)):
         outs = gradients(c)
         dq, dq_far = outs[0], outs[1:sources]
         dk_keep, dk_send, dv_keep, dv_send = outs[sources:]

time: 265 us -> 260 us (0.981)
  Pallas kernels: 64.8 us -> 47.3 us
  waiting for transfers between devices: 129 us -> 136 us
  starting transfers between devices: 39.1 us -> 41.8 us
    pallas_call x2, Pallas kernels: 52.7 us -> 35.2 us  [gradients(): pl.pallas_call(partial(grads_kernel, sizes, head0), grid_spec=pltpu.Prefe...]
    ppermute x14, waiting for transfers between devices: 63.9 us -> 69.7 us  [flip(): return lax.ppermute(array, 'seq', [(i, i ^ j) for i in range(seq_count)])]
    ppermute x5, starting transfers between devices: 9.51 us -> 13.8 us  [shift(): return lax.ppermute(array, 'seq', pairs)]
  transfers between devices with their start and end apart: 22 -> 22, of which waited for: 9 -> 8; matrix products, arithmetic and copies ran while one was open for 11% -> 12% of each run, Pallas kernels for 24% -> 18%
where the time goes in v4:
time: 260 us; the launch traced here: 259 us
  waiting for transfers between devices  136 us (52%)
  Pallas kernels  47.3 us (18%)
  starting transfers between devices  41.8 us (16%)
  other arithmetic  23.1 us (9%)
  local copies, waits for them, and re-layouts  10.1 us (4%)
    ppermute x14, waiting for transfers between devices, flip(): return lax.ppermute(array, 'seq', [(i, i ^ j) for i in range(seq_count)])  69.7 us
    ppermute x5, waiting for transfers between devices, shift(): return lax.ppermute(array, 'seq', pairs)  44.5 us
    pallas_call x2, Pallas kernels, gradients(): pl.pallas_call(partial(grads_kernel, sizes, head0), grid_spec=pltpu.Prefe...  35.2 us
    all_to_all x3, waiting for transfers between devices, to_tokens(): lax.all_to_all(array, 'head', split_axis=0, concat_axis=1, tiled=True)  21.6 us
    ppermute x14, starting transfers between devices, flip(): return lax.ppermute(array, 'seq', [(i, i ^ j) for i in range(seq_count)])  16.8 us
    ppermute x5, starting transfers between devices, shift(): return lax.ppermute(array, 'seq', pairs)  13.8 us
    pallas_call x1, Pallas kernels, on_device(): pl.pallas_call(partial(norm_kernel, sizes), grid_spec=pltpu.PrefetchScala...  12.2 us
    all_to_all x3, starting transfers between devices, to_tokens(): lax.all_to_all(array, 'head', split_axis=0, concat_axis=1, tiled=True)  11.3 us
  transfers between devices with their start and end apart: 22, of which 8 were waited for; matrix products, arithmetic and copies ran while one was open for 12% of the time, Pallas kernels for 18%

profile of v4, /device:TPU:8, one launch (start us, length us, event | category | flops | bytes accessed | tf_op | source)
XLA Modules:
  0.0 259.2 jit_solution(15052571362296603443)
XLA Ops:
  0.7 3.2 %pad_maximum_fusion = bf16[2,512,1024]{2,1,0:T(8,128)(2,1)} fusion(bf16[1,512,1024]{2,1,0:T(8,128)(2,1)} %bitcast.76, bf16[1,512,1024]{2,1,0:T(8,128)(2,1)} %bitcast.75), kind=kLoop, calls=%fused_computation | loop fusion | flops 1048576 | bytes 4194304 | tf_op jit(solution)/shard_map/stack | solution.py:355
  4.0 1.9 collective-permute-start.2
  5.9 2.6 collective-permute-start
  8.4 33.4 %collective-permute-done.3.refs_4_.refs_6_ = bf16[512,1024]{1,0:T(8,128)(2,1)S(1)} collective-permute-done((bf16[512,1024]{1,0:T(8,128)(2,1)}, bf16[512,1024]{1,0:T(8,128)(2,1)S(1)}, u32[]{:S(2)}, u32[]{:S(2)}) %collective-permute-start.3) | collective-permute-done | bytes 1048608 | tf_op jit(solution)/shard_map/ppermute | solution.py:341
  41.9 2.6 %collective-permute-start.4 = (bf16[512,1024]{1,0:T(8,128)(2,1)S(1)}, bf16[512,1024]{1,0:T(8,128)(2,1)}, u32[]{:S(2)}, u32[]{:S(2)}) collective-permute-start(bf16[512,1024]{1,0:T(8,128)(2,1)S(1)} %collective-permute-done.3.refs_4_.refs_6_), channel_id=1, source_target_pairs={{0,4},{4,0},{8,12},{12,8},{16,20},{20,16},{24,28},{28,24},{1,5},{5... | collective-permute-start | bytes 3145736 | tf_op jit(solution)/shard_map/ppermute | solution.py:341
  44.5 3.4 %collective-permute-start.1 = (bf16[512,1024]{1,0:T(8,128)(2,1)}, bf16[512,1024]{1,0:T(8,128)(2,1)}, u32[]{:S(2)}, u32[]{:S(2)}) collective-permute-start(bf16[512,1024]{1,0:T(8,128)(2,1)} %refs_2_.5), channel_id=1, source_target_pairs={{0,16},{4,20},{8,24},{12,28},{16,0},{20,4},{24,8},{28,12},{1,17},{... | collective-permute-start | bytes 3145736 | tf_op jit(solution)/shard_map/ppermute | solution.py:338
  49.9 1.6 multiply_bitcast_fusion
  51.5 1.8 copy.32
  53.3 2.3 reduce_sum.27
  55.9 26.2 %collective-permute-done.5.refs_10_ = bf16[512,512]{1,0:T(8,128)(2,1)} collective-permute-done((bf16[512,512]{1,0:T(8,128)(2,1)}, bf16[512,512]{1,0:T(8,128)(2,1)}, u32[]{:S(2)}, u32[]{:S(2)}) %collective-permute-start.5) | collective-permute-done | bytes 524320 | tf_op jit(solution)/shard_map/ppermute | solution.py:341
  82.1 1.5 collective-permute-start.6
  83.7 12.2 %partial_norms.1 = f32[2,8,8,64]{3,2,1,0:T(8,128)S(1)} custom-call(s32[3]{0:T(128)S(1)} %pad_add_fusion.meta, s32[1536]{0:T(1024)S(1)} %reshape.99.table, bf16[512,1024]{1,0:T(8,128)(2,1)S(1)} %copy-done.1, bf16[512,1024]{1,0:T(8,128)(2,1)} %collective-permute-done.refs_1_, bf16[512,1024]{1,0:T(8,128)(2,1)S(1)} %copy-done, ...), custom_call_target="tpu_custom_call" | custom-call | tf_op jit(solution)/shard_map/partial_norms/pallas_call | solution.py:389
  96.5 1.3 slice_bitcast_fusion
  98.9 2.5 collective-permute-start.9
  102.7 18.3 %gradients.2 = (f32[512,512]{1,0:T(8,128)S(1)}, bf16[512,512]{1,0:T(8,128)(2,1)S(1)}, bf16[2,512,512]{2,1,0:T(8,128)(2,1)S(1)}, bf16[2,512,512]{2,1,0:T(8,128)(2...) custom-call(s32[3]{0:T(128)S(1)} %pad_add_fusion.meta, s32[1536]{0:T(1024)S(1)} %reshape.99.table, ...), custom_call_target="tpu_custom_call" | custom-call | tf_op jit(solution)/shard_map/gradients/pallas_call | solution.py:435
  122.2 7.2 %collective-permute-start.8 = (bf16[512,512]{1,0:T(8,128)(2,1)S(1)}, bf16[512,512]{1,0:T(8,128)(2,1)S(1)}, u32[]{:S(2)}, u32[]{:S(2)}) collective-permute-start(bf16[512,512]{1,0:T(8,128)(2,1)S(1)} %get-tuple-element.19), channel_id=1, source_target_pairs={{0,16},{4,20},{8,24},{12,28},{16,0},{20,4},{24,8},{28,12},{1,17},{... | collective-permute-start | bytes 1572872 | tf_op jit(solution)/shard_map/ppermute | solution.py:338
  130.2 16.9 %gradients.3 = (f32[512,512]{1,0:T(8,128)S(1)}, bf16[512,512]{1,0:T(8,128)(2,1)S(1)}, bf16[2,512,512]{2,1,0:T(8,128)(2,1)S(1)}, bf16[2,512,512]{2,1,0:T(8,128)(2...) custom-call(s32[3]{0:T(128)S(1)} %pad_add_fusion.meta, s32[1536]{0:T(1024)S(1)} %reshape.99.table, ...), custom_call_target="tpu_custom_call" | custom-call | tf_op jit(solution)/shard_map/gradients/pallas_call | solution.py:435
  147.1 3.2 %collective-permute-start.17 = (bf16[2,512,512]{2,1,0:T(8,128)(2,1)}, bf16[2,512,512]{2,1,0:T(8,128)(2,1)}, u32[]{:S(2)}, u32[]{:S(2)}) collective-permute-start(bf16[2,512,512]{2,1,0:T(8,128)(2,1)} %get-tuple-element.30), channel_id=1, source_target_pairs={{0,8},{4,12},{8,0},{12,4},{16,24},{20,28},{24,16},{28,20},{1,9},{5... | collective-permute-start | bytes 3145736 | tf_op jit(solution)/shard_map/ppermute | solution.py:341
  150.4 14.5 %collective-permute-done.8 = bf16[512,512]{1,0:T(8,128)(2,1)S(1)} collective-permute-done((bf16[512,512]{1,0:T(8,128)(2,1)S(1)}, bf16[512,512]{1,0:T(8,128)(2,1)S(1)}, u32[]{:S(2)}, u32[]{:S(2)}) %collective-permute-start.8) | collective-permute-done | bytes 524320 | tf_op jit(solution)/shard_map/ppermute | solution.py:338
  169.3 29.3 %collective-permute-done.10 = bf16[512,512]{1,0:T(8,128)(2,1)S(1)} collective-permute-done((bf16[512,512]{1,0:T(8,128)(2,1)S(1)}, bf16[512,512]{1,0:T(8,128)(2,1)S(1)}, u32[]{:S(2)}, u32[]{:S(2)}) %collective-permute-start.10) | collective-permute-done | bytes 524320 | tf_op jit(solution)/shard_map/ppermute | solution.py:338
  199.9 4.2 %all-to-all-start = ((bf16[4,128,1024]{2,1,0:T(8,128)(2,1)}), bf16[4,128,1024]{2,1,0:T(8,128)(2,1)}, u32[]{:S(2)}, u32[]{:S(2)}) async-start(bf16[4,128,1024]{2,1,0:T(8,128)(2,1)} %bitcast.78), calls=%async_computation | async-start | bytes 2097152 | tf_op jit(solution)/shard_map/all_to_all | solution.py:484
  204.2 1.3 fusion.7
  206.4 1.4 fusion.1
  207.8 2.0 fusion.5
  209.8 10.1 %collective-permute-done.18 = bf16[512,512]{1,0:T(8,128)(2,1)S(1)} collective-permute-done((bf16[512,512]{1,0:T(8,128)(2,1)S(1)}, bf16[512,512]{1,0:T(8,128)(2,1)S(1)}, u32[]{:S(2)}, u32[]{:S(2)}) %collective-permute-start.18) | collective-permute-done | bytes 524320 | tf_op jit(solution)/shard_map/ppermute | solution.py:341
  222.2 3.5 %all-to-all-start.2 = ((bf16[4,128,1024]{2,1,0:T(8,128)(2,1)}), bf16[4,128,1024]{2,1,0:T(8,128)(2,1)S(1)}, u32[]{:S(2)}, u32[]{:S(2)}) async-start(bf16[4,128,1024]{2,1,0:T(8,128)(2,1)} %bitcast.80), calls=%async_computation.2 | async-start | bytes 2097152 | tf_op jit(solution)/shard_map/all_to_all | solution.py:484
  225.8 1.4 fusion.3
  227.2 1.4 fusion.2
  229.7 10.5 %all-to-all-done.2 = bf16[4,128,1024]{2,1,0:T(8,128)(2,1)S(1)} async-done(((bf16[4,128,1024]{2,1,0:T(8,128)(2,1)}), bf16[4,128,1024]{2,1,0:T(8,128)(2,1)S(1)}, u32[]{:S(2)}, u32[]{:S(2)}) %all-to-all-start.2) | async-done | bytes 1048608 | tf_op jit(solution)/shard_map/all_to_all | solution.py:484
  240.2 3.5 %all-to-all-start.1 = ((bf16[4,128,1024]{2,1,0:T(8,128)(2,1)}), bf16[4,128,1024]{2,1,0:T(8,128)(2,1)S(1)}, u32[]{:S(2)}, u32[]{:S(2)}) async-start(bf16[4,128,1024]{2,1,0:T(8,128)(2,1)} %bitcast.24), calls=%async_computation.1 | async-start | bytes 2097152 | tf_op jit(solution)/shard_map/all_to_all | solution.py:484
  243.7 2.3 copy.29
  247.0 11.1 %all-to-all-done.1 = bf16[4,128,1024]{2,1,0:T(8,128)(2,1)S(1)} async-done(((bf16[4,128,1024]{2,1,0:T(8,128)(2,1)}), bf16[4,128,1024]{2,1,0:T(8,128)(2,1)S(1)}, u32[]{:S(2)}, u32[]{:S(2)}) %all-to-all-start.1) | async-done | bytes 1048608 | tf_op jit(solution)/shard_map/all_to_all | solution.py:484
  (83 shorter events, 19.6 us)
Async XLA Ops:
  0.6 41.2 %collective-permute-start.3 = (bf16[512,1024]{1,0:T(8,128)(2,1)}, bf16[512,1024]{1,0:T(8,128)(2,1)S(1)}, u32[]{:S(2)}, u32[]{:S(2)}) collective-permute-start(bf16[512,1024]{1,0:T(8,128)(2,1)} %refs_4_.3), channel_id=1, source_target_pairs={{0,8},{4,12},{8,0},{12,4},{16,24},{20,28},{24,16},{28,20},{1,9},{5... | collective-permute-start | bytes 3145736 | tf_op jit(solution)/shard_map/ppermute | solution.py:341
  0.7 5.1 %copy-start.1 = (bf16[512,1024]{1,0:T(8,128)(2,1)S(1)}, bf16[512,1024]{1,0:T(8,128)(2,1)}, u32[]{:S(2)}) copy-start(bf16[512,1024]{1,0:T(8,128)(2,1)} %refs_0_.5) | copy-start | bytes 3145732
  0.7 47.1 %copy-start.10 = (s32[64,8,3]{0,1,2:T(8,128)S(1)}, s32[64,8,3]{0,1,2:T(8,128)}, u32[]{:S(2)}) copy-start(s32[64,8,3]{0,1,2:T(8,128)} %param.12) | copy-start | bytes 18436
  0.7 47.5 %copy-start.5 = (bf16[512,1024]{1,0:T(8,128)(2,1)S(1)}, bf16[512,1024]{1,0:T(8,128)(2,1)}, u32[]{:S(2)}) copy-start(bf16[512,1024]{1,0:T(8,128)(2,1)} %refs_8_.3) | copy-start | bytes 3145732
  4.0 79.7 %collective-permute-start.2 = (bf16[2,512,1024]{2,1,0:T(8,128)(2,1)}, bf16[2,512,1024]{2,1,0:T(8,128)(2,1)}, u32[]{:S(2)}, u32[]{:S(2)}) collective-permute-start(bf16[2,512,1024]{2,1,0:T(8,128)(2,1)} %pad_maximum_fusion), channel_id=1, source_target_pairs={{0,4},{4,0},{8,12},{12,8},{16,20},{20,16},{24,28},{28,24},{1,5},{5... | collective-permute-start | bytes 6291464 | tf_op jit(solution)/shard_map/ppermute | solution.py:341
  5.9 77.8 %collective-permute-start = (bf16[512,1024]{1,0:T(8,128)(2,1)S(1)}, bf16[512,1024]{1,0:T(8,128)(2,1)}, u32[]{:S(2)}, u32[]{:S(2)}) collective-permute-start(bf16[512,1024]{1,0:T(8,128)(2,1)S(1)} %copy-done.1), channel_id=1, source_target_pairs={{0,16},{4,20},{8,24},{12,28},{16,0},{20,4},{24,8},{28,12},{1,17},{... | collective-permute-start | bytes 3145736 | tf_op jit(solution)/shard_map/ppermute | solution.py:338
  41.8 41.8 %copy-start.2 = (bf16[512,1024]{1,0:T(8,128)(2,1)}, bf16[512,1024]{1,0:T(8,128)(2,1)S(1)}, u32[]{:S(2)}) copy-start(bf16[512,1024]{1,0:T(8,128)(2,1)S(1)} %collective-permute-done.3.refs_4_.refs_6_) | copy-start | bytes 3145732
  41.9 41.8 %collective-permute-start.4 = (bf16[512,1024]{1,0:T(8,128)(2,1)S(1)}, bf16[512,1024]{1,0:T(8,128)(2,1)}, u32[]{:S(2)}, u32[]{:S(2)}) collective-permute-start(bf16[512,1024]{1,0:T(8,128)(2,1)S(1)} %collective-permute-done.3.refs_4_.refs_6_), channel_id=1, source_target_pairs={{0,4},{4,0},{8,12},{12,8},{16,20},{20,16},{24,28},{28,24},{1,5},{5... | collective-permute-start | bytes 3145736 | tf_op jit(solution)/shard_map/ppermute | solution.py:341
  44.5 58.2 %collective-permute-start.1 = (bf16[512,1024]{1,0:T(8,128)(2,1)}, bf16[512,1024]{1,0:T(8,128)(2,1)}, u32[]{:S(2)}, u32[]{:S(2)}) collective-permute-start(bf16[512,1024]{1,0:T(8,128)(2,1)} %refs_2_.5), channel_id=1, source_target_pairs={{0,16},{4,20},{8,24},{12,28},{16,0},{20,4},{24,8},{28,12},{1,17},{... | collective-permute-start | bytes 3145736 | tf_op jit(solution)/shard_map/ppermute | solution.py:338
  49.3 32.8 %collective-permute-start.5 = (bf16[512,512]{1,0:T(8,128)(2,1)}, bf16[512,512]{1,0:T(8,128)(2,1)}, u32[]{:S(2)}, u32[]{:S(2)}) collective-permute-start(bf16[512,512]{1,0:T(8,128)(2,1)} %get-tuple-element.17), channel_id=1, source_target_pairs={{0,8},{4,12},{8,0},{12,4},{16,24},{20,28},{24,16},{28,20},{1,9},{5... | collective-permute-start | bytes 1572872 | tf_op jit(solution)/shard_map/ppermute | solution.py:341
  53.3 2.5 copy-start.11
  53.3 30.3 %copy-start = (bf16[512,1024]{1,0:T(8,128)(2,1)S(1)}, bf16[512,1024]{1,0:T(8,128)(2,1)}, u32[]{:S(2)}) copy-start(bf16[512,1024]{1,0:T(8,128)(2,1)} %refs_4_.3) | copy-start | bytes 3145732
  82.1 20.6 %collective-permute-start.6 = (bf16[512,512]{1,0:T(8,128)(2,1)}, bf16[512,512]{1,0:T(8,128)(2,1)}, u32[]{:S(2)}, u32[]{:S(2)}) collective-permute-start(bf16[512,512]{1,0:T(8,128)(2,1)} %collective-permute-done.5.refs_10_), channel_id=1, source_target_pairs={{0,4},{4,0},{8,12},{12,8},{16,20},{20,16},{24,28},{28,24},{1,5},{5... | collective-permute-start | bytes 1572872 | tf_op jit(solution)/shard_map/ppermute | solution.py:341
  95.9 6.2 %collective-permute-start.7 = (f32[3,8,8,64]{3,2,1,0:T(8,128)S(1)}, f32[3,8,8,64]{3,2,1,0:T(8,128)S(1)}, u32[]{:S(2)}, u32[]{:S(2)}) collective-permute-start(f32[3,8,8,64]{3,2,1,0:T(8,128)S(1)} %pad_maximum_fusion.5), channel_id=1, source_target_pairs={{0,16},{4,20},{8,24},{12,28},{16,0},{20,4},{24,8},{28,12},{1,17},{... | collective-permute-start | bytes 147464 | tf_op jit(solution)/shard_map/ppermute | solution.py:338
  98.9 31.3 %collective-permute-start.9 = (bf16[2,512,512]{2,1,0:T(8,128)(2,1)}, bf16[2,512,512]{2,1,0:T(8,128)(2,1)}, u32[]{:S(2)}, u32[]{:S(2)}) collective-permute-start(bf16[2,512,512]{2,1,0:T(8,128)(2,1)} %pad_maximum_fusion.1), channel_id=1, source_target_pairs={{0,8},{4,12},{8,0},{12,4},{16,24},{20,28},{24,16},{28,20},{1,9},{5... | collective-permute-start | bytes 3145736 | tf_op jit(solution)/shard_map/ppermute | solution.py:341
  121.0 44.9 %collective-permute-start.15 = (bf16[2,512,512]{2,1,0:T(8,128)(2,1)}, bf16[2,512,512]{2,1,0:T(8,128)(2,1)S(1)}, u32[]{:S(2)}, u32[]{:S(2)}) collective-permute-start(bf16[2,512,512]{2,1,0:T(8,128)(2,1)} %get-tuple-element.28), channel_id=1, source_target_pairs={{0,8},{4,12},{8,0},{12,4},{16,24},{20,28},{24,16},{28,20},{1,9},{5... | collective-permute-start | bytes 3145736 | tf_op jit(solution)/shard_map/ppermute | solution.py:341
  122.2 42.7 %collective-permute-start.8 = (bf16[512,512]{1,0:T(8,128)(2,1)S(1)}, bf16[512,512]{1,0:T(8,128)(2,1)S(1)}, u32[]{:S(2)}, u32[]{:S(2)}) collective-permute-start(bf16[512,512]{1,0:T(8,128)(2,1)S(1)} %get-tuple-element.19), channel_id=1, source_target_pairs={{0,16},{4,20},{8,24},{12,28},{16,0},{20,4},{24,8},{28,12},{1,17},{... | collective-permute-start | bytes 1572872 | tf_op jit(solution)/shard_map/ppermute | solution.py:338
  129.4 38.9 %collective-permute-start.11 = (bf16[2,512,512]{2,1,0:T(8,128)(2,1)S(1)}, bf16[2,512,512]{2,1,0:T(8,128)(2,1)S(1)}, u32[]{:S(2)}, u32[]{:S(2)}) collective-permute-start(bf16[2,512,512]{2,1,0:T(8,128)(2,1)S(1)} %get-tuple-element.24), channel_id=1, source_target_pairs={{0,4},{4,0},{8,12},{12,8},{16,20},{20,16},{24,28},{28,24},{1,5},{5... | collective-permute-start | bytes 3145736 | tf_op jit(solution)/shard_map/ppermute | solution.py:341
  147.1 22.2 %copy-start.3 = (bf16[2,512,512]{2,1,0:T(8,128)(2,1)}, bf16[2,512,512]{2,1,0:T(8,128)(2,1)S(1)}, u32[]{:S(2)}) copy-start(bf16[2,512,512]{2,1,0:T(8,128)(2,1)S(1)} %get-tuple-element.29) | copy-start | bytes 3145732
  147.1 57.0 %collective-permute-start.17 = (bf16[2,512,512]{2,1,0:T(8,128)(2,1)}, bf16[2,512,512]{2,1,0:T(8,128)(2,1)}, u32[]{:S(2)}, u32[]{:S(2)}) collective-permute-start(bf16[2,512,512]{2,1,0:T(8,128)(2,1)} %get-tuple-element.30), channel_id=1, source_target_pairs={{0,8},{4,12},{8,0},{12,4},{16,24},{20,28},{24,16},{28,20},{1,9},{5... | collective-permute-start | bytes 3145736 | tf_op jit(solution)/shard_map/ppermute | solution.py:341
  165.1 42.7 %collective-permute-start.13 = (bf16[2,512,512]{2,1,0:T(8,128)(2,1)}, bf16[2,512,512]{2,1,0:T(8,128)(2,1)}, u32[]{:S(2)}, u32[]{:S(2)}) collective-permute-start(bf16[2,512,512]{2,1,0:T(8,128)(2,1)} %get-tuple-element.26), channel_id=1, source_target_pairs={{0,4},{4,0},{8,12},{12,8},{16,20},{20,16},{24,28},{28,24},{1,5},{5... | collective-permute-start | bytes 3145736 | tf_op jit(solution)/shard_map/ppermute | solution.py:341
  165.9 32.7 %collective-permute-start.10 = (bf16[512,512]{1,0:T(8,128)(2,1)S(1)}, bf16[512,512]{1,0:T(8,128)(2,1)S(1)}, u32[]{:S(2)}, u32[]{:S(2)}) collective-permute-start(bf16[512,512]{1,0:T(8,128)(2,1)S(1)} %get-tuple-element.22), channel_id=1, source_target_pairs={{0,16},{4,20},{8,24},{12,28},{16,0},{20,4},{24,8},{28,12},{1,17},{... | collective-permute-start | bytes 1572872 | tf_op jit(solution)/shard_map/ppermute | solution.py:338
  165.9 32.9 %copy-start.8 = (bf16[2,512,512]{2,1,0:T(8,128)(2,1)}, bf16[2,512,512]{2,1,0:T(8,128)(2,1)S(1)}, u32[]{:S(2)}) copy-start(bf16[2,512,512]{2,1,0:T(8,128)(2,1)S(1)} %collective-permute-done.15) | copy-start | bytes 3145732
  167.0 39.3 %collective-permute-start.16 = (bf16[512,512]{1,0:T(8,128)(2,1)}, bf16[512,512]{1,0:T(8,128)(2,1)}, u32[]{:S(2)}, u32[]{:S(2)}) collective-permute-start(bf16[512,512]{1,0:T(8,128)(2,1)} %fusion.6), channel_id=1, source_target_pairs={{0,4},{4,0},{8,12},{12,8},{16,20},{20,16},{24,28},{28,24},{1,5},{5... | collective-permute-start | bytes 1572872 | tf_op jit(solution)/shard_map/ppermute | solution.py:341
  168.3 31.6 %copy-start.7 = (bf16[2,512,512]{2,1,0:T(8,128)(2,1)}, bf16[2,512,512]{2,1,0:T(8,128)(2,1)S(1)}, u32[]{:S(2)}) copy-start(bf16[2,512,512]{2,1,0:T(8,128)(2,1)S(1)} %collective-permute-done.11) | copy-start | bytes 3145732
  169.3 56.4 %collective-permute-start.12 = (bf16[512,512]{1,0:T(8,128)(2,1)}, bf16[512,512]{1,0:T(8,128)(2,1)}, u32[]{:S(2)}, u32[]{:S(2)}) collective-permute-start(bf16[512,512]{1,0:T(8,128)(2,1)} %fusion.4), channel_id=1, source_target_pairs={{0,8},{4,12},{8,0},{12,4},{16,24},{20,28},{24,16},{28,20},{1,9},{5... | collective-permute-start | bytes 1572872 | tf_op jit(solution)/shard_map/ppermute | solution.py:341
  199.9 22.3 %all-to-all-start = ((bf16[4,128,1024]{2,1,0:T(8,128)(2,1)}), bf16[4,128,1024]{2,1,0:T(8,128)(2,1)}, u32[]{:S(2)}, u32[]{:S(2)}) async-start(bf16[4,128,1024]{2,1,0:T(8,128)(2,1)} %bitcast.78), calls=%async_computation | async-start | bytes 2097152 | tf_op jit(solution)/shard_map/all_to_all | solution.py:484
  205.5 14.4 %copy-start.4 = (bf16[2,512,512]{2,1,0:T(8,128)(2,1)S(1)}, bf16[2,512,512]{2,1,0:T(8,128)(2,1)}, u32[]{:S(2)}) copy-start(bf16[2,512,512]{2,1,0:T(8,128)(2,1)} %copy-done.3) | copy-start | bytes 3145732
  205.5 14.3 %collective-permute-start.18 = (bf16[512,512]{1,0:T(8,128)(2,1)S(1)}, bf16[512,512]{1,0:T(8,128)(2,1)S(1)}, u32[]{:S(2)}, u32[]{:S(2)}) collective-permute-start(bf16[512,512]{1,0:T(8,128)(2,1)S(1)} %fusion.7), channel_id=1, source_target_pairs={{0,4},{4,0},{8,12},{12,8},{16,20},{20,16},{24,28},{28,24},{1,5},{5... | collective-permute-start | bytes 1572872 | tf_op jit(solution)/shard_map/ppermute | solution.py:341
  209.8 17.4 %collective-permute-start.14 = (bf16[512,512]{1,0:T(8,128)(2,1)}, bf16[512,512]{1,0:T(8,128)(2,1)}, u32[]{:S(2)}, u32[]{:S(2)}) collective-permute-start(bf16[512,512]{1,0:T(8,128)(2,1)} %fusion.5), channel_id=1, source_target_pairs={{0,8},{4,12},{8,0},{12,4},{16,24},{20,28},{24,16},{28,20},{1,9},{5... | collective-permute-start | bytes 1572872 | tf_op jit(solution)/shard_map/ppermute | solution.py:341
  222.2 18.0 %all-to-all-start.2 = ((bf16[4,128,1024]{2,1,0:T(8,128)(2,1)}), bf16[4,128,1024]{2,1,0:T(8,128)(2,1)S(1)}, u32[]{:S(2)}, u32[]{:S(2)}) async-start(bf16[4,128,1024]{2,1,0:T(8,128)(2,1)} %bitcast.80), calls=%async_computation.2 | async-start | bytes 2097152 | tf_op jit(solution)/shard_map/all_to_all | solution.py:484
  240.2 18.0 %all-to-all-start.1 = ((bf16[4,128,1024]{2,1,0:T(8,128)(2,1)}), bf16[4,128,1024]{2,1,0:T(8,128)(2,1)S(1)}, u32[]{:S(2)}, u32[]{:S(2)}) async-start(bf16[4,128,1024]{2,1,0:T(8,128)(2,1)} %bitcast.24), calls=%async_computation.1 | async-start | bytes 2097152 | tf_op jit(solution)/shard_map/all_to_all | solution.py:484
  (2 other events, 3.6 us)

commit v5 on v4

--- a/solution.py
+++ b/solution.py
@@ -77,36 +77,42 @@
     globs = [local_block(meta[1 + j], group, group_blocks) for j in range(2)]
     glob_keys = [key_rows[pl.ds(aligned(BS + p * BS), BS), :] for p, _ in globs]
 
+    pos = lax.rem(me, GROUP)
+    lane = lax.broadcasted_iota(jnp.int32, (1, 2 * BS), 1)
     for r in range(sources):
         src = lax.rem(me - GROUP * r + seq_count, seq_count)
-        for b in range(blocks):
-            q = q_refs[r][pl.ds(b * BS, BS), :]
-            tiles, ok = [], []
+        for t in range(blocks // 2):
+            q = q_refs[r][pl.ds(t * 2 * BS, 2 * BS), :]
+            tiles, off = [], []
             if r == 0:
-                start = aligned((lax.rem(me, GROUP) * blocks + b) * BS)
-                window = key_rows[pl.ds(start, 3 * BS), :]
-                tiles += [window[j * BS : (j + 1) * BS] for j in range(3)]
-                at_first = (lax.rem(me, GROUP) > 0) if b == 0 else None
-                at_last = (lax.rem(me, GROUP) < GROUP - 1) if b == blocks - 1 else None
-                ok += [at_first, None, at_last]
-            else:
-                found = edge_block(src, b, blocks, seq_count, group, group_blocks)
-                if found is not None:
-                    tiles.append(key_rows[pl.ds(aligned(BS + found[0] * BS), BS), :])
-                    ok.append(found[1])
+                start = aligned((pos * blocks + 2 * t) * BS)
+                tiles.append(key_rows[pl.ds(start, 4 * BS), :])
+                first = jnp.where(pos > 0, 0.0, OFF) if t == 0 else 0.0
+                last = jnp.where(pos < GROUP - 1, 0.0, OFF) if t == blocks // 2 - 1 else 0.0
+                off += [(first, OFF), None, None, (OFF, last)]
             for j in range(2):
                 tiles.append(glob_keys[j])
-                ok.append(globs[j][1])
-            for j in range(3):
-                entry = table[((src * blocks + b) * heads + head) * 3 + j]
-                place, inside = local_block(entry, group, group_blocks)
-                tiles.append(key_rows[pl.ds(aligned(BS + place * BS), BS), :])
-                ok.append(inside)
+                here = jnp.where(globs[j][1], 0.0, OFF)
+                off.append((here, here))
+            for u in range(2):
+                b = 2 * t + u
+                found = [
+                    local_block(table[((src * blocks + b) * heads + head) * 3 + j], group, group_blocks)
+                    for j in range(3)
+                ]
+                edge = edge_block(src, b, blocks, seq_count, group, group_blocks)
+                if r > 0 and edge is not None:
+                    found.append(edge)
+                for place, inside in found:
+                    tiles.append(key_rows[pl.ds(aligned(BS + place * BS), BS), :])
+                    here = jnp.where(inside, 0.0, OFF)
+                    off.append((here, OFF) if u == 0 else (OFF, here))
+            products = dot(jnp.concatenate(tiles, axis=0), q, NT)
             scores = []
-            for tile, flag in zip(tiles, ok):
-                s = dot(tile, q, NT) * c2
-                if flag is not None:
-                    s = s - jnp.where(flag, 0.0, OFF)
+            for j, pair in enumerate(off):
+                s = products[j * BS : (j + 1) * BS] * c2
+                if pair is not None:
+                    s = s - jnp.where(lane < BS, pair[0], pair[1])
                 scores.append(s)
             top = scores[0]
             for s in scores[1:]:
@@ -115,8 +121,9 @@
             total = jnp.exp2(scores[0] - top)
             for s in scores[1:]:
                 total = total + jnp.exp2(s - top)
-            total = jnp.sum(total, axis=0, keepdims=True)
-            out_ref[r, 0, pl.ds(b, 1), :] = top + jnp.log2(total)
+            found = top + jnp.log2(jnp.sum(total, axis=0, keepdims=True))
+            out_ref[r, 0, pl.ds(2 * t, 1), :] = found[:, :BS]
+            out_ref[r, 0, pl.ds(2 * t + 1, 1), :] = found[:, BS:]
 
 
 def grads_kernel(sizes, head0, meta, table, *refs):
@@ -183,35 +190,33 @@
     lane = lax.broadcasted_iota(jnp.int32, (1, 2 * BS), 1)
 
     globs = [local_block(meta[1 + j], group, group_blocks) for j in range(2)]
-    wide = 4 * BS if blocks % 4 == 0 else 2 * BS
-
-    @pl.when(globs[0][1] | globs[1][1])
-    def _():
-        spans = [pl.ds(aligned(BS + p * BS), BS) for p, _ in globs]
-        k = jnp.concatenate([k_rows[s, :] for s in spans], axis=0)
-        v = jnp.concatenate([v_rows[s, :] for s in spans], axis=0)
-        off = [jnp.where(inside, 0.0, OFF) for _, inside in globs]
-        dk = jnp.zeros((2 * BS, DH), jnp.float32)
-        dv = jnp.zeros((2 * BS, DH), jnp.float32)
-        for r in range(sources):
-            for t in range(tokens // wide):
-                rows = pl.ds(r * tokens + t * wide, wide)
-                q, g = q_rows[rows, :], g_rows[rows, :]
-                norm = norm_flat[r, 0, :, t * wide : (t + 1) * wide]
-                rdot = dot_flat[r, 0, :, t * wide : (t + 1) * wide]
-                s = dot(k, q, NT) * c2
-                w = jnp.concatenate(
-                    [jnp.exp2(s[:BS] - (norm + off[0])), jnp.exp2(s[BS:] - (norm + off[1]))],
-                    axis=0,
-                )
-                ds = w * (dot(v, g, NT) - rdot)
-                wb, dsb = w.astype(jnp.bfloat16), ds.astype(jnp.bfloat16)
-                dq_sum[rows, :] += dot(dsb, k, TN)
-                dk = dk + dot(dsb, q)
-                dv = dv + dot(wb, g)
-        for j, span in enumerate(spans):
-            dk_sum[span, :] += dk[j * BS : (j + 1) * BS]
-            dv_sum[span, :] += dv[j * BS : (j + 1) * BS]
+    wide = tokens
+
+    spans = [pl.ds(aligned(BS + p * BS), BS) for p, _ in globs]
+    k = jnp.concatenate([k_rows[s, :] for s in spans], axis=0)
+    v = jnp.concatenate([v_rows[s, :] for s in spans], axis=0)
+    off = [jnp.where(inside, 0.0, OFF) for _, inside in globs]
+    dk = jnp.zeros((2 * BS, DH), jnp.float32)
+    dv = jnp.zeros((2 * BS, DH), jnp.float32)
+    for r in range(sources):
+        for t in range(tokens // wide):
+            rows = pl.ds(r * tokens + t * wide, wide)
+            q, g = q_rows[rows, :], g_rows[rows, :]
+            norm = norm_flat[r, 0, :, t * wide : (t + 1) * wide]
+            rdot = dot_flat[r, 0, :, t * wide : (t + 1) * wide]
+            s = dot(k, q, NT) * c2
+            w = jnp.concatenate(
+                [jnp.exp2(s[:BS] - (norm + off[0])), jnp.exp2(s[BS:] - (norm + off[1]))],
+                axis=0,
+            )
+            ds = w * (dot(v, g, NT) - rdot)
+            wb, dsb = w.astype(jnp.bfloat16), ds.astype(jnp.bfloat16)
+            dq_sum[rows, :] += dot(dsb, k, TN)
+            dk = dk + dot(dsb, q)
+            dv = dv + dot(wb, g)
+    for j, span in enumerate(spans):
+        dk_sum[span, :] += dk[j * BS : (j + 1) * BS]
+        dv_sum[span, :] += dv[j * BS : (j + 1) * BS]
 
     def places(step):
         rows, spans = [], []

time: 260 us -> 256 us (0.985)
    ppermute x5, starting transfers between devices: 13.8 us -> 7.64 us  [shift(): return lax.ppermute(array, 'seq', pairs)]
    ppermute x14, starting transfers between devices: 16.8 us -> 20.3 us  [flip(): return lax.ppermute(array, 'seq', [(i, i ^ j) for i in range(seq_count)])]
    pallas_call x2, Pallas kernels: 35.2 us -> 37.9 us  [gradients(): pl.pallas_call(partial(grads_kernel, sizes, head0), grid_spec=pltpu.Prefe...]
  transfers between devices with their start and end apart: 22 -> 22, of which waited for: 8 -> 8; matrix products, arithmetic and copies ran while one was open for 12% -> 12% of each run, Pallas kernels for 18% -> 19%
where the time goes in v5:
time: 256 us
  waiting for transfers between devices  134 us (52%)
  Pallas kernels  48.2 us (19%)
  starting transfers between devices  39.2 us (15%)
  other arithmetic  23.1 us (9%)
  local copies, waits for them, and re-layouts  10.1 us (4%)
    ppermute x14, waiting for transfers between devices, flip(): return lax.ppermute(array, 'seq', [(i, i ^ j) for i in range(seq_count)])  69.6 us
    ppermute x5, waiting for transfers between devices, shift(): return lax.ppermute(array, 'seq', pairs)  43 us
    pallas_call x2, Pallas kernels, gradients(): pl.pallas_call(partial(grads_kernel, sizes, head0), grid_spec=pltpu.Prefe...  37.9 us
    all_to_all x3, waiting for transfers between devices, to_tokens(): lax.all_to_all(array, 'head', split_axis=0, concat_axis=1, tiled=True)  21.6 us
    ppermute x14, starting transfers between devices, flip(): return lax.ppermute(array, 'seq', [(i, i ^ j) for i in range(seq_count)])  20.3 us
    all_to_all x3, starting transfers between devices, to_tokens(): lax.all_to_all(array, 'head', split_axis=0, concat_axis=1, tiled=True)  11.3 us
    pallas_call x1, Pallas kernels, on_device(): pl.pallas_call(partial(norm_kernel, sizes), grid_spec=pltpu.PrefetchScala...  10.3 us
    ppermute x5, starting transfers between devices, shift(): return lax.ppermute(array, 'seq', pairs)  7.64 us
  transfers between devices with their start and end apart: 22, of which 8 were waited for; matrix products, arithmetic and copies ran while one was open for 12% of the time, Pallas kernels for 19%

profile of v5, /device:TPU:8, one launch (start us, length us, event | category | flops | bytes accessed | tf_op | source)
XLA Modules:
  0.0 255.8 jit_solution(4600175261861640986)
XLA Ops:
  0.7 3.2 %pad_maximum_fusion = bf16[2,512,1024]{2,1,0:T(8,128)(2,1)} fusion(bf16[1,512,1024]{2,1,0:T(8,128)(2,1)} %bitcast.76, bf16[1,512,1024]{2,1,0:T(8,128)(2,1)} %bitcast.75), kind=kLoop, calls=%fused_computation | loop fusion | flops 1048576 | bytes 4194304 | tf_op jit(solution)/shard_map/stack | solution.py:360
  4.0 1.9 collective-permute-start.2
  5.9 2.6 %collective-permute-start = (bf16[512,1024]{1,0:T(8,128)(2,1)S(1)}, bf16[512,1024]{1,0:T(8,128)(2,1)}, u32[]{:S(2)}, u32[]{:S(2)}) collective-permute-start(bf16[512,1024]{1,0:T(8,128)(2,1)S(1)} %copy-done.1), channel_id=1, source_target_pairs={{0,16},{4,20},{8,24},{12,28},{16,0},{20,4},{24,8},{28,12},{1,17},{... | collective-permute-start | bytes 3145736 | tf_op jit(solution)/shard_map/ppermute | solution.py:343
  8.4 33.4 %collective-permute-done.3.refs_4_.refs_6_ = bf16[512,1024]{1,0:T(8,128)(2,1)S(1)} collective-permute-done((bf16[512,1024]{1,0:T(8,128)(2,1)}, bf16[512,1024]{1,0:T(8,128)(2,1)S(1)}, u32[]{:S(2)}, u32[]{:S(2)}) %collective-permute-start.3) | collective-permute-done | bytes 1048608 | tf_op jit(solution)/shard_map/ppermute | solution.py:346
  41.9 2.6 %collective-permute-start.4 = (bf16[512,1024]{1,0:T(8,128)(2,1)S(1)}, bf16[512,1024]{1,0:T(8,128)(2,1)}, u32[]{:S(2)}, u32[]{:S(2)}) collective-permute-start(bf16[512,1024]{1,0:T(8,128)(2,1)S(1)} %collective-permute-done.3.refs_4_.refs_6_), channel_id=1, source_target_pairs={{0,4},{4,0},{8,12},{12,8},{16,20},{20,16},{24,28},{28,24},{1,5},{5... | collective-permute-start | bytes 3145736 | tf_op jit(solution)/shard_map/ppermute | solution.py:346
  44.5 3.4 %collective-permute-start.1 = (bf16[512,1024]{1,0:T(8,128)(2,1)}, bf16[512,1024]{1,0:T(8,128)(2,1)}, u32[]{:S(2)}, u32[]{:S(2)}) collective-permute-start(bf16[512,1024]{1,0:T(8,128)(2,1)} %refs_2_.5), channel_id=1, source_target_pairs={{0,16},{4,20},{8,24},{12,28},{16,0},{20,4},{24,8},{28,12},{1,17},{... | collective-permute-start | bytes 3145736 | tf_op jit(solution)/shard_map/ppermute | solution.py:343
  49.9 1.6 multiply_bitcast_fusion
  51.5 1.8 copy.32
  53.3 2.3 reduce_sum.27
  55.9 26.2 %collective-permute-done.5.refs_10_ = bf16[512,512]{1,0:T(8,128)(2,1)} collective-permute-done((bf16[512,512]{1,0:T(8,128)(2,1)}, bf16[512,512]{1,0:T(8,128)(2,1)}, u32[]{:S(2)}, u32[]{:S(2)}) %collective-permute-start.5) | collective-permute-done | bytes 524320 | tf_op jit(solution)/shard_map/ppermute | solution.py:346
  82.1 1.5 collective-permute-start.6
  83.7 10.3 %partial_norms.1 = f32[2,8,8,64]{3,2,1,0:T(8,128)S(1)} custom-call(s32[3]{0:T(128)S(1)} %pad_add_fusion.meta, s32[1536]{0:T(1024)S(1)} %reshape.99.table, bf16[512,1024]{1,0:T(8,128)(2,1)S(1)} %copy-done.1, bf16[512,1024]{1,0:T(8,128)(2,1)} %collective-permute-done.refs_1_, bf16[512,1024]{1,0:T(8,128)(2,1)S(1)} %copy-done, ...), custom_call_target="tpu_custom_call" | custom-call | tf_op jit(solution)/shard_map/partial_norms/pallas_call | solution.py:394
  97.0 2.5 collective-permute-start.9
  99.5 2.5 collective-permute-done.7
  102.6 19.0 %gradients.2 = (f32[512,512]{1,0:T(8,128)S(1)}, bf16[512,512]{1,0:T(8,128)(2,1)S(1)}, bf16[2,512,512]{2,1,0:T(8,128)(2,1)S(1)}, bf16[2,512,512]{2,1,0:T(8,128)(2...) custom-call(s32[3]{0:T(128)S(1)} %pad_add_fusion.meta, s32[1536]{0:T(1024)S(1)} %reshape.99.table, ...), custom_call_target="tpu_custom_call" | custom-call | tf_op jit(solution)/shard_map/gradients/pallas_call | solution.py:440
  121.6 3.4 %collective-permute-start.15 = (bf16[2,512,512]{2,1,0:T(8,128)(2,1)}, bf16[2,512,512]{2,1,0:T(8,128)(2,1)S(1)}, u32[]{:S(2)}, u32[]{:S(2)}) collective-permute-start(bf16[2,512,512]{2,1,0:T(8,128)(2,1)} %get-tuple-element.28), channel_id=1, source_target_pairs={{0,8},{4,12},{8,0},{12,4},{16,24},{20,28},{24,16},{28,20},{1,9},{5... | collective-permute-start | bytes 3145736 | tf_op jit(solution)/shard_map/ppermute | solution.py:346
  127.0 18.9 %gradients.3 = (f32[512,512]{1,0:T(8,128)S(1)}, bf16[512,512]{1,0:T(8,128)(2,1)S(1)}, bf16[2,512,512]{2,1,0:T(8,128)(2,1)S(1)}, bf16[2,512,512]{2,1,0:T(8,128)(2...) custom-call(s32[3]{0:T(128)S(1)} %pad_add_fusion.meta, s32[1536]{0:T(1024)S(1)} %reshape.99.table, ...), custom_call_target="tpu_custom_call" | custom-call | tf_op jit(solution)/shard_map/gradients/pallas_call | solution.py:440
  145.9 2.4 collective-permute-start.17
  148.3 13.2 %collective-permute-done.8 = bf16[512,512]{1,0:T(8,128)(2,1)S(1)} collective-permute-done((bf16[512,512]{1,0:T(8,128)(2,1)S(1)}, bf16[512,512]{1,0:T(8,128)(2,1)S(1)}, u32[]{:S(2)}, u32[]{:S(2)}) %collective-permute-start.8) | collective-permute-done | bytes 524320 | tf_op jit(solution)/shard_map/ppermute | solution.py:343
  165.9 2.0 collective-permute-start.12
  167.9 27.3 %collective-permute-done.10 = bf16[512,512]{1,0:T(8,128)(2,1)S(1)} collective-permute-done((bf16[512,512]{1,0:T(8,128)(2,1)S(1)}, bf16[512,512]{1,0:T(8,128)(2,1)S(1)}, u32[]{:S(2)}, u32[]{:S(2)}) %collective-permute-start.10) | collective-permute-done | bytes 524320 | tf_op jit(solution)/shard_map/ppermute | solution.py:343
  196.5 4.2 %all-to-all-start = ((bf16[4,128,1024]{2,1,0:T(8,128)(2,1)}), bf16[4,128,1024]{2,1,0:T(8,128)(2,1)}, u32[]{:S(2)}, u32[]{:S(2)}) async-start(bf16[4,128,1024]{2,1,0:T(8,128)(2,1)} %bitcast.78), calls=%async_computation | async-start | bytes 2097152 | tf_op jit(solution)/shard_map/all_to_all | solution.py:489
  203.1 1.4 fusion.1
  204.5 2.0 fusion.5
  206.5 9.9 %collective-permute-done.18 = bf16[512,512]{1,0:T(8,128)(2,1)S(1)} collective-permute-done((bf16[512,512]{1,0:T(8,128)(2,1)S(1)}, bf16[512,512]{1,0:T(8,128)(2,1)S(1)}, u32[]{:S(2)}, u32[]{:S(2)}) %collective-permute-start.18) | collective-permute-done | bytes 524320 | tf_op jit(solution)/shard_map/ppermute | solution.py:346
  218.8 3.5 %all-to-all-start.2 = ((bf16[4,128,1024]{2,1,0:T(8,128)(2,1)}), bf16[4,128,1024]{2,1,0:T(8,128)(2,1)S(1)}, u32[]{:S(2)}, u32[]{:S(2)}) async-start(bf16[4,128,1024]{2,1,0:T(8,128)(2,1)} %bitcast.80), calls=%async_computation.2 | async-start | bytes 2097152 | tf_op jit(solution)/shard_map/all_to_all | solution.py:489
  222.3 1.4 fusion.3
  223.8 1.4 fusion.2
  226.3 10.5 %all-to-all-done.2 = bf16[4,128,1024]{2,1,0:T(8,128)(2,1)S(1)} async-done(((bf16[4,128,1024]{2,1,0:T(8,128)(2,1)}), bf16[4,128,1024]{2,1,0:T(8,128)(2,1)S(1)}, u32[]{:S(2)}, u32[]{:S(2)}) %all-to-all-start.2) | async-done | bytes 1048608 | tf_op jit(solution)/shard_map/all_to_all | solution.py:489
  236.8 3.5 %all-to-all-start.1 = ((bf16[4,128,1024]{2,1,0:T(8,128)(2,1)}), bf16[4,128,1024]{2,1,0:T(8,128)(2,1)S(1)}, u32[]{:S(2)}, u32[]{:S(2)}) async-start(bf16[4,128,1024]{2,1,0:T(8,128)(2,1)} %bitcast.24), calls=%async_computation.1 | async-start | bytes 2097152 | tf_op jit(solution)/shard_map/all_to_all | solution.py:489
  240.3 2.3 copy.29
  243.6 11.1 %all-to-all-done.1 = bf16[4,128,1024]{2,1,0:T(8,128)(2,1)S(1)} async-done(((bf16[4,128,1024]{2,1,0:T(8,128)(2,1)}), bf16[4,128,1024]{2,1,0:T(8,128)(2,1)S(1)}, u32[]{:S(2)}, u32[]{:S(2)}) %all-to-all-start.1) | async-done | bytes 1048608 | tf_op jit(solution)/shard_map/all_to_all | solution.py:489
  (83 shorter events, 21.6 us)
Async XLA Ops:
  0.6 41.2 %collective-permute-start.3 = (bf16[512,1024]{1,0:T(8,128)(2,1)}, bf16[512,1024]{1,0:T(8,128)(2,1)S(1)}, u32[]{:S(2)}, u32[]{:S(2)}) collective-permute-start(bf16[512,1024]{1,0:T(8,128)(2,1)} %refs_4_.3), channel_id=1, source_target_pairs={{0,8},{4,12},{8,0},{12,4},{16,24},{20,28},{24,16},{28,20},{1,9},{5... | collective-permute-start | bytes 3145736 | tf_op jit(solution)/shard_map/ppermute | solution.py:346
  0.7 5.1 %copy-start.1 = (bf16[512,1024]{1,0:T(8,128)(2,1)S(1)}, bf16[512,1024]{1,0:T(8,128)(2,1)}, u32[]{:S(2)}) copy-start(bf16[512,1024]{1,0:T(8,128)(2,1)} %refs_0_.5) | copy-start | bytes 3145732
  0.7 47.1 %copy-start.10 = (s32[64,8,3]{0,1,2:T(8,128)S(1)}, s32[64,8,3]{0,1,2:T(8,128)}, u32[]{:S(2)}) copy-start(s32[64,8,3]{0,1,2:T(8,128)} %param.12) | copy-start | bytes 18436
  0.7 47.5 %copy-start.5 = (bf16[512,1024]{1,0:T(8,128)(2,1)S(1)}, bf16[512,1024]{1,0:T(8,128)(2,1)}, u32[]{:S(2)}) copy-start(bf16[512,1024]{1,0:T(8,128)(2,1)} %refs_8_.3) | copy-start | bytes 3145732
  4.0 79.7 %collective-permute-start.2 = (bf16[2,512,1024]{2,1,0:T(8,128)(2,1)}, bf16[2,512,1024]{2,1,0:T(8,128)(2,1)}, u32[]{:S(2)}, u32[]{:S(2)}) collective-permute-start(bf16[2,512,1024]{2,1,0:T(8,128)(2,1)} %pad_maximum_fusion), channel_id=1, source_target_pairs={{0,4},{4,0},{8,12},{12,8},{16,20},{20,16},{24,28},{28,24},{1,5},{5... | collective-permute-start | bytes 6291464 | tf_op jit(solution)/shard_map/ppermute | solution.py:346
  5.9 77.8 %collective-permute-start = (bf16[512,1024]{1,0:T(8,128)(2,1)S(1)}, bf16[512,1024]{1,0:T(8,128)(2,1)}, u32[]{:S(2)}, u32[]{:S(2)}) collective-permute-start(bf16[512,1024]{1,0:T(8,128)(2,1)S(1)} %copy-done.1), channel_id=1, source_target_pairs={{0,16},{4,20},{8,24},{12,28},{16,0},{20,4},{24,8},{28,12},{1,17},{... | collective-permute-start | bytes 3145736 | tf_op jit(solution)/shard_map/ppermute | solution.py:343
  41.8 41.8 %copy-start.2 = (bf16[512,1024]{1,0:T(8,128)(2,1)}, bf16[512,1024]{1,0:T(8,128)(2,1)S(1)}, u32[]{:S(2)}) copy-start(bf16[512,1024]{1,0:T(8,128)(2,1)S(1)} %collective-permute-done.3.refs_4_.refs_6_) | copy-start | bytes 3145732
  41.9 41.8 %collective-permute-start.4 = (bf16[512,1024]{1,0:T(8,128)(2,1)S(1)}, bf16[512,1024]{1,0:T(8,128)(2,1)}, u32[]{:S(2)}, u32[]{:S(2)}) collective-permute-start(bf16[512,1024]{1,0:T(8,128)(2,1)S(1)} %collective-permute-done.3.refs_4_.refs_6_), channel_id=1, source_target_pairs={{0,4},{4,0},{8,12},{12,8},{16,20},{20,16},{24,28},{28,24},{1,5},{5... | collective-permute-start | bytes 3145736 | tf_op jit(solution)/shard_map/ppermute | solution.py:346
  44.5 58.1 %collective-permute-start.1 = (bf16[512,1024]{1,0:T(8,128)(2,1)}, bf16[512,1024]{1,0:T(8,128)(2,1)}, u32[]{:S(2)}, u32[]{:S(2)}) collective-permute-start(bf16[512,1024]{1,0:T(8,128)(2,1)} %refs_2_.5), channel_id=1, source_target_pairs={{0,16},{4,20},{8,24},{12,28},{16,0},{20,4},{24,8},{28,12},{1,17},{... | collective-permute-start | bytes 3145736 | tf_op jit(solution)/shard_map/ppermute | solution.py:343
  49.3 32.8 %collective-permute-start.5 = (bf16[512,512]{1,0:T(8,128)(2,1)}, bf16[512,512]{1,0:T(8,128)(2,1)}, u32[]{:S(2)}, u32[]{:S(2)}) collective-permute-start(bf16[512,512]{1,0:T(8,128)(2,1)} %get-tuple-element.17), channel_id=1, source_target_pairs={{0,8},{4,12},{8,0},{12,4},{16,24},{20,28},{24,16},{28,20},{1,9},{5... | collective-permute-start | bytes 1572872 | tf_op jit(solution)/shard_map/ppermute | solution.py:346
  53.3 2.5 copy-start.11
  53.3 30.3 %copy-start = (bf16[512,1024]{1,0:T(8,128)(2,1)S(1)}, bf16[512,1024]{1,0:T(8,128)(2,1)}, u32[]{:S(2)}) copy-start(bf16[512,1024]{1,0:T(8,128)(2,1)} %refs_4_.3) | copy-start | bytes 3145732
  82.1 20.5 %collective-permute-start.6 = (bf16[512,512]{1,0:T(8,128)(2,1)}, bf16[512,512]{1,0:T(8,128)(2,1)}, u32[]{:S(2)}, u32[]{:S(2)}) collective-permute-start(bf16[512,512]{1,0:T(8,128)(2,1)} %collective-permute-done.5.refs_10_), channel_id=1, source_target_pairs={{0,4},{4,0},{8,12},{12,8},{16,20},{20,16},{24,28},{28,24},{1,5},{5... | collective-permute-start | bytes 1572872 | tf_op jit(solution)/shard_map/ppermute | solution.py:346
  94.0 8.0 %collective-permute-start.7 = (f32[3,8,8,64]{3,2,1,0:T(8,128)S(1)}, f32[3,8,8,64]{3,2,1,0:T(8,128)S(1)}, u32[]{:S(2)}, u32[]{:S(2)}) collective-permute-start(f32[3,8,8,64]{3,2,1,0:T(8,128)S(1)} %pad_maximum_fusion.5), channel_id=1, source_target_pairs={{0,16},{4,20},{8,24},{12,28},{16,0},{20,4},{24,8},{28,12},{1,17},{... | collective-permute-start | bytes 147464 | tf_op jit(solution)/shard_map/ppermute | solution.py:343
  97.0 30.0 %collective-permute-start.9 = (bf16[2,512,512]{2,1,0:T(8,128)(2,1)}, bf16[2,512,512]{2,1,0:T(8,128)(2,1)}, u32[]{:S(2)}, u32[]{:S(2)}) collective-permute-start(bf16[2,512,512]{2,1,0:T(8,128)(2,1)} %pad_maximum_fusion.1), channel_id=1, source_target_pairs={{0,8},{4,12},{8,0},{12,4},{16,24},{20,28},{24,16},{28,20},{1,9},{5... | collective-permute-start | bytes 3145736 | tf_op jit(solution)/shard_map/ppermute | solution.py:346
  121.6 41.0 %collective-permute-start.15 = (bf16[2,512,512]{2,1,0:T(8,128)(2,1)}, bf16[2,512,512]{2,1,0:T(8,128)(2,1)S(1)}, u32[]{:S(2)}, u32[]{:S(2)}) collective-permute-start(bf16[2,512,512]{2,1,0:T(8,128)(2,1)} %get-tuple-element.28), channel_id=1, source_target_pairs={{0,8},{4,12},{8,0},{12,4},{16,24},{20,28},{24,16},{28,20},{1,9},{5... | collective-permute-start | bytes 3145736 | tf_op jit(solution)/shard_map/ppermute | solution.py:346
  125.0 36.5 %collective-permute-start.8 = (bf16[512,512]{1,0:T(8,128)(2,1)S(1)}, bf16[512,512]{1,0:T(8,128)(2,1)S(1)}, u32[]{:S(2)}, u32[]{:S(2)}) collective-permute-start(bf16[512,512]{1,0:T(8,128)(2,1)S(1)} %get-tuple-element.19), channel_id=1, source_target_pairs={{0,16},{4,20},{8,24},{12,28},{16,0},{20,4},{24,8},{28,12},{1,17},{... | collective-permute-start | bytes 1572872 | tf_op jit(solution)/shard_map/ppermute | solution.py:343
  126.0 38.8 %collective-permute-start.11 = (bf16[2,512,512]{2,1,0:T(8,128)(2,1)S(1)}, bf16[2,512,512]{2,1,0:T(8,128)(2,1)S(1)}, u32[]{:S(2)}, u32[]{:S(2)}) collective-permute-start(bf16[2,512,512]{2,1,0:T(8,128)(2,1)S(1)} %get-tuple-element.24), channel_id=1, source_target_pairs={{0,4},{4,0},{8,12},{12,8},{16,20},{20,16},{24,28},{28,24},{1,5},{5... | collective-permute-start | bytes 3145736 | tf_op jit(solution)/shard_map/ppermute | solution.py:346
  145.9 20.0 %copy-start.3 = (bf16[2,512,512]{2,1,0:T(8,128)(2,1)}, bf16[2,512,512]{2,1,0:T(8,128)(2,1)S(1)}, u32[]{:S(2)}) copy-start(bf16[2,512,512]{2,1,0:T(8,128)(2,1)S(1)} %get-tuple-element.29) | copy-start | bytes 3145732
  145.9 54.9 %collective-permute-start.17 = (bf16[2,512,512]{2,1,0:T(8,128)(2,1)}, bf16[2,512,512]{2,1,0:T(8,128)(2,1)}, u32[]{:S(2)}, u32[]{:S(2)}) collective-permute-start(bf16[2,512,512]{2,1,0:T(8,128)(2,1)} %get-tuple-element.30), channel_id=1, source_target_pairs={{0,8},{4,12},{8,0},{12,4},{16,24},{20,28},{24,16},{28,20},{1,9},{5... | collective-permute-start | bytes 3145736 | tf_op jit(solution)/shard_map/ppermute | solution.py:346
  161.6 42.9 %collective-permute-start.13 = (bf16[2,512,512]{2,1,0:T(8,128)(2,1)}, bf16[2,512,512]{2,1,0:T(8,128)(2,1)}, u32[]{:S(2)}, u32[]{:S(2)}) collective-permute-start(bf16[2,512,512]{2,1,0:T(8,128)(2,1)} %get-tuple-element.26), channel_id=1, source_target_pairs={{0,4},{4,0},{8,12},{12,8},{16,20},{20,16},{24,28},{28,24},{1,5},{5... | collective-permute-start | bytes 3145736 | tf_op jit(solution)/shard_map/ppermute | solution.py:346
  162.7 32.5 %collective-permute-start.10 = (bf16[512,512]{1,0:T(8,128)(2,1)S(1)}, bf16[512,512]{1,0:T(8,128)(2,1)S(1)}, u32[]{:S(2)}, u32[]{:S(2)}) collective-permute-start(bf16[512,512]{1,0:T(8,128)(2,1)S(1)} %get-tuple-element.22), channel_id=1, source_target_pairs={{0,16},{4,20},{8,24},{12,28},{16,0},{20,4},{24,8},{28,12},{1,17},{... | collective-permute-start | bytes 1572872 | tf_op jit(solution)/shard_map/ppermute | solution.py:343
  162.7 32.7 %copy-start.8 = (bf16[2,512,512]{2,1,0:T(8,128)(2,1)}, bf16[2,512,512]{2,1,0:T(8,128)(2,1)S(1)}, u32[]{:S(2)}) copy-start(bf16[2,512,512]{2,1,0:T(8,128)(2,1)S(1)} %collective-permute-done.15) | copy-start | bytes 3145732
  163.8 39.3 %collective-permute-start.16 = (bf16[512,512]{1,0:T(8,128)(2,1)}, bf16[512,512]{1,0:T(8,128)(2,1)}, u32[]{:S(2)}, u32[]{:S(2)}) collective-permute-start(bf16[512,512]{1,0:T(8,128)(2,1)} %fusion.6), channel_id=1, source_target_pairs={{0,4},{4,0},{8,12},{12,8},{16,20},{20,16},{24,28},{28,24},{1,5},{5... | collective-permute-start | bytes 1572872 | tf_op jit(solution)/shard_map/ppermute | solution.py:346
  164.9 31.6 %copy-start.7 = (bf16[2,512,512]{2,1,0:T(8,128)(2,1)}, bf16[2,512,512]{2,1,0:T(8,128)(2,1)S(1)}, u32[]{:S(2)}) copy-start(bf16[2,512,512]{2,1,0:T(8,128)(2,1)S(1)} %collective-permute-done.11) | copy-start | bytes 3145732
  165.9 56.4 %collective-permute-start.12 = (bf16[512,512]{1,0:T(8,128)(2,1)}, bf16[512,512]{1,0:T(8,128)(2,1)}, u32[]{:S(2)}, u32[]{:S(2)}) collective-permute-start(bf16[512,512]{1,0:T(8,128)(2,1)} %fusion.4), channel_id=1, source_target_pairs={{0,8},{4,12},{8,0},{12,4},{16,24},{20,28},{24,16},{28,20},{1,9},{5... | collective-permute-start | bytes 1572872 | tf_op jit(solution)/shard_map/ppermute | solution.py:346
  196.5 22.3 %all-to-all-start = ((bf16[4,128,1024]{2,1,0:T(8,128)(2,1)}), bf16[4,128,1024]{2,1,0:T(8,128)(2,1)}, u32[]{:S(2)}, u32[]{:S(2)}) async-start(bf16[4,128,1024]{2,1,0:T(8,128)(2,1)} %bitcast.78), calls=%async_computation | async-start | bytes 2097152 | tf_op jit(solution)/shard_map/all_to_all | solution.py:489
  202.1 14.4 %copy-start.4 = (bf16[2,512,512]{2,1,0:T(8,128)(2,1)S(1)}, bf16[2,512,512]{2,1,0:T(8,128)(2,1)}, u32[]{:S(2)}) copy-start(bf16[2,512,512]{2,1,0:T(8,128)(2,1)} %copy-done.3) | copy-start | bytes 3145732
  202.1 14.3 %collective-permute-start.18 = (bf16[512,512]{1,0:T(8,128)(2,1)S(1)}, bf16[512,512]{1,0:T(8,128)(2,1)S(1)}, u32[]{:S(2)}, u32[]{:S(2)}) collective-permute-start(bf16[512,512]{1,0:T(8,128)(2,1)S(1)} %fusion.7), channel_id=1, source_target_pairs={{0,4},{4,0},{8,12},{12,8},{16,20},{20,16},{24,28},{28,24},{1,5},{5... | collective-permute-start | bytes 1572872 | tf_op jit(solution)/shard_map/ppermute | solution.py:346
  206.5 17.2 %collective-permute-start.14 = (bf16[512,512]{1,0:T(8,128)(2,1)}, bf16[512,512]{1,0:T(8,128)(2,1)}, u32[]{:S(2)}, u32[]{:S(2)}) collective-permute-start(bf16[512,512]{1,0:T(8,128)(2,1)} %fusion.5), channel_id=1, source_target_pairs={{0,8},{4,12},{8,0},{12,4},{16,24},{20,28},{24,16},{28,20},{1,9},{5... | collective-permute-start | bytes 1572872 | tf_op jit(solution)/shard_map/ppermute | solution.py:346
  218.8 18.0 %all-to-all-start.2 = ((bf16[4,128,1024]{2,1,0:T(8,128)(2,1)}), bf16[4,128,1024]{2,1,0:T(8,128)(2,1)S(1)}, u32[]{:S(2)}, u32[]{:S(2)}) async-start(bf16[4,128,1024]{2,1,0:T(8,128)(2,1)} %bitcast.80), calls=%async_computation.2 | async-start | bytes 2097152 | tf_op jit(solution)/shard_map/all_to_all | solution.py:489
  236.8 18.0 %all-to-all-start.1 = ((bf16[4,128,1024]{2,1,0:T(8,128)(2,1)}), bf16[4,128,1024]{2,1,0:T(8,128)(2,1)S(1)}, u32[]{:S(2)}, u32[]{:S(2)}) async-start(bf16[4,128,1024]{2,1,0:T(8,128)(2,1)} %bitcast.24), calls=%async_computation.1 | async-start | bytes 2097152 | tf_op jit(solution)/shard_map/all_to_all | solution.py:489
  (2 other events, 3.6 us)

commit v6 on v5

--- a/solution.py
+++ b/solution.py
@@ -498,9 +498,24 @@
         dq_parts.append(dq.astype(jnp.bfloat16))
         dk_parts.append(reduced(dk_keep, dk_send, 1, 2))
         dv_parts.append(reduced(dv_keep, dv_send, 2, 1))
-    dq, dk, dv = (
-        to_tokens(jnp.concatenate(parts, axis=1)) for parts in (dq_parts, dk_parts, dv_parts)
-    )
+    def to_tokens_by_steps(array):
+        groups = lax.axis_size("head")
+        here = lax.axis_index("head")
+        rows = array.reshape(groups, tokens // groups, -1)
+
+        def row(stack, index):
+            return lax.dynamic_index_in_dim(stack, lax.rem(index, groups), 0, keepdims=False)
+
+        got = [row(rows, here)]
+        for m in range(1, groups):
+            pairs = [(i, (i + m) % groups) for i in range(groups)]
+            got.append(lax.ppermute(row(rows, here + m), "head", pairs))
+        got = jnp.stack(got)
+        return jnp.concatenate([row(got, here + groups - j) for j in range(groups)], axis=1)
+
+    dq = to_tokens_by_steps(jnp.concatenate(dq_parts, axis=1))
+    dk = to_tokens(jnp.concatenate(dk_parts, axis=1))
+    dv = to_tokens(jnp.concatenate(dv_parts, axis=1))
     return dq, dk, dv
 
 

time: 256 us -> 252 us (0.984)
  waiting for transfers between devices: 134 us -> 130 us
    all_to_all x3 -> x2, waiting for transfers between devices: 21.6 us -> 15.1 us  [to_tokens(): lax.all_to_all(array, 'head', split_axis=0, concat_axis=1, tiled=True)]
    ppermute x0 -> x3, waiting for transfers between devices: none -> 5.31 us  [to_tokens_by_steps(): got.append(lax.ppermute(row(rows, here + m), 'head', pairs))]
    ppermute x14, waiting for transfers between devices: 69.6 us -> 65.9 us  [flip(): return lax.ppermute(array, 'seq', [(i, i ^ j) for i in range(seq_count)])]
    all_to_all x3 -> x2, starting transfers between devices: 11.3 us -> 7.76 us  [to_tokens(): lax.all_to_all(array, 'head', split_axis=0, concat_axis=1, tiled=True)]
    ppermute x0 -> x3, starting transfers between devices: none -> 3.41 us  [to_tokens_by_steps(): got.append(lax.ppermute(row(rows, here + m), 'head', pairs))]
  transfers between devices with their start and end apart: 22 -> 24, of which waited for: 8 -> 11; matrix products, arithmetic and copies ran while one was open for 12% -> 13% of each run, Pallas kernels for 19% -> 19%
where the time goes in v6:
time: 252 us; the launch traced here: 250 us
  waiting for transfers between devices  130 us (52%)
  Pallas kernels  47.3 us (19%)
  starting transfers between devices  37.8 us (15%)
  other arithmetic  23 us (9%)
  local copies, waits for them, and re-layouts  11.1 us (4%)
    ppermute x14, waiting for transfers between devices, flip(): return lax.ppermute(array, 'seq', [(i, i ^ j) for i in range(seq_count)])  65.9 us
    ppermute x5, waiting for transfers between devices, shift(): return lax.ppermute(array, 'seq', pairs)  43.4 us
    pallas_call x2, Pallas kernels, gradients(): pl.pallas_call(partial(grads_kernel, sizes, head0), grid_spec=pltpu.Prefe...  36.8 us
    ppermute x14, starting transfers between devices, flip(): return lax.ppermute(array, 'seq', [(i, i ^ j) for i in range(seq_count)])  18.2 us
    all_to_all x2, waiting for transfers between devices, to_tokens(): lax.all_to_all(array, 'head', split_axis=0, concat_axis=1, tiled=True)  15.1 us
    pallas_call x1, Pallas kernels, on_device(): pl.pallas_call(partial(norm_kernel, sizes), grid_spec=pltpu.PrefetchScala...  10.5 us
    ppermute x5, starting transfers between devices, shift(): return lax.ppermute(array, 'seq', pairs)  8.48 us
    all_to_all x2, starting transfers between devices, to_tokens(): lax.all_to_all(array, 'head', split_axis=0, concat_axis=1, tiled=True)  7.76 us
  transfers between devices with their start and end apart: 24, of which 11 were waited for; matrix products, arithmetic and copies ran while one was open for 13% of the time, Pallas kernels for 19%

profile of v6, /device:TPU:8, one launch (start us, length us, event | category | flops | bytes accessed | tf_op | source)
XLA Modules:
  0.0 250.1 jit_solution(9523908176143327730)
XLA Ops:
  0.7 3.2 %pad_maximum_fusion = bf16[2,512,1024]{2,1,0:T(8,128)(2,1)} fusion(bf16[1,512,1024]{2,1,0:T(8,128)(2,1)} %bitcast.90, bf16[1,512,1024]{2,1,0:T(8,128)(2,1)} %bitcast.89), kind=kLoop, calls=%fused_computation | loop fusion | flops 1048576 | bytes 4194304 | tf_op jit(solution)/shard_map/stack | solution.py:360
  3.9 1.9 collective-permute-start.2
  5.9 2.6 %collective-permute-start = (bf16[512,1024]{1,0:T(8,128)(2,1)S(1)}, bf16[512,1024]{1,0:T(8,128)(2,1)}, u32[]{:S(2)}, u32[]{:S(2)}) collective-permute-start(bf16[512,1024]{1,0:T(8,128)(2,1)S(1)} %copy-done.1), channel_id=1, source_target_pairs={{0,16},{4,20},{8,24},{12,28},{16,0},{20,4},{24,8},{28,12},{1,17},{... | collective-permute-start | bytes 3145736 | tf_op jit(solution)/shard_map/ppermute | solution.py:343
  8.4 33.4 %collective-permute-done.3.refs_4_.refs_6_ = bf16[512,1024]{1,0:T(8,128)(2,1)S(1)} collective-permute-done((bf16[512,1024]{1,0:T(8,128)(2,1)}, bf16[512,1024]{1,0:T(8,128)(2,1)S(1)}, u32[]{:S(2)}, u32[]{:S(2)}) %collective-permute-start.3) | collective-permute-done | bytes 1048608 | tf_op jit(solution)/shard_map/ppermute | solution.py:346
  41.9 2.6 %collective-permute-start.4 = (bf16[512,1024]{1,0:T(8,128)(2,1)S(1)}, bf16[512,1024]{1,0:T(8,128)(2,1)}, u32[]{:S(2)}, u32[]{:S(2)}) collective-permute-start(bf16[512,1024]{1,0:T(8,128)(2,1)S(1)} %collective-permute-done.3.refs_4_.refs_6_), channel_id=1, source_target_pairs={{0,4},{4,0},{8,12},{12,8},{16,20},{20,16},{24,28},{28,24},{1,5},{5... | collective-permute-start | bytes 3145736 | tf_op jit(solution)/shard_map/ppermute | solution.py:346
  44.5 3.4 %collective-permute-start.1 = (bf16[512,1024]{1,0:T(8,128)(2,1)}, bf16[512,1024]{1,0:T(8,128)(2,1)}, u32[]{:S(2)}, u32[]{:S(2)}) collective-permute-start(bf16[512,1024]{1,0:T(8,128)(2,1)} %refs_2_.5), channel_id=1, source_target_pairs={{0,16},{4,20},{8,24},{12,28},{16,0},{20,4},{24,8},{28,12},{1,17},{... | collective-permute-start | bytes 3145736 | tf_op jit(solution)/shard_map/ppermute | solution.py:343
  49.9 1.6 multiply_bitcast_fusion
  51.5 1.9 copy.28
  53.3 2.3 reduce_sum.27
  55.9 26.2 %collective-permute-done.5.refs_10_ = bf16[512,512]{1,0:T(8,128)(2,1)} collective-permute-done((bf16[512,512]{1,0:T(8,128)(2,1)}, bf16[512,512]{1,0:T(8,128)(2,1)}, u32[]{:S(2)}, u32[]{:S(2)}) %collective-permute-start.5) | collective-permute-done | bytes 524320 | tf_op jit(solution)/shard_map/ppermute | solution.py:346
  82.1 1.5 collective-permute-start.6
  83.7 10.5 %partial_norms.1 = f32[2,8,8,64]{3,2,1,0:T(8,128)S(1)} custom-call(s32[3]{0:T(128)S(1)} %pad_add_fusion.meta, s32[1536]{0:T(1024)S(1)} %reshape.99.table, bf16[512,1024]{1,0:T(8,128)(2,1)S(1)} %copy-done.1, bf16[512,1024]{1,0:T(8,128)(2,1)} %collective-permute-done.refs_1_, bf16[512,1024]{1,0:T(8,128)(2,1)S(1)} %copy-done, ...), custom_call_target="tpu_custom_call" | custom-call | tf_op jit(solution)/shard_map/partial_norms/pallas_call | solution.py:394
  96.3 2.5 %collective-permute-start.9 = (bf16[2,512,512]{2,1,0:T(8,128)(2,1)S(1)}, bf16[2,512,512]{2,1,0:T(8,128)(2,1)}, u32[]{:S(2)}, u32[]{:S(2)}) collective-permute-start(bf16[2,512,512]{2,1,0:T(8,128)(2,1)S(1)} %pad_maximum_fusion.1), channel_id=1, source_target_pairs={{0,8},{4,12},{8,0},{12,4},{16,24},{20,28},{24,16},{28,20},{1,9},{5... | collective-permute-start | bytes 3145736 | tf_op jit(solution)/shard_map/ppermute | solution.py:346
  98.8 3.3 %collective-permute-done.7 = f32[3,8,8,64]{3,2,1,0:T(8,128)S(1)} collective-permute-done((f32[3,8,8,64]{3,2,1,0:T(8,128)S(1)}, f32[3,8,8,64]{3,2,1,0:T(8,128)S(1)}, u32[]{:S(2)}, u32[]{:S(2)}) %collective-permute-start.7) | collective-permute-done | bytes 49184 | tf_op jit(solution)/shard_map/ppermute | solution.py:343
  102.7 18.3 %gradients.2 = (f32[512,512]{1,0:T(8,128)S(1)}, bf16[512,512]{1,0:T(8,128)(2,1)}, bf16[2,512,512]{2,1,0:T(8,128)(2,1)S(1)}, bf16[2,512,512]{2,1,0:T(8,128)(2,1)}...) custom-call(s32[3]{0:T(128)S(1)} %pad_add_fusion.meta, s32[1536]{0:T(1024)S(1)} %reshape.99.table, ...), custom_call_target="tpu_custom_call" | custom-call | tf_op jit(solution)/shard_map/gradients/pallas_call | solution.py:440
  122.0 2.8 %collective-permute-start.18 = (bf16[2,512,512]{2,1,0:T(8,128)(2,1)}, bf16[2,512,512]{2,1,0:T(8,128)(2,1)}, u32[]{:S(2)}, u32[]{:S(2)}) collective-permute-start(bf16[2,512,512]{2,1,0:T(8,128)(2,1)} %get-tuple-element.28), channel_id=1, source_target_pairs={{0,8},{4,12},{8,0},{12,4},{16,24},{20,28},{24,16},{28,20},{1,9},{5... | collective-permute-start | bytes 3145736 | tf_op jit(solution)/shard_map/ppermute | solution.py:346
  124.8 1.9 collective-permute-start.8
  127.2 18.5 %gradients.3 = (f32[512,512]{1,0:T(8,128)S(1)}, bf16[512,512]{1,0:T(8,128)(2,1)S(1)}, bf16[2,512,512]{2,1,0:T(8,128)(2,1)S(1)}, bf16[2,512,512]{2,1,0:T(8,128)(2...) custom-call(s32[3]{0:T(128)S(1)} %pad_add_fusion.meta, s32[1536]{0:T(1024)S(1)} %reshape.99.table, ...), custom_call_target="tpu_custom_call" | custom-call | tf_op jit(solution)/shard_map/gradients/pallas_call | solution.py:440
  145.7 2.5 collective-permute-start.20
  148.2 14.1 %collective-permute-done.8 = bf16[512,512]{1,0:T(8,128)(2,1)} collective-permute-done((bf16[512,512]{1,0:T(8,128)(2,1)}, bf16[512,512]{1,0:T(8,128)(2,1)}, u32[]{:S(2)}, u32[]{:S(2)}) %collective-permute-start.8) | collective-permute-done | bytes 524320 | tf_op jit(solution)/shard_map/ppermute | solution.py:343
  165.3 1.6 collective-permute-start.19
  166.8 2.0 fusion.4
  169.9 26.0 %collective-permute-done.10 = bf16[512,512]{1,0:T(8,128)(2,1)S(1)} collective-permute-done((bf16[512,512]{1,0:T(8,128)(2,1)S(1)}, bf16[512,512]{1,0:T(8,128)(2,1)S(1)}, u32[]{:S(2)}, u32[]{:S(2)}) %collective-permute-start.10) | collective-permute-done | bytes 524320 | tf_op jit(solution)/shard_map/ppermute | solution.py:343
  200.2 6.3 %collective-permute-done.21 = bf16[512,512]{1,0:T(8,128)(2,1)S(1)} collective-permute-done((bf16[512,512]{1,0:T(8,128)(2,1)S(1)}, bf16[512,512]{1,0:T(8,128)(2,1)S(1)}, u32[]{:S(2)}, u32[]{:S(2)}) %collective-permute-start.21) | collective-permute-done | bytes 524320 | tf_op jit(solution)/shard_map/ppermute | solution.py:346
  207.9 4.2 %all-to-all-start.1 = ((bf16[4,128,1024]{2,1,0:T(8,128)(2,1)}), bf16[4,128,1024]{2,1,0:T(8,128)(2,1)}, u32[]{:S(2)}, u32[]{:S(2)}) async-start(bf16[4,128,1024]{2,1,0:T(8,128)(2,1)} %bitcast.94), calls=%async_computation.1 | async-start | bytes 2097152 | tf_op jit(solution)/shard_map/all_to_all | solution.py:489
  213.6 1.7 collective-permute-start.12
  216.6 1.4 fusion.3
  220.4 6.7 %all-to-all-done.1 = bf16[4,128,1024]{2,1,0:T(8,128)(2,1)} async-done(((bf16[4,128,1024]{2,1,0:T(8,128)(2,1)}), bf16[4,128,1024]{2,1,0:T(8,128)(2,1)}, u32[]{:S(2)}, u32[]{:S(2)}) %all-to-all-start.1) | async-done | bytes 1048608 | tf_op jit(solution)/shard_map/all_to_all | solution.py:489
  227.2 3.5 %all-to-all-start = ((bf16[4,128,1024]{2,1,0:T(8,128)(2,1)}), bf16[4,128,1024]{2,1,0:T(8,128)(2,1)S(1)}, u32[]{:S(2)}, u32[]{:S(2)}) async-start(bf16[4,128,1024]{2,1,0:T(8,128)(2,1)} %bitcast.33), calls=%async_computation | async-start | bytes 2097152 | tf_op jit(solution)/shard_map/all_to_all | solution.py:489
  232.8 3.2 %collective-permute-done.13 = bf16[128,1024]{1,0:T(8,128)(2,1)} collective-permute-done((bf16[128,1024]{1,0:T(8,128)(2,1)}, bf16[128,1024]{1,0:T(8,128)(2,1)}, u32[]{:S(2)}, u32[]{:S(2)}) %collective-permute-start.13) | collective-permute-done | bytes 262176 | tf_op jit(solution)/shard_map/ppermute | solution.py:512
  238.4 2.3 copy.27
  240.7 8.4 %all-to-all-done = bf16[4,128,1024]{2,1,0:T(8,128)(2,1)S(1)} async-done(((bf16[4,128,1024]{2,1,0:T(8,128)(2,1)}), bf16[4,128,1024]{2,1,0:T(8,128)(2,1)S(1)}, u32[]{:S(2)}, u32[]{:S(2)}) %all-to-all-start) | async-done | bytes 1048608 | tf_op jit(solution)/shard_map/all_to_all | solution.py:489
  (94 shorter events, 26.8 us)
Async XLA Ops:
  0.6 41.2 %collective-permute-start.3 = (bf16[512,1024]{1,0:T(8,128)(2,1)}, bf16[512,1024]{1,0:T(8,128)(2,1)S(1)}, u32[]{:S(2)}, u32[]{:S(2)}) collective-permute-start(bf16[512,1024]{1,0:T(8,128)(2,1)} %refs_4_.3), channel_id=1, source_target_pairs={{0,8},{4,12},{8,0},{12,4},{16,24},{20,28},{24,16},{28,20},{1,9},{5... | collective-permute-start | bytes 3145736 | tf_op jit(solution)/shard_map/ppermute | solution.py:346
  0.7 47.1 %copy-start.12 = (s32[64,8,3]{0,1,2:T(8,128)S(1)}, s32[64,8,3]{0,1,2:T(8,128)}, u32[]{:S(2)}) copy-start(s32[64,8,3]{0,1,2:T(8,128)} %param.12) | copy-start | bytes 18436
  0.7 47.5 %copy-start.5 = (bf16[512,1024]{1,0:T(8,128)(2,1)S(1)}, bf16[512,1024]{1,0:T(8,128)(2,1)}, u32[]{:S(2)}) copy-start(bf16[512,1024]{1,0:T(8,128)(2,1)} %refs_8_.3) | copy-start | bytes 3145732
  3.9 79.7 %collective-permute-start.2 = (bf16[2,512,1024]{2,1,0:T(8,128)(2,1)}, bf16[2,512,1024]{2,1,0:T(8,128)(2,1)}, u32[]{:S(2)}, u32[]{:S(2)}) collective-permute-start(bf16[2,512,1024]{2,1,0:T(8,128)(2,1)} %pad_maximum_fusion), channel_id=1, source_target_pairs={{0,4},{4,0},{8,12},{12,8},{16,20},{20,16},{24,28},{28,24},{1,5},{5... | collective-permute-start | bytes 6291464 | tf_op jit(solution)/shard_map/ppermute | solution.py:346
  5.9 77.8 %collective-permute-start = (bf16[512,1024]{1,0:T(8,128)(2,1)S(1)}, bf16[512,1024]{1,0:T(8,128)(2,1)}, u32[]{:S(2)}, u32[]{:S(2)}) collective-permute-start(bf16[512,1024]{1,0:T(8,128)(2,1)S(1)} %copy-done.1), channel_id=1, source_target_pairs={{0,16},{4,20},{8,24},{12,28},{16,0},{20,4},{24,8},{28,12},{1,17},{... | collective-permute-start | bytes 3145736 | tf_op jit(solution)/shard_map/ppermute | solution.py:343
  41.9 41.8 %copy-start.2 = (bf16[512,1024]{1,0:T(8,128)(2,1)}, bf16[512,1024]{1,0:T(8,128)(2,1)S(1)}, u32[]{:S(2)}) copy-start(bf16[512,1024]{1,0:T(8,128)(2,1)S(1)} %collective-permute-done.3.refs_4_.refs_6_) | copy-start | bytes 3145732
  41.9 41.8 %collective-permute-start.4 = (bf16[512,1024]{1,0:T(8,128)(2,1)S(1)}, bf16[512,1024]{1,0:T(8,128)(2,1)}, u32[]{:S(2)}, u32[]{:S(2)}) collective-permute-start(bf16[512,1024]{1,0:T(8,128)(2,1)S(1)} %collective-permute-done.3.refs_4_.refs_6_), channel_id=1, source_target_pairs={{0,4},{4,0},{8,12},{12,8},{16,20},{20,16},{24,28},{28,24},{1,5},{5... | collective-permute-start | bytes 3145736 | tf_op jit(solution)/shard_map/ppermute | solution.py:346
  44.5 58.2 %collective-permute-start.1 = (bf16[512,1024]{1,0:T(8,128)(2,1)}, bf16[512,1024]{1,0:T(8,128)(2,1)}, u32[]{:S(2)}, u32[]{:S(2)}) collective-permute-start(bf16[512,1024]{1,0:T(8,128)(2,1)} %refs_2_.5), channel_id=1, source_target_pairs={{0,16},{4,20},{8,24},{12,28},{16,0},{20,4},{24,8},{28,12},{1,17},{... | collective-permute-start | bytes 3145736 | tf_op jit(solution)/shard_map/ppermute | solution.py:343
  49.3 32.8 %collective-permute-start.5 = (bf16[512,512]{1,0:T(8,128)(2,1)}, bf16[512,512]{1,0:T(8,128)(2,1)}, u32[]{:S(2)}, u32[]{:S(2)}) collective-permute-start(bf16[512,512]{1,0:T(8,128)(2,1)} %get-tuple-element.17), channel_id=1, source_target_pairs={{0,8},{4,12},{8,0},{12,4},{16,24},{20,28},{24,16},{28,20},{1,9},{5... | collective-permute-start | bytes 1572872 | tf_op jit(solution)/shard_map/ppermute | solution.py:346
  53.3 30.3 %copy-start = (bf16[512,1024]{1,0:T(8,128)(2,1)S(1)}, bf16[512,1024]{1,0:T(8,128)(2,1)}, u32[]{:S(2)}) copy-start(bf16[512,1024]{1,0:T(8,128)(2,1)} %refs_4_.3) | copy-start | bytes 3145732
  82.1 20.5 %collective-permute-start.6 = (bf16[512,512]{1,0:T(8,128)(2,1)}, bf16[512,512]{1,0:T(8,128)(2,1)}, u32[]{:S(2)}, u32[]{:S(2)}) collective-permute-start(bf16[512,512]{1,0:T(8,128)(2,1)} %collective-permute-done.5.refs_10_), channel_id=1, source_target_pairs={{0,4},{4,0},{8,12},{12,8},{16,20},{20,16},{24,28},{28,24},{1,5},{5... | collective-permute-start | bytes 1572872 | tf_op jit(solution)/shard_map/ppermute | solution.py:346
  94.2 7.8 %collective-permute-start.7 = (f32[3,8,8,64]{3,2,1,0:T(8,128)S(1)}, f32[3,8,8,64]{3,2,1,0:T(8,128)S(1)}, u32[]{:S(2)}, u32[]{:S(2)}) collective-permute-start(f32[3,8,8,64]{3,2,1,0:T(8,128)S(1)} %pad_maximum_fusion.7), channel_id=1, source_target_pairs={{0,16},{4,20},{8,24},{12,28},{16,0},{20,4},{24,8},{28,12},{1,17},{... | collective-permute-start | bytes 147464 | tf_op jit(solution)/shard_map/ppermute | solution.py:343
  96.3 30.9 %collective-permute-start.9 = (bf16[2,512,512]{2,1,0:T(8,128)(2,1)S(1)}, bf16[2,512,512]{2,1,0:T(8,128)(2,1)}, u32[]{:S(2)}, u32[]{:S(2)}) collective-permute-start(bf16[2,512,512]{2,1,0:T(8,128)(2,1)S(1)} %pad_maximum_fusion.1), channel_id=1, source_target_pairs={{0,8},{4,12},{8,0},{12,4},{16,24},{20,28},{24,16},{28,20},{1,9},{5... | collective-permute-start | bytes 3145736 | tf_op jit(solution)/shard_map/ppermute | solution.py:346
  122.0 42.1 %collective-permute-start.18 = (bf16[2,512,512]{2,1,0:T(8,128)(2,1)}, bf16[2,512,512]{2,1,0:T(8,128)(2,1)}, u32[]{:S(2)}, u32[]{:S(2)}) collective-permute-start(bf16[2,512,512]{2,1,0:T(8,128)(2,1)} %get-tuple-element.28), channel_id=1, source_target_pairs={{0,8},{4,12},{8,0},{12,4},{16,24},{20,28},{24,16},{28,20},{1,9},{5... | collective-permute-start | bytes 3145736 | tf_op jit(solution)/shard_map/ppermute | solution.py:346
  124.8 37.5 %collective-permute-start.8 = (bf16[512,512]{1,0:T(8,128)(2,1)}, bf16[512,512]{1,0:T(8,128)(2,1)}, u32[]{:S(2)}, u32[]{:S(2)}) collective-permute-start(bf16[512,512]{1,0:T(8,128)(2,1)} %get-tuple-element.19), channel_id=1, source_target_pairs={{0,16},{4,20},{8,24},{12,28},{16,0},{20,4},{24,8},{28,12},{1,17},{... | collective-permute-start | bytes 1572872 | tf_op jit(solution)/shard_map/ppermute | solution.py:343
  126.7 40.2 %collective-permute-start.14 = (bf16[2,512,512]{2,1,0:T(8,128)(2,1)}, bf16[2,512,512]{2,1,0:T(8,128)(2,1)}, u32[]{:S(2)}, u32[]{:S(2)}) collective-permute-start(bf16[2,512,512]{2,1,0:T(8,128)(2,1)} %get-tuple-element.24), channel_id=1, source_target_pairs={{0,4},{4,0},{8,12},{12,8},{16,20},{20,16},{24,28},{28,24},{1,5},{5... | collective-permute-start | bytes 3145736 | tf_op jit(solution)/shard_map/ppermute | solution.py:346
  127.2 35.1 %copy-start.4 = (f32[512,512]{1,0:T(8,128)S(1)}, f32[512,512]{1,0:T(8,128)}, u32[]{:S(2)}) copy-start(f32[512,512]{1,0:T(8,128)} %copy-done.3) | copy-start | bytes 3145732
  145.7 51.5 %collective-permute-start.20 = (bf16[2,512,512]{2,1,0:T(8,128)(2,1)S(1)}, bf16[2,512,512]{2,1,0:T(8,128)(2,1)S(1)}, u32[]{:S(2)}, u32[]{:S(2)}) collective-permute-start(bf16[2,512,512]{2,1,0:T(8,128)(2,1)S(1)} %get-tuple-element.30), channel_id=1, source_target_pairs={{0,8},{4,12},{8,0},{12,4},{16,24},{20,28},{24,16},{28,20},{1,9},{5... | collective-permute-start | bytes 3145736 | tf_op jit(solution)/shard_map/ppermute | solution.py:346
  163.5 35.7 %collective-permute-start.16 = (bf16[2,512,512]{2,1,0:T(8,128)(2,1)S(1)}, bf16[2,512,512]{2,1,0:T(8,128)(2,1)S(1)}, u32[]{:S(2)}, u32[]{:S(2)}) collective-permute-start(bf16[2,512,512]{2,1,0:T(8,128)(2,1)S(1)} %get-tuple-element.26), channel_id=1, source_target_pairs={{0,4},{4,0},{8,12},{12,8},{16,20},{20,16},{24,28},{28,24},{1,5},{5... | collective-permute-start | bytes 3145736 | tf_op jit(solution)/shard_map/ppermute | solution.py:346
  164.1 31.8 %collective-permute-start.10 = (bf16[512,512]{1,0:T(8,128)(2,1)S(1)}, bf16[512,512]{1,0:T(8,128)(2,1)S(1)}, u32[]{:S(2)}, u32[]{:S(2)}) collective-permute-start(bf16[512,512]{1,0:T(8,128)(2,1)S(1)} %get-tuple-element.22), channel_id=1, source_target_pairs={{0,16},{4,20},{8,24},{12,28},{16,0},{20,4},{24,8},{28,12},{1,17},{... | collective-permute-start | bytes 1572872 | tf_op jit(solution)/shard_map/ppermute | solution.py:343
  165.3 32.6 %collective-permute-start.19 = (bf16[512,512]{1,0:T(8,128)(2,1)S(1)}, bf16[512,512]{1,0:T(8,128)(2,1)S(1)}, u32[]{:S(2)}, u32[]{:S(2)}) collective-permute-start(bf16[512,512]{1,0:T(8,128)(2,1)S(1)} %fusion.6), channel_id=1, source_target_pairs={{0,4},{4,0},{8,12},{12,8},{16,20},{20,16},{24,28},{28,24},{1,5},{5... | collective-permute-start | bytes 1572872 | tf_op jit(solution)/shard_map/ppermute | solution.py:346
  168.8 47.8 %collective-permute-start.15 = (bf16[512,512]{1,0:T(8,128)(2,1)}, bf16[512,512]{1,0:T(8,128)(2,1)}, u32[]{:S(2)}, u32[]{:S(2)}) collective-permute-start(bf16[512,512]{1,0:T(8,128)(2,1)} %fusion.4), channel_id=1, source_target_pairs={{0,8},{4,12},{8,0},{12,4},{16,24},{20,28},{24,16},{28,20},{1,9},{5... | collective-permute-start | bytes 1572872 | tf_op jit(solution)/shard_map/ppermute | solution.py:346
  197.3 9.2 %collective-permute-start.21 = (bf16[512,512]{1,0:T(8,128)(2,1)S(1)}, bf16[512,512]{1,0:T(8,128)(2,1)S(1)}, u32[]{:S(2)}, u32[]{:S(2)}) collective-permute-start(bf16[512,512]{1,0:T(8,128)(2,1)S(1)} %fusion.7), channel_id=1, source_target_pairs={{0,4},{4,0},{8,12},{12,8},{16,20},{20,16},{24,28},{28,24},{1,5},{5... | collective-permute-start | bytes 1572872 | tf_op jit(solution)/shard_map/ppermute | solution.py:346
  199.2 8.7 %copy-start.8 = (bf16[2,512,512]{2,1,0:T(8,128)(2,1)}, bf16[2,512,512]{2,1,0:T(8,128)(2,1)S(1)}, u32[]{:S(2)}) copy-start(bf16[2,512,512]{2,1,0:T(8,128)(2,1)S(1)} %collective-permute-done.16) | copy-start | bytes 3145732
  200.2 17.8 %collective-permute-start.17 = (bf16[512,512]{1,0:T(8,128)(2,1)}, bf16[512,512]{1,0:T(8,128)(2,1)}, u32[]{:S(2)}, u32[]{:S(2)}) collective-permute-start(bf16[512,512]{1,0:T(8,128)(2,1)} %fusion.5), channel_id=1, source_target_pairs={{0,8},{4,12},{8,0},{12,4},{16,24},{20,28},{24,16},{28,20},{1,9},{5... | collective-permute-start | bytes 1572872 | tf_op jit(solution)/shard_map/ppermute | solution.py:346
  207.9 19.2 %all-to-all-start.1 = ((bf16[4,128,1024]{2,1,0:T(8,128)(2,1)}), bf16[4,128,1024]{2,1,0:T(8,128)(2,1)}, u32[]{:S(2)}, u32[]{:S(2)}) async-start(bf16[4,128,1024]{2,1,0:T(8,128)(2,1)} %bitcast.94), calls=%async_computation.1 | async-start | bytes 2097152 | tf_op jit(solution)/shard_map/all_to_all | solution.py:489
  212.2 5.8 %copy-start.9 = (bf16[2,512,512]{2,1,0:T(8,128)(2,1)S(1)}, bf16[2,512,512]{2,1,0:T(8,128)(2,1)}, u32[]{:S(2)}) copy-start(bf16[2,512,512]{2,1,0:T(8,128)(2,1)} %copy-done.8) | copy-start | bytes 3145732
  213.2 18.6 %collective-permute-start.11 = (bf16[128,1024]{1,0:T(8,128)(2,1)}, bf16[128,1024]{1,0:T(8,128)(2,1)}, u32[]{:S(2)}, u32[]{:S(2)}) collective-permute-start(bf16[128,1024]{1,0:T(8,128)(2,1)} %get-tuple-element.38), channel_id=1, source_target_pairs={{0,1},{1,2},{2,3},{3,0},{4,5},{5,6},{6,7},{7,4},{8,9},{9,10},{10,1... | collective-permute-start | bytes 786440 | tf_op jit(solution)/shard_map/ppermute | solution.py:512
  213.6 19.2 %collective-permute-start.12 = (bf16[128,1024]{1,0:T(8,128)(2,1)}, bf16[128,1024]{1,0:T(8,128)(2,1)}, u32[]{:S(2)}, u32[]{:S(2)}) collective-permute-start(bf16[128,1024]{1,0:T(8,128)(2,1)} %get-tuple-element.37), channel_id=1, source_target_pairs={{0,2},{1,3},{2,0},{3,1},{4,6},{5,7},{6,4},{7,5},{8,10},{9,11},{10,... | collective-permute-start | bytes 786440 | tf_op jit(solution)/shard_map/ppermute | solution.py:512
  215.3 20.7 %collective-permute-start.13 = (bf16[128,1024]{1,0:T(8,128)(2,1)}, bf16[128,1024]{1,0:T(8,128)(2,1)}, u32[]{:S(2)}, u32[]{:S(2)}) collective-permute-start(bf16[128,1024]{1,0:T(8,128)(2,1)} %get-tuple-element.36), channel_id=1, source_target_pairs={{0,3},{1,0},{2,1},{3,2},{4,7},{5,4},{6,5},{7,6},{8,11},{9,8},{10,9... | collective-permute-start | bytes 786440 | tf_op jit(solution)/shard_map/ppermute | solution.py:512
  219.3 16.7 %copy-start.11 = (bf16[1,128,1024]{2,1,0:T(8,128)(2,1)S(1)}, bf16[1,128,1024]{2,1,0:T(8,128)(2,1)}, u32[]{:S(2)}) copy-start(bf16[1,128,1024]{2,1,0:T(8,128)(2,1)} %get-tuple-element.35) | copy-start | bytes 786436
  227.2 21.9 %all-to-all-start = ((bf16[4,128,1024]{2,1,0:T(8,128)(2,1)}), bf16[4,128,1024]{2,1,0:T(8,128)(2,1)S(1)}, u32[]{:S(2)}, u32[]{:S(2)}) async-start(bf16[4,128,1024]{2,1,0:T(8,128)(2,1)} %bitcast.33), calls=%async_computation | async-start | bytes 2097152 | tf_op jit(solution)/shard_map/all_to_all | solution.py:489
  (6 other events, 17.7 us)

commit v7 on v6

--- a/solution.py
+++ b/solution.py
@@ -13,6 +13,7 @@
 GROUP = 4
 BATCH = 8
 CUTS = (0.0, 0.5, 1.0)
+VALUE_AXES = (1, 2)
 JOINED = 4
 LOG2E = math.log2(math.e)
 SCALE = DH**-0.5
@@ -126,7 +127,7 @@
             out_ref[r, 0, pl.ds(2 * t + 1, 1), :] = found[:, BS:]
 
 
-def grads_kernel(sizes, head0, meta, table, *refs):
+def grads_kernel(sizes, value_axis, head0, meta, table, *refs):
     seq_count, remote, blocks, heads = sizes
     sources = remote + 1
     tokens = blocks * BS
@@ -310,14 +311,14 @@
 
     lax.fori_loop(0, (count + BATCH - 1) // BATCH, batch, 0)
 
-    dq_own[...] = dq_sum[pl.ds(0, tokens), :] * SCALE
+    dq_own[...] = (dq_sum[pl.ds(0, tokens), :] * SCALE).astype(jnp.bfloat16)
     for r in range(remote):
         dq_far[r][...] = (dq_sum[pl.ds((r + 1) * tokens, tokens), :] * SCALE).astype(jnp.bfloat16)
     for j in range(GROUP):
         rows = pl.ds(aligned(BS + (pos ^ j) * tokens), tokens)
         for total, keep, send, axis, factor in (
             (dk_sum, dk_keep, dk_send, 1, SCALE),
-            (dv_sum, dv_keep, dv_send, 2, 1.0),
+            (dv_sum, dv_keep, dv_send, value_axis, 1.0),
         ):
             slot = (j >> 1) if axis == 1 else (j & 1)
             target = send if j & axis else keep
@@ -438,7 +439,7 @@
         half_spec = pl.BlockSpec((GROUP // 2, tokens, DH), lambda h, *_: (0, 0, h))
         half_shape = jax.ShapeDtypeStruct((GROUP // 2, tokens, width), jnp.bfloat16)
         return pl.pallas_call(
-            partial(grads_kernel, sizes, head0),
+            partial(grads_kernel, sizes, VALUE_AXES[c], head0),
             grid_spec=pltpu.PrefetchScalarGridSpec(
                 num_scalar_prefetch=2,
                 grid=(count,),
@@ -462,7 +463,7 @@
                     pltpu.SMEM((2, sources * (3 * blocks + 2) + 2 * BATCH), jnp.int32),
                 ],
             ),
-            out_shape=[jax.ShapeDtypeStruct((tokens, width), jnp.float32)]
+            out_shape=[jax.ShapeDtypeStruct((tokens, width), jnp.bfloat16)]
             + [jax.ShapeDtypeStruct((tokens, width), jnp.bfloat16)] * remote
             + [half_shape] * 4,
             compiler_params=pltpu.CompilerParams(vmem_limit_bytes=48 * 2**20),
@@ -491,13 +492,13 @@
     dq_parts, dk_parts, dv_parts = [], [], []
     for c in range(len(chunks)):
         outs = gradients(c)
-        dq, dq_far = outs[0], outs[1:sources]
+        dq, dq_far = wide(outs[0]), outs[1:sources]
         dk_keep, dk_send, dv_keep, dv_send = outs[sources:]
         for r in range(1, sources):
             dq = dq + wide(shift(dq_far[r - 1], -r))
         dq_parts.append(dq.astype(jnp.bfloat16))
         dk_parts.append(reduced(dk_keep, dk_send, 1, 2))
-        dv_parts.append(reduced(dv_keep, dv_send, 2, 1))
+        dv_parts.append(reduced(dv_keep, dv_send, VALUE_AXES[c], 3 - VALUE_AXES[c]))
     def to_tokens_by_steps(array):
         groups = lax.axis_size("head")
         here = lax.axis_index("head")

time: 252 us -> 250 us (level); the launches traced: 250 us -> 245 us
  waiting for transfers between devices: 130 us -> 123 us
    ppermute x5, waiting for transfers between devices: 43.4 us -> 11.6 us  [shift(): return lax.ppermute(array, 'seq', pairs)]
    ppermute x14, waiting for transfers between devices: 65.9 us -> 93.4 us  [flip(): return lax.ppermute(array, 'seq', [(i, i ^ j) for i in range(seq_count)])]
    ppermute x5, starting transfers between devices: 8.48 us -> 13.5 us  [shift(): return lax.ppermute(array, 'seq', pairs)]
    ppermute x14, starting transfers between devices: 18.2 us -> 14.9 us  [flip(): return lax.ppermute(array, 'seq', [(i, i ^ j) for i in range(seq_count)])]
    all_to_all x2, waiting for transfers between devices: 15.1 us -> 12.6 us  [to_tokens(): lax.all_to_all(array, 'head', split_axis=0, concat_axis=1, tiled=True)]
  transfers between devices with their start and end apart: 24 -> 24, of which waited for: 11 -> 13; matrix products, arithmetic and copies ran while one was open for 13% -> 13% of each run, Pallas kernels for 19% -> 19%
where the time goes in v7:
time: 250 us; the launch traced here: 245 us
  waiting for transfers between devices  123 us (49%)
  Pallas kernels  47.6 us (19%)
  starting transfers between devices  39.5 us (16%)
  other arithmetic  23 us (9%)
  local copies, waits for them, and re-layouts  10.9 us (4%)
    ppermute x14, waiting for transfers between devices, flip(): return lax.ppermute(array, 'seq', [(i, i ^ j) for i in range(seq_count)])  93.4 us
    pallas_call x2, Pallas kernels, gradients(): pl.pallas_call(partial(grads_kernel, sizes, VALUE_AXES[c], head0), grid_s...  37.2 us
    ppermute x14, starting transfers between devices, flip(): return lax.ppermute(array, 'seq', [(i, i ^ j) for i in range(seq_count)])  14.9 us
    ppermute x5, starting transfers between devices, shift(): return lax.ppermute(array, 'seq', pairs)  13.5 us
    all_to_all x2, waiting for transfers between devices, to_tokens(): lax.all_to_all(array, 'head', split_axis=0, concat_axis=1, tiled=True)  12.6 us
    ppermute x5, waiting for transfers between devices, shift(): return lax.ppermute(array, 'seq', pairs)  11.6 us
    pallas_call x1, Pallas kernels, on_device(): pl.pallas_call(partial(norm_kernel, sizes), grid_spec=pltpu.PrefetchScala...  10.5 us
    all_to_all x2, starting transfers between devices, to_tokens(): lax.all_to_all(array, 'head', split_axis=0, concat_axis=1, tiled=True)  7.76 us
  transfers between devices with their start and end apart: 24, of which 13 were waited for; matrix products, arithmetic and copies ran while one was open for 13% of the time, Pallas kernels for 19%

profile of v7, /device:TPU:8, one launch (start us, length us, event | category | flops | bytes accessed | tf_op | source)
XLA Modules:
  0.0 245.0 jit_solution(4510475441788149136)
XLA Ops:
  0.7 3.2 %pad_maximum_fusion = bf16[2,512,1024]{2,1,0:T(8,128)(2,1)} fusion(bf16[1,512,1024]{2,1,0:T(8,128)(2,1)} %bitcast.90, bf16[1,512,1024]{2,1,0:T(8,128)(2,1)} %bitcast.89), kind=kLoop, calls=%fused_computation | loop fusion | flops 1048576 | bytes 4194304 | tf_op jit(solution)/shard_map/stack | solution.py:361
  3.9 1.9 collective-permute-start.2
  5.9 2.6 %collective-permute-start = (bf16[512,1024]{1,0:T(8,128)(2,1)S(1)}, bf16[512,1024]{1,0:T(8,128)(2,1)}, u32[]{:S(2)}, u32[]{:S(2)}) collective-permute-start(bf16[512,1024]{1,0:T(8,128)(2,1)S(1)} %copy-done.1), channel_id=1, source_target_pairs={{0,16},{4,20},{8,24},{12,28},{16,0},{20,4},{24,8},{28,12},{1,17},{... | collective-permute-start | bytes 3145736 | tf_op jit(solution)/shard_map/ppermute | solution.py:344
  8.4 33.4 %collective-permute-done.3.refs_4_.refs_6_ = bf16[512,1024]{1,0:T(8,128)(2,1)S(1)} collective-permute-done((bf16[512,1024]{1,0:T(8,128)(2,1)}, bf16[512,1024]{1,0:T(8,128)(2,1)S(1)}, u32[]{:S(2)}, u32[]{:S(2)}) %collective-permute-start.3) | collective-permute-done | bytes 1048608 | tf_op jit(solution)/shard_map/ppermute | solution.py:347
  41.9 2.6 %collective-permute-start.4 = (bf16[512,1024]{1,0:T(8,128)(2,1)S(1)}, bf16[512,1024]{1,0:T(8,128)(2,1)}, u32[]{:S(2)}, u32[]{:S(2)}) collective-permute-start(bf16[512,1024]{1,0:T(8,128)(2,1)S(1)} %collective-permute-done.3.refs_4_.refs_6_), channel_id=1, source_target_pairs={{0,4},{4,0},{8,12},{12,8},{16,20},{20,16},{24,28},{28,24},{1,5},{5... | collective-permute-start | bytes 3145736 | tf_op jit(solution)/shard_map/ppermute | solution.py:347
  44.5 3.4 %collective-permute-start.1 = (bf16[512,1024]{1,0:T(8,128)(2,1)}, bf16[512,1024]{1,0:T(8,128)(2,1)}, u32[]{:S(2)}, u32[]{:S(2)}) collective-permute-start(bf16[512,1024]{1,0:T(8,128)(2,1)} %refs_2_.5), channel_id=1, source_target_pairs={{0,16},{4,20},{8,24},{12,28},{16,0},{20,4},{24,8},{28,12},{1,17},{... | collective-permute-start | bytes 3145736 | tf_op jit(solution)/shard_map/ppermute | solution.py:344
  49.9 1.6 multiply_bitcast_fusion
  51.5 1.9 copy.28
  53.3 2.3 reduce_sum.27
  55.9 26.2 %collective-permute-done.5.refs_10_ = bf16[512,512]{1,0:T(8,128)(2,1)} collective-permute-done((bf16[512,512]{1,0:T(8,128)(2,1)}, bf16[512,512]{1,0:T(8,128)(2,1)}, u32[]{:S(2)}, u32[]{:S(2)}) %collective-permute-start.5) | collective-permute-done | bytes 524320 | tf_op jit(solution)/shard_map/ppermute | solution.py:347
  82.1 1.5 collective-permute-start.6
  83.7 10.5 %partial_norms.1 = f32[2,8,8,64]{3,2,1,0:T(8,128)S(1)} custom-call(s32[3]{0:T(128)S(1)} %pad_add_fusion.meta, s32[1536]{0:T(1024)S(1)} %reshape.99.table, bf16[512,1024]{1,0:T(8,128)(2,1)S(1)} %copy-done.1, bf16[512,1024]{1,0:T(8,128)(2,1)} %collective-permute-done.refs_1_, bf16[512,1024]{1,0:T(8,128)(2,1)S(1)} %copy-done, ...), custom_call_target="tpu_custom_call" | custom-call | tf_op jit(solution)/shard_map/partial_norms/pallas_call | solution.py:395
  96.3 2.5 %collective-permute-start.9 = (bf16[2,512,512]{2,1,0:T(8,128)(2,1)S(1)}, bf16[2,512,512]{2,1,0:T(8,128)(2,1)}, u32[]{:S(2)}, u32[]{:S(2)}) collective-permute-start(bf16[2,512,512]{2,1,0:T(8,128)(2,1)S(1)} %pad_maximum_fusion.1), channel_id=1, source_target_pairs={{0,8},{4,12},{8,0},{12,4},{16,24},{20,28},{24,16},{28,20},{1,9},{5... | collective-permute-start | bytes 3145736 | tf_op jit(solution)/shard_map/ppermute | solution.py:347
  98.8 3.3 %collective-permute-done.7 = f32[3,8,8,64]{3,2,1,0:T(8,128)S(1)} collective-permute-done((f32[3,8,8,64]{3,2,1,0:T(8,128)S(1)}, f32[3,8,8,64]{3,2,1,0:T(8,128)S(1)}, u32[]{:S(2)}, u32[]{:S(2)}) %collective-permute-start.7) | collective-permute-done | bytes 49184 | tf_op jit(solution)/shard_map/ppermute | solution.py:344
  102.7 18.7 %gradients.2 = (bf16[512,512]{1,0:T(8,128)(2,1)S(1)}, bf16[512,512]{1,0:T(8,128)(2,1)}, bf16[2,512,512]{2,1,0:T(8,128)(2,1)S(1)}, bf16[2,512,512]{2,1,0:T(8,128)...) custom-call(s32[3]{0:T(128)S(1)} %pad_add_fusion.meta, s32[1536]{0:T(1024)S(1)} %reshape.99.table, ...), custom_call_target="tpu_custom_call" | custom-call | tf_op jit(solution)/shard_map/gradients/pallas_call | solution.py:441
  123.1 3.4 %collective-permute-start.8 = (bf16[512,512]{1,0:T(8,128)(2,1)}, bf16[512,512]{1,0:T(8,128)(2,1)}, u32[]{:S(2)}, u32[]{:S(2)}) collective-permute-start(bf16[512,512]{1,0:T(8,128)(2,1)} %get-tuple-element.19), channel_id=1, source_target_pairs={{0,16},{4,20},{8,24},{12,28},{16,0},{20,4},{24,8},{28,12},{1,17},{... | collective-permute-start | bytes 1572872 | tf_op jit(solution)/shard_map/ppermute | solution.py:344
  128.0 18.5 %gradients.3 = (bf16[512,512]{1,0:T(8,128)(2,1)S(1)}, bf16[512,512]{1,0:T(8,128)(2,1)S(1)}, bf16[2,512,512]{2,1,0:T(8,128)(2,1)S(1)}, bf16[2,512,512]{2,1,0:T(8,...) custom-call(s32[3]{0:T(128)S(1)} %pad_add_fusion.meta, s32[1536]{0:T(1024)S(1)} %reshape.99.table, ...), custom_call_target="tpu_custom_call" | custom-call | tf_op jit(solution)/shard_map/gradients/pallas_call | solution.py:441
  148.6 3.5 %collective-permute-start.10 = (bf16[512,512]{1,0:T(8,128)(2,1)S(1)}, bf16[512,512]{1,0:T(8,128)(2,1)S(1)}, u32[]{:S(2)}, u32[]{:S(2)}) collective-permute-start(bf16[512,512]{1,0:T(8,128)(2,1)S(1)} %get-tuple-element.22), channel_id=1, source_target_pairs={{0,16},{4,20},{8,24},{12,28},{16,0},{20,4},{24,8},{28,12},{1,17},{... | collective-permute-start | bytes 1572872 | tf_op jit(solution)/shard_map/ppermute | solution.py:344
  153.6 17.4 %collective-permute-done.14 = bf16[2,512,512]{2,1,0:T(8,128)(2,1)} collective-permute-done((bf16[2,512,512]{2,1,0:T(8,128)(2,1)}, bf16[2,512,512]{2,1,0:T(8,128)(2,1)}, u32[]{:S(2)}, u32[]{:S(2)}) %collective-permute-start.14) | collective-permute-done | bytes 1048608 | tf_op jit(solution)/shard_map/ppermute | solution.py:347
  171.1 2.0 fusion.4
  173.0 2.4 collective-permute-start.15
  175.4 8.3 %collective-permute-done.10 = bf16[512,512]{1,0:T(8,128)(2,1)S(1)} collective-permute-done((bf16[512,512]{1,0:T(8,128)(2,1)S(1)}, bf16[512,512]{1,0:T(8,128)(2,1)S(1)}, u32[]{:S(2)}, u32[]{:S(2)}) %collective-permute-start.10) | collective-permute-done | bytes 524320 | tf_op jit(solution)/shard_map/ppermute | solution.py:344
  185.4 9.8 %collective-permute-done.19 = bf16[512,512]{1,0:T(8,128)(2,1)S(1)} collective-permute-done((bf16[512,512]{1,0:T(8,128)(2,1)S(1)}, bf16[512,512]{1,0:T(8,128)(2,1)S(1)}, u32[]{:S(2)}, u32[]{:S(2)}) %collective-permute-start.19) | collective-permute-done | bytes 524320 | tf_op jit(solution)/shard_map/ppermute | solution.py:347
  197.5 4.0 %collective-permute-done.21 = bf16[512,512]{1,0:T(8,128)(2,1)S(1)} collective-permute-done((bf16[512,512]{1,0:T(8,128)(2,1)S(1)}, bf16[512,512]{1,0:T(8,128)(2,1)S(1)}, u32[]{:S(2)}, u32[]{:S(2)}) %collective-permute-start.21) | collective-permute-done | bytes 524320 | tf_op jit(solution)/shard_map/ppermute | solution.py:347
  202.8 4.2 %all-to-all-start.1 = ((bf16[4,128,1024]{2,1,0:T(8,128)(2,1)}), bf16[4,128,1024]{2,1,0:T(8,128)(2,1)}, u32[]{:S(2)}, u32[]{:S(2)}) async-start(bf16[4,128,1024]{2,1,0:T(8,128)(2,1)} %bitcast.94), calls=%async_computation.1 | async-start | bytes 2097152 | tf_op jit(solution)/shard_map/all_to_all | solution.py:490
  208.5 1.7 collective-permute-start.12
  212.9 2.6 %collective-permute-done.17 = bf16[512,512]{1,0:T(8,128)(2,1)} collective-permute-done((bf16[512,512]{1,0:T(8,128)(2,1)}, bf16[512,512]{1,0:T(8,128)(2,1)}, u32[]{:S(2)}, u32[]{:S(2)}) %collective-permute-start.17) | collective-permute-done | bytes 524320 | tf_op jit(solution)/shard_map/ppermute | solution.py:347
  217.9 4.2 %all-to-all-done.1 = bf16[4,128,1024]{2,1,0:T(8,128)(2,1)} async-done(((bf16[4,128,1024]{2,1,0:T(8,128)(2,1)}), bf16[4,128,1024]{2,1,0:T(8,128)(2,1)}, u32[]{:S(2)}, u32[]{:S(2)}) %all-to-all-start.1) | async-done | bytes 1048608 | tf_op jit(solution)/shard_map/all_to_all | solution.py:490
  222.1 3.5 %all-to-all-start = ((bf16[4,128,1024]{2,1,0:T(8,128)(2,1)}), bf16[4,128,1024]{2,1,0:T(8,128)(2,1)S(1)}, u32[]{:S(2)}, u32[]{:S(2)}) async-start(bf16[4,128,1024]{2,1,0:T(8,128)(2,1)} %bitcast.33), calls=%async_computation | async-start | bytes 2097152 | tf_op jit(solution)/shard_map/all_to_all | solution.py:490
  227.7 3.2 %collective-permute-done.13 = bf16[128,1024]{1,0:T(8,128)(2,1)} collective-permute-done((bf16[128,1024]{1,0:T(8,128)(2,1)}, bf16[128,1024]{1,0:T(8,128)(2,1)}, u32[]{:S(2)}, u32[]{:S(2)}) %collective-permute-start.13) | collective-permute-done | bytes 262176 | tf_op jit(solution)/shard_map/ppermute | solution.py:513
  233.3 2.3 copy.27
  235.6 8.4 %all-to-all-done = bf16[4,128,1024]{2,1,0:T(8,128)(2,1)S(1)} async-done(((bf16[4,128,1024]{2,1,0:T(8,128)(2,1)}), bf16[4,128,1024]{2,1,0:T(8,128)(2,1)S(1)}, u32[]{:S(2)}, u32[]{:S(2)}) %all-to-all-start) | async-done | bytes 1048608 | tf_op jit(solution)/shard_map/all_to_all | solution.py:490
  (94 shorter events, 29.2 us)
Async XLA Ops:
  0.6 41.2 %collective-permute-start.3 = (bf16[512,1024]{1,0:T(8,128)(2,1)}, bf16[512,1024]{1,0:T(8,128)(2,1)S(1)}, u32[]{:S(2)}, u32[]{:S(2)}) collective-permute-start(bf16[512,1024]{1,0:T(8,128)(2,1)} %refs_4_.3), channel_id=1, source_target_pairs={{0,8},{4,12},{8,0},{12,4},{16,24},{20,28},{24,16},{28,20},{1,9},{5... | collective-permute-start | bytes 3145736 | tf_op jit(solution)/shard_map/ppermute | solution.py:347
  0.7 47.1 %copy-start.12 = (s32[64,8,3]{0,1,2:T(8,128)S(1)}, s32[64,8,3]{0,1,2:T(8,128)}, u32[]{:S(2)}) copy-start(s32[64,8,3]{0,1,2:T(8,128)} %param.12) | copy-start | bytes 18436
  0.7 47.5 %copy-start.5 = (bf16[512,1024]{1,0:T(8,128)(2,1)S(1)}, bf16[512,1024]{1,0:T(8,128)(2,1)}, u32[]{:S(2)}) copy-start(bf16[512,1024]{1,0:T(8,128)(2,1)} %refs_8_.3) | copy-start | bytes 3145732
  3.9 79.7 %collective-permute-start.2 = (bf16[2,512,1024]{2,1,0:T(8,128)(2,1)}, bf16[2,512,1024]{2,1,0:T(8,128)(2,1)}, u32[]{:S(2)}, u32[]{:S(2)}) collective-permute-start(bf16[2,512,1024]{2,1,0:T(8,128)(2,1)} %pad_maximum_fusion), channel_id=1, source_target_pairs={{0,4},{4,0},{8,12},{12,8},{16,20},{20,16},{24,28},{28,24},{1,5},{5... | collective-permute-start | bytes 6291464 | tf_op jit(solution)/shard_map/ppermute | solution.py:347
  5.9 77.8 %collective-permute-start = (bf16[512,1024]{1,0:T(8,128)(2,1)S(1)}, bf16[512,1024]{1,0:T(8,128)(2,1)}, u32[]{:S(2)}, u32[]{:S(2)}) collective-permute-start(bf16[512,1024]{1,0:T(8,128)(2,1)S(1)} %copy-done.1), channel_id=1, source_target_pairs={{0,16},{4,20},{8,24},{12,28},{16,0},{20,4},{24,8},{28,12},{1,17},{... | collective-permute-start | bytes 3145736 | tf_op jit(solution)/shard_map/ppermute | solution.py:344
  41.9 41.8 %copy-start.2 = (bf16[512,1024]{1,0:T(8,128)(2,1)}, bf16[512,1024]{1,0:T(8,128)(2,1)S(1)}, u32[]{:S(2)}) copy-start(bf16[512,1024]{1,0:T(8,128)(2,1)S(1)} %collective-permute-done.3.refs_4_.refs_6_) | copy-start | bytes 3145732
  41.9 41.8 %collective-permute-start.4 = (bf16[512,1024]{1,0:T(8,128)(2,1)S(1)}, bf16[512,1024]{1,0:T(8,128)(2,1)}, u32[]{:S(2)}, u32[]{:S(2)}) collective-permute-start(bf16[512,1024]{1,0:T(8,128)(2,1)S(1)} %collective-permute-done.3.refs_4_.refs_6_), channel_id=1, source_target_pairs={{0,4},{4,0},{8,12},{12,8},{16,20},{20,16},{24,28},{28,24},{1,5},{5... | collective-permute-start | bytes 3145736 | tf_op jit(solution)/shard_map/ppermute | solution.py:347
  44.5 58.2 %collective-permute-start.1 = (bf16[512,1024]{1,0:T(8,128)(2,1)}, bf16[512,1024]{1,0:T(8,128)(2,1)}, u32[]{:S(2)}, u32[]{:S(2)}) collective-permute-start(bf16[512,1024]{1,0:T(8,128)(2,1)} %refs_2_.5), channel_id=1, source_target_pairs={{0,16},{4,20},{8,24},{12,28},{16,0},{20,4},{24,8},{28,12},{1,17},{... | collective-permute-start | bytes 3145736 | tf_op jit(solution)/shard_map/ppermute | solution.py:344
  49.3 32.8 %collective-permute-start.5 = (bf16[512,512]{1,0:T(8,128)(2,1)}, bf16[512,512]{1,0:T(8,128)(2,1)}, u32[]{:S(2)}, u32[]{:S(2)}) collective-permute-start(bf16[512,512]{1,0:T(8,128)(2,1)} %get-tuple-element.17), channel_id=1, source_target_pairs={{0,8},{4,12},{8,0},{12,4},{16,24},{20,28},{24,16},{28,20},{1,9},{5... | collective-permute-start | bytes 1572872 | tf_op jit(solution)/shard_map/ppermute | solution.py:347
  53.3 30.3 %copy-start = (bf16[512,1024]{1,0:T(8,128)(2,1)S(1)}, bf16[512,1024]{1,0:T(8,128)(2,1)}, u32[]{:S(2)}) copy-start(bf16[512,1024]{1,0:T(8,128)(2,1)} %refs_4_.3) | copy-start | bytes 3145732
  82.1 20.5 %collective-permute-start.6 = (bf16[512,512]{1,0:T(8,128)(2,1)}, bf16[512,512]{1,0:T(8,128)(2,1)}, u32[]{:S(2)}, u32[]{:S(2)}) collective-permute-start(bf16[512,512]{1,0:T(8,128)(2,1)} %collective-permute-done.5.refs_10_), channel_id=1, source_target_pairs={{0,4},{4,0},{8,12},{12,8},{16,20},{20,16},{24,28},{28,24},{1,5},{5... | collective-permute-start | bytes 1572872 | tf_op jit(solution)/shard_map/ppermute | solution.py:347
  94.2 7.8 %collective-permute-start.7 = (f32[3,8,8,64]{3,2,1,0:T(8,128)S(1)}, f32[3,8,8,64]{3,2,1,0:T(8,128)S(1)}, u32[]{:S(2)}, u32[]{:S(2)}) collective-permute-start(f32[3,8,8,64]{3,2,1,0:T(8,128)S(1)} %pad_maximum_fusion.7), channel_id=1, source_target_pairs={{0,16},{4,20},{8,24},{12,28},{16,0},{20,4},{24,8},{28,12},{1,17},{... | collective-permute-start | bytes 147464 | tf_op jit(solution)/shard_map/ppermute | solution.py:344
  96.3 31.8 %collective-permute-start.9 = (bf16[2,512,512]{2,1,0:T(8,128)(2,1)S(1)}, bf16[2,512,512]{2,1,0:T(8,128)(2,1)}, u32[]{:S(2)}, u32[]{:S(2)}) collective-permute-start(bf16[2,512,512]{2,1,0:T(8,128)(2,1)S(1)} %pad_maximum_fusion.1), channel_id=1, source_target_pairs={{0,8},{4,12},{8,0},{12,4},{16,24},{20,28},{24,16},{28,20},{1,9},{5... | collective-permute-start | bytes 3145736 | tf_op jit(solution)/shard_map/ppermute | solution.py:347
  122.2 29.9 %collective-permute-start.18 = (bf16[2,512,512]{2,1,0:T(8,128)(2,1)}, bf16[2,512,512]{2,1,0:T(8,128)(2,1)}, u32[]{:S(2)}, u32[]{:S(2)}) collective-permute-start(bf16[2,512,512]{2,1,0:T(8,128)(2,1)} %get-tuple-element.28), channel_id=1, source_target_pairs={{0,4},{4,0},{8,12},{12,8},{16,20},{20,16},{24,28},{28,24},{1,5},{5... | collective-permute-start | bytes 3145736 | tf_op jit(solution)/shard_map/ppermute | solution.py:347
  123.1 23.5 %collective-permute-start.8 = (bf16[512,512]{1,0:T(8,128)(2,1)}, bf16[512,512]{1,0:T(8,128)(2,1)}, u32[]{:S(2)}, u32[]{:S(2)}) collective-permute-start(bf16[512,512]{1,0:T(8,128)(2,1)} %get-tuple-element.19), channel_id=1, source_target_pairs={{0,16},{4,20},{8,24},{12,28},{16,0},{20,4},{24,8},{28,12},{1,17},{... | collective-permute-start | bytes 1572872 | tf_op jit(solution)/shard_map/ppermute | solution.py:344
  126.6 44.5 %collective-permute-start.14 = (bf16[2,512,512]{2,1,0:T(8,128)(2,1)}, bf16[2,512,512]{2,1,0:T(8,128)(2,1)}, u32[]{:S(2)}, u32[]{:S(2)}) collective-permute-start(bf16[2,512,512]{2,1,0:T(8,128)(2,1)} %get-tuple-element.24), channel_id=1, source_target_pairs={{0,4},{4,0},{8,12},{12,8},{16,20},{20,16},{24,28},{28,24},{1,5},{5... | collective-permute-start | bytes 3145736 | tf_op jit(solution)/shard_map/ppermute | solution.py:347
  128.0 18.6 %copy-start.4 = (bf16[512,512]{1,0:T(8,128)(2,1)S(1)}, bf16[512,512]{1,0:T(8,128)(2,1)}, u32[]{:S(2)}) copy-start(bf16[512,512]{1,0:T(8,128)(2,1)} %copy-done.3) | copy-start | bytes 1572868
  146.5 38.5 %collective-permute-start.20 = (bf16[2,512,512]{2,1,0:T(8,128)(2,1)S(1)}, bf16[2,512,512]{2,1,0:T(8,128)(2,1)S(1)}, u32[]{:S(2)}, u32[]{:S(2)}) collective-permute-start(bf16[2,512,512]{2,1,0:T(8,128)(2,1)S(1)} %get-tuple-element.30), channel_id=1, source_target_pairs={{0,8},{4,12},{8,0},{12,4},{16,24},{20,28},{24,16},{28,20},{1,9},{5... | collective-permute-start | bytes 3145736 | tf_op jit(solution)/shard_map/ppermute | solution.py:347
  147.8 48.6 %collective-permute-start.16 = (bf16[2,512,512]{2,1,0:T(8,128)(2,1)S(1)}, bf16[2,512,512]{2,1,0:T(8,128)(2,1)S(1)}, u32[]{:S(2)}, u32[]{:S(2)}) collective-permute-start(bf16[2,512,512]{2,1,0:T(8,128)(2,1)S(1)} %get-tuple-element.26), channel_id=1, source_target_pairs={{0,4},{4,0},{8,12},{12,8},{16,20},{20,16},{24,28},{28,24},{1,5},{5... | collective-permute-start | bytes 3145736 | tf_op jit(solution)/shard_map/ppermute | solution.py:347
  148.6 35.1 %collective-permute-start.10 = (bf16[512,512]{1,0:T(8,128)(2,1)S(1)}, bf16[512,512]{1,0:T(8,128)(2,1)S(1)}, u32[]{:S(2)}, u32[]{:S(2)}) collective-permute-start(bf16[512,512]{1,0:T(8,128)(2,1)S(1)} %get-tuple-element.22), channel_id=1, source_target_pairs={{0,16},{4,20},{8,24},{12,28},{16,0},{20,4},{24,8},{28,12},{1,17},{... | collective-permute-start | bytes 1572872 | tf_op jit(solution)/shard_map/ppermute | solution.py:344
  153.3 41.9 %collective-permute-start.19 = (bf16[512,512]{1,0:T(8,128)(2,1)S(1)}, bf16[512,512]{1,0:T(8,128)(2,1)S(1)}, u32[]{:S(2)}, u32[]{:S(2)}) collective-permute-start(bf16[512,512]{1,0:T(8,128)(2,1)S(1)} %fusion.6), channel_id=1, source_target_pairs={{0,8},{4,12},{8,0},{12,4},{16,24},{20,28},{24,16},{28,20},{1,9},{5... | collective-permute-start | bytes 1572872 | tf_op jit(solution)/shard_map/ppermute | solution.py:347
  173.0 38.5 %collective-permute-start.15 = (bf16[512,512]{1,0:T(8,128)(2,1)}, bf16[512,512]{1,0:T(8,128)(2,1)}, u32[]{:S(2)}, u32[]{:S(2)}) collective-permute-start(bf16[512,512]{1,0:T(8,128)(2,1)} %fusion.4), channel_id=1, source_target_pairs={{0,8},{4,12},{8,0},{12,4},{16,24},{20,28},{24,16},{28,20},{1,9},{5... | collective-permute-start | bytes 1572872 | tf_op jit(solution)/shard_map/ppermute | solution.py:347
  185.2 16.3 %collective-permute-start.21 = (bf16[512,512]{1,0:T(8,128)(2,1)S(1)}, bf16[512,512]{1,0:T(8,128)(2,1)S(1)}, u32[]{:S(2)}, u32[]{:S(2)}) collective-permute-start(bf16[512,512]{1,0:T(8,128)(2,1)S(1)} %fusion.7), channel_id=1, source_target_pairs={{0,4},{4,0},{8,12},{12,8},{16,20},{20,16},{24,28},{28,24},{1,5},{5... | collective-permute-start | bytes 1572872 | tf_op jit(solution)/shard_map/ppermute | solution.py:347
  196.4 6.4 %copy-start.8 = (bf16[2,512,512]{2,1,0:T(8,128)(2,1)}, bf16[2,512,512]{2,1,0:T(8,128)(2,1)S(1)}, u32[]{:S(2)}) copy-start(bf16[2,512,512]{2,1,0:T(8,128)(2,1)S(1)} %collective-permute-done.16) | copy-start | bytes 3145732
  197.5 18.0 %collective-permute-start.17 = (bf16[512,512]{1,0:T(8,128)(2,1)}, bf16[512,512]{1,0:T(8,128)(2,1)}, u32[]{:S(2)}, u32[]{:S(2)}) collective-permute-start(bf16[512,512]{1,0:T(8,128)(2,1)} %fusion.5), channel_id=1, source_target_pairs={{0,8},{4,12},{8,0},{12,4},{16,24},{20,28},{24,16},{28,20},{1,9},{5... | collective-permute-start | bytes 1572872 | tf_op jit(solution)/shard_map/ppermute | solution.py:347
  202.8 19.2 %all-to-all-start.1 = ((bf16[4,128,1024]{2,1,0:T(8,128)(2,1)}), bf16[4,128,1024]{2,1,0:T(8,128)(2,1)}, u32[]{:S(2)}, u32[]{:S(2)}) async-start(bf16[4,128,1024]{2,1,0:T(8,128)(2,1)} %bitcast.94), calls=%async_computation.1 | async-start | bytes 2097152 | tf_op jit(solution)/shard_map/all_to_all | solution.py:490
  207.1 8.4 %copy-start.9 = (bf16[2,512,512]{2,1,0:T(8,128)(2,1)S(1)}, bf16[2,512,512]{2,1,0:T(8,128)(2,1)}, u32[]{:S(2)}) copy-start(bf16[2,512,512]{2,1,0:T(8,128)(2,1)} %copy-done.8) | copy-start | bytes 3145732
  208.1 18.6 %collective-permute-start.11 = (bf16[128,1024]{1,0:T(8,128)(2,1)}, bf16[128,1024]{1,0:T(8,128)(2,1)}, u32[]{:S(2)}, u32[]{:S(2)}) collective-permute-start(bf16[128,1024]{1,0:T(8,128)(2,1)} %get-tuple-element.38), channel_id=1, source_target_pairs={{0,1},{1,2},{2,3},{3,0},{4,5},{5,6},{6,7},{7,4},{8,9},{9,10},{10,1... | collective-permute-start | bytes 786440 | tf_op jit(solution)/shard_map/ppermute | solution.py:513
  208.5 19.2 %collective-permute-start.12 = (bf16[128,1024]{1,0:T(8,128)(2,1)}, bf16[128,1024]{1,0:T(8,128)(2,1)}, u32[]{:S(2)}, u32[]{:S(2)}) collective-permute-start(bf16[128,1024]{1,0:T(8,128)(2,1)} %get-tuple-element.37), channel_id=1, source_target_pairs={{0,2},{1,3},{2,0},{3,1},{4,6},{5,7},{6,4},{7,5},{8,10},{9,11},{10,... | collective-permute-start | bytes 786440 | tf_op jit(solution)/shard_map/ppermute | solution.py:513
  210.2 20.7 %collective-permute-start.13 = (bf16[128,1024]{1,0:T(8,128)(2,1)}, bf16[128,1024]{1,0:T(8,128)(2,1)}, u32[]{:S(2)}, u32[]{:S(2)}) collective-permute-start(bf16[128,1024]{1,0:T(8,128)(2,1)} %get-tuple-element.36), channel_id=1, source_target_pairs={{0,3},{1,0},{2,1},{3,2},{4,7},{5,4},{6,5},{7,6},{8,11},{9,8},{10,9... | collective-permute-start | bytes 786440 | tf_op jit(solution)/shard_map/ppermute | solution.py:513
  216.8 14.2 %copy-start.11 = (bf16[1,128,1024]{2,1,0:T(8,128)(2,1)S(1)}, bf16[1,128,1024]{2,1,0:T(8,128)(2,1)}, u32[]{:S(2)}) copy-start(bf16[1,128,1024]{2,1,0:T(8,128)(2,1)} %get-tuple-element.35) | copy-start | bytes 786436
  222.1 21.9 %all-to-all-start = ((bf16[4,128,1024]{2,1,0:T(8,128)(2,1)}), bf16[4,128,1024]{2,1,0:T(8,128)(2,1)S(1)}, u32[]{:S(2)}, u32[]{:S(2)}) async-start(bf16[4,128,1024]{2,1,0:T(8,128)(2,1)} %bitcast.33), calls=%async_computation | async-start | bytes 2097152 | tf_op jit(solution)/shard_map/all_to_all | solution.py:490
  (6 other events, 17.5 us)

commit v8 on v7

--- a/solution.py
+++ b/solution.py
@@ -11,7 +11,7 @@
 DH = 128
 BS = 64
 GROUP = 4
-BATCH = 8
+BATCH = 16
 CUTS = (0.0, 0.5, 1.0)
 VALUE_AXES = (1, 2)
 JOINED = 4

time: 250 us -> 251 us (level)
  transfers between devices with their start and end apart: 24 -> 24, of which waited for: 13 -> 13; matrix products, arithmetic and copies ran while one was open for 13% -> 13% of each run, Pallas kernels for 19% -> 20%
where the time goes in v8:
time: 251 us; the launch traced here: 246 us
  waiting for transfers between devices  123 us (49%)
  Pallas kernels  48.8 us (19%)
  starting transfers between devices  39.3 us (16%)
  other arithmetic  23 us (9%)
  local copies, waits for them, and re-layouts  10.9 us (4%)
    ppermute x14, waiting for transfers between devices, flip(): return lax.ppermute(array, 'seq', [(i, i ^ j) for i in range(seq_count)])  91.9 us
    pallas_call x2, Pallas kernels, gradients(): pl.pallas_call(partial(grads_kernel, sizes, VALUE_AXES[c], head0), grid_s...  38.3 us
    ppermute x14, starting transfers between devices, flip(): return lax.ppermute(array, 'seq', [(i, i ^ j) for i in range(seq_count)])  14.6 us
    all_to_all x2, waiting for transfers between devices, to_tokens(): lax.all_to_all(array, 'head', split_axis=0, concat_axis=1, tiled=True)  14 us
    ppermute x5, starting transfers between devices, shift(): return lax.ppermute(array, 'seq', pairs)  13.5 us
    ppermute x5, waiting for transfers between devices, shift(): return lax.ppermute(array, 'seq', pairs)  11.8 us
    pallas_call x1, Pallas kernels, on_device(): pl.pallas_call(partial(norm_kernel, sizes), grid_spec=pltpu.PrefetchScala...  10.5 us
    all_to_all x2, starting transfers between devices, to_tokens(): lax.all_to_all(array, 'head', split_axis=0, concat_axis=1, tiled=True)  7.76 us
  transfers between devices with their start and end apart: 24, of which 13 were waited for; matrix products, arithmetic and copies ran while one was open for 13% of the time, Pallas kernels for 20%

profile of v8, /device:TPU:8, one launch (start us, length us, event | category | flops | bytes accessed | tf_op | source)
XLA Modules:
  0.0 246.0 jit_solution(8214683229704089231)
XLA Ops:
  0.7 3.2 %pad_maximum_fusion = bf16[2,512,1024]{2,1,0:T(8,128)(2,1)} fusion(bf16[1,512,1024]{2,1,0:T(8,128)(2,1)} %bitcast.90, bf16[1,512,1024]{2,1,0:T(8,128)(2,1)} %bitcast.89), kind=kLoop, calls=%fused_computation | loop fusion | flops 1048576 | bytes 4194304 | tf_op jit(solution)/shard_map/stack | solution.py:361
  3.9 1.9 collective-permute-start.2
  5.9 2.6 %collective-permute-start = (bf16[512,1024]{1,0:T(8,128)(2,1)S(1)}, bf16[512,1024]{1,0:T(8,128)(2,1)}, u32[]{:S(2)}, u32[]{:S(2)}) collective-permute-start(bf16[512,1024]{1,0:T(8,128)(2,1)S(1)} %copy-done.1), channel_id=1, source_target_pairs={{0,16},{4,20},{8,24},{12,28},{16,0},{20,4},{24,8},{28,12},{1,17},{... | collective-permute-start | bytes 3145736 | tf_op jit(solution)/shard_map/ppermute | solution.py:344
  8.4 33.4 %collective-permute-done.3.refs_4_.refs_6_ = bf16[512,1024]{1,0:T(8,128)(2,1)S(1)} collective-permute-done((bf16[512,1024]{1,0:T(8,128)(2,1)}, bf16[512,1024]{1,0:T(8,128)(2,1)S(1)}, u32[]{:S(2)}, u32[]{:S(2)}) %collective-permute-start.3) | collective-permute-done | bytes 1048608 | tf_op jit(solution)/shard_map/ppermute | solution.py:347
  41.9 2.6 %collective-permute-start.4 = (bf16[512,1024]{1,0:T(8,128)(2,1)S(1)}, bf16[512,1024]{1,0:T(8,128)(2,1)}, u32[]{:S(2)}, u32[]{:S(2)}) collective-permute-start(bf16[512,1024]{1,0:T(8,128)(2,1)S(1)} %collective-permute-done.3.refs_4_.refs_6_), channel_id=1, source_target_pairs={{0,4},{4,0},{8,12},{12,8},{16,20},{20,16},{24,28},{28,24},{1,5},{5... | collective-permute-start | bytes 3145736 | tf_op jit(solution)/shard_map/ppermute | solution.py:347
  44.5 3.4 %collective-permute-start.1 = (bf16[512,1024]{1,0:T(8,128)(2,1)}, bf16[512,1024]{1,0:T(8,128)(2,1)}, u32[]{:S(2)}, u32[]{:S(2)}) collective-permute-start(bf16[512,1024]{1,0:T(8,128)(2,1)} %refs_2_.5), channel_id=1, source_target_pairs={{0,16},{4,20},{8,24},{12,28},{16,0},{20,4},{24,8},{28,12},{1,17},{... | collective-permute-start | bytes 3145736 | tf_op jit(solution)/shard_map/ppermute | solution.py:344
  49.9 1.6 multiply_bitcast_fusion
  51.5 1.9 copy.28
  53.3 2.3 reduce_sum.27
  55.9 26.2 %collective-permute-done.5.refs_10_ = bf16[512,512]{1,0:T(8,128)(2,1)} collective-permute-done((bf16[512,512]{1,0:T(8,128)(2,1)}, bf16[512,512]{1,0:T(8,128)(2,1)}, u32[]{:S(2)}, u32[]{:S(2)}) %collective-permute-start.5) | collective-permute-done | bytes 524320 | tf_op jit(solution)/shard_map/ppermute | solution.py:347
  82.1 1.5 collective-permute-start.6
  83.7 10.5 %partial_norms.1 = f32[2,8,8,64]{3,2,1,0:T(8,128)S(1)} custom-call(s32[3]{0:T(128)S(1)} %pad_add_fusion.meta, s32[1536]{0:T(1024)S(1)} %reshape.99.table, bf16[512,1024]{1,0:T(8,128)(2,1)S(1)} %copy-done.1, bf16[512,1024]{1,0:T(8,128)(2,1)} %collective-permute-done.refs_1_, bf16[512,1024]{1,0:T(8,128)(2,1)S(1)} %copy-done, ...), custom_call_target="tpu_custom_call" | custom-call | tf_op jit(solution)/shard_map/partial_norms/pallas_call | solution.py:395
  96.3 2.5 %collective-permute-start.9 = (bf16[2,512,512]{2,1,0:T(8,128)(2,1)S(1)}, bf16[2,512,512]{2,1,0:T(8,128)(2,1)}, u32[]{:S(2)}, u32[]{:S(2)}) collective-permute-start(bf16[2,512,512]{2,1,0:T(8,128)(2,1)S(1)} %pad_maximum_fusion.1), channel_id=1, source_target_pairs={{0,8},{4,12},{8,0},{12,4},{16,24},{20,28},{24,16},{28,20},{1,9},{5... | collective-permute-start | bytes 3145736 | tf_op jit(solution)/shard_map/ppermute | solution.py:347
  98.8 3.3 %collective-permute-done.7 = f32[3,8,8,64]{3,2,1,0:T(8,128)S(1)} collective-permute-done((f32[3,8,8,64]{3,2,1,0:T(8,128)S(1)}, f32[3,8,8,64]{3,2,1,0:T(8,128)S(1)}, u32[]{:S(2)}, u32[]{:S(2)}) %collective-permute-start.7) | collective-permute-done | bytes 49184 | tf_op jit(solution)/shard_map/ppermute | solution.py:344
  102.7 19.3 %gradients.2 = (bf16[512,512]{1,0:T(8,128)(2,1)S(1)}, bf16[512,512]{1,0:T(8,128)(2,1)}, bf16[2,512,512]{2,1,0:T(8,128)(2,1)S(1)}, bf16[2,512,512]{2,1,0:T(8,128)...) custom-call(s32[3]{0:T(128)S(1)} %pad_add_fusion.meta, s32[1536]{0:T(1024)S(1)} %reshape.99.table, ...), custom_call_target="tpu_custom_call" | custom-call | tf_op jit(solution)/shard_map/gradients/pallas_call | solution.py:441
  123.3 3.4 %collective-permute-start.8 = (bf16[512,512]{1,0:T(8,128)(2,1)}, bf16[512,512]{1,0:T(8,128)(2,1)}, u32[]{:S(2)}, u32[]{:S(2)}) collective-permute-start(bf16[512,512]{1,0:T(8,128)(2,1)} %get-tuple-element.19), channel_id=1, source_target_pairs={{0,16},{4,20},{8,24},{12,28},{16,0},{20,4},{24,8},{28,12},{1,17},{... | collective-permute-start | bytes 1572872 | tf_op jit(solution)/shard_map/ppermute | solution.py:344
  126.7 1.5 collective-permute-start.14
  128.2 19.0 %gradients.3 = (bf16[512,512]{1,0:T(8,128)(2,1)S(1)}, bf16[512,512]{1,0:T(8,128)(2,1)S(1)}, bf16[2,512,512]{2,1,0:T(8,128)(2,1)S(1)}, bf16[2,512,512]{2,1,0:T(8,...) custom-call(s32[3]{0:T(128)S(1)} %pad_add_fusion.meta, s32[1536]{0:T(1024)S(1)} %reshape.99.table, ...), custom_call_target="tpu_custom_call" | custom-call | tf_op jit(solution)/shard_map/gradients/pallas_call | solution.py:441
  149.2 3.4 %collective-permute-start.10 = (bf16[512,512]{1,0:T(8,128)(2,1)S(1)}, bf16[512,512]{1,0:T(8,128)(2,1)S(1)}, u32[]{:S(2)}, u32[]{:S(2)}) collective-permute-start(bf16[512,512]{1,0:T(8,128)(2,1)S(1)} %get-tuple-element.22), channel_id=1, source_target_pairs={{0,16},{4,20},{8,24},{12,28},{16,0},{20,4},{24,8},{28,12},{1,17},{... | collective-permute-start | bytes 1572872 | tf_op jit(solution)/shard_map/ppermute | solution.py:344
  154.1 17.5 %collective-permute-done.14 = bf16[2,512,512]{2,1,0:T(8,128)(2,1)} collective-permute-done((bf16[2,512,512]{2,1,0:T(8,128)(2,1)}, bf16[2,512,512]{2,1,0:T(8,128)(2,1)}, u32[]{:S(2)}, u32[]{:S(2)}) %collective-permute-start.14) | collective-permute-done | bytes 1048608 | tf_op jit(solution)/shard_map/ppermute | solution.py:347
  171.6 2.0 fusion.4
  173.6 2.4 collective-permute-start.15
  176.0 8.5 %collective-permute-done.10 = bf16[512,512]{1,0:T(8,128)(2,1)S(1)} collective-permute-done((bf16[512,512]{1,0:T(8,128)(2,1)S(1)}, bf16[512,512]{1,0:T(8,128)(2,1)S(1)}, u32[]{:S(2)}, u32[]{:S(2)}) %collective-permute-start.10) | collective-permute-done | bytes 524320 | tf_op jit(solution)/shard_map/ppermute | solution.py:344
  186.5 9.4 %collective-permute-done.19 = bf16[512,512]{1,0:T(8,128)(2,1)S(1)} collective-permute-done((bf16[512,512]{1,0:T(8,128)(2,1)S(1)}, bf16[512,512]{1,0:T(8,128)(2,1)S(1)}, u32[]{:S(2)}, u32[]{:S(2)}) %collective-permute-start.19) | collective-permute-done | bytes 524320 | tf_op jit(solution)/shard_map/ppermute | solution.py:347
  198.2 4.2 %collective-permute-done.21 = bf16[512,512]{1,0:T(8,128)(2,1)S(1)} collective-permute-done((bf16[512,512]{1,0:T(8,128)(2,1)S(1)}, bf16[512,512]{1,0:T(8,128)(2,1)S(1)}, u32[]{:S(2)}, u32[]{:S(2)}) %collective-permute-start.21) | collective-permute-done | bytes 524320 | tf_op jit(solution)/shard_map/ppermute | solution.py:347
  203.8 4.2 %all-to-all-start.1 = ((bf16[4,128,1024]{2,1,0:T(8,128)(2,1)}), bf16[4,128,1024]{2,1,0:T(8,128)(2,1)}, u32[]{:S(2)}, u32[]{:S(2)}) async-start(bf16[4,128,1024]{2,1,0:T(8,128)(2,1)} %bitcast.94), calls=%async_computation.1 | async-start | bytes 2097152 | tf_op jit(solution)/shard_map/all_to_all | solution.py:490
  209.5 1.7 collective-permute-start.12
  217.4 5.6 %all-to-all-done.1 = bf16[4,128,1024]{2,1,0:T(8,128)(2,1)} async-done(((bf16[4,128,1024]{2,1,0:T(8,128)(2,1)}), bf16[4,128,1024]{2,1,0:T(8,128)(2,1)}, u32[]{:S(2)}, u32[]{:S(2)}) %all-to-all-start.1) | async-done | bytes 1048608 | tf_op jit(solution)/shard_map/all_to_all | solution.py:490
  223.0 3.5 %all-to-all-start = ((bf16[4,128,1024]{2,1,0:T(8,128)(2,1)}), bf16[4,128,1024]{2,1,0:T(8,128)(2,1)S(1)}, u32[]{:S(2)}, u32[]{:S(2)}) async-start(bf16[4,128,1024]{2,1,0:T(8,128)(2,1)} %bitcast.33), calls=%async_computation | async-start | bytes 2097152 | tf_op jit(solution)/shard_map/all_to_all | solution.py:490
  228.7 3.2 %collective-permute-done.13 = bf16[128,1024]{1,0:T(8,128)(2,1)} collective-permute-done((bf16[128,1024]{1,0:T(8,128)(2,1)}, bf16[128,1024]{1,0:T(8,128)(2,1)}, u32[]{:S(2)}, u32[]{:S(2)}) %collective-permute-start.13) | collective-permute-done | bytes 262176 | tf_op jit(solution)/shard_map/ppermute | solution.py:513
  234.3 2.3 copy.27
  236.6 8.4 %all-to-all-done = bf16[4,128,1024]{2,1,0:T(8,128)(2,1)S(1)} async-done(((bf16[4,128,1024]{2,1,0:T(8,128)(2,1)}), bf16[4,128,1024]{2,1,0:T(8,128)(2,1)S(1)}, u32[]{:S(2)}, u32[]{:S(2)}) %all-to-all-start) | async-done | bytes 1048608 | tf_op jit(solution)/shard_map/all_to_all | solution.py:490
  (94 shorter events, 28.5 us)
Async XLA Ops:
  0.6 41.2 %collective-permute-start.3 = (bf16[512,1024]{1,0:T(8,128)(2,1)}, bf16[512,1024]{1,0:T(8,128)(2,1)S(1)}, u32[]{:S(2)}, u32[]{:S(2)}) collective-permute-start(bf16[512,1024]{1,0:T(8,128)(2,1)} %refs_4_.3), channel_id=1, source_target_pairs={{0,8},{4,12},{8,0},{12,4},{16,24},{20,28},{24,16},{28,20},{1,9},{5... | collective-permute-start | bytes 3145736 | tf_op jit(solution)/shard_map/ppermute | solution.py:347
  0.7 47.1 %copy-start.12 = (s32[64,8,3]{0,1,2:T(8,128)S(1)}, s32[64,8,3]{0,1,2:T(8,128)}, u32[]{:S(2)}) copy-start(s32[64,8,3]{0,1,2:T(8,128)} %param.12) | copy-start | bytes 18436
  0.7 47.5 %copy-start.5 = (bf16[512,1024]{1,0:T(8,128)(2,1)S(1)}, bf16[512,1024]{1,0:T(8,128)(2,1)}, u32[]{:S(2)}) copy-start(bf16[512,1024]{1,0:T(8,128)(2,1)} %refs_8_.3) | copy-start | bytes 3145732
  3.9 79.7 %collective-permute-start.2 = (bf16[2,512,1024]{2,1,0:T(8,128)(2,1)}, bf16[2,512,1024]{2,1,0:T(8,128)(2,1)}, u32[]{:S(2)}, u32[]{:S(2)}) collective-permute-start(bf16[2,512,1024]{2,1,0:T(8,128)(2,1)} %pad_maximum_fusion), channel_id=1, source_target_pairs={{0,4},{4,0},{8,12},{12,8},{16,20},{20,16},{24,28},{28,24},{1,5},{5... | collective-permute-start | bytes 6291464 | tf_op jit(solution)/shard_map/ppermute | solution.py:347
  5.9 77.8 %collective-permute-start = (bf16[512,1024]{1,0:T(8,128)(2,1)S(1)}, bf16[512,1024]{1,0:T(8,128)(2,1)}, u32[]{:S(2)}, u32[]{:S(2)}) collective-permute-start(bf16[512,1024]{1,0:T(8,128)(2,1)S(1)} %copy-done.1), channel_id=1, source_target_pairs={{0,16},{4,20},{8,24},{12,28},{16,0},{20,4},{24,8},{28,12},{1,17},{... | collective-permute-start | bytes 3145736 | tf_op jit(solution)/shard_map/ppermute | solution.py:344
  41.9 41.8 %copy-start.2 = (bf16[512,1024]{1,0:T(8,128)(2,1)}, bf16[512,1024]{1,0:T(8,128)(2,1)S(1)}, u32[]{:S(2)}) copy-start(bf16[512,1024]{1,0:T(8,128)(2,1)S(1)} %collective-permute-done.3.refs_4_.refs_6_) | copy-start | bytes 3145732
  41.9 41.8 %collective-permute-start.4 = (bf16[512,1024]{1,0:T(8,128)(2,1)S(1)}, bf16[512,1024]{1,0:T(8,128)(2,1)}, u32[]{:S(2)}, u32[]{:S(2)}) collective-permute-start(bf16[512,1024]{1,0:T(8,128)(2,1)S(1)} %collective-permute-done.3.refs_4_.refs_6_), channel_id=1, source_target_pairs={{0,4},{4,0},{8,12},{12,8},{16,20},{20,16},{24,28},{28,24},{1,5},{5... | collective-permute-start | bytes 3145736 | tf_op jit(solution)/shard_map/ppermute | solution.py:347
  44.5 58.2 %collective-permute-start.1 = (bf16[512,1024]{1,0:T(8,128)(2,1)}, bf16[512,1024]{1,0:T(8,128)(2,1)}, u32[]{:S(2)}, u32[]{:S(2)}) collective-permute-start(bf16[512,1024]{1,0:T(8,128)(2,1)} %refs_2_.5), channel_id=1, source_target_pairs={{0,16},{4,20},{8,24},{12,28},{16,0},{20,4},{24,8},{28,12},{1,17},{... | collective-permute-start | bytes 3145736 | tf_op jit(solution)/shard_map/ppermute | solution.py:344
  49.3 32.8 %collective-permute-start.5 = (bf16[512,512]{1,0:T(8,128)(2,1)}, bf16[512,512]{1,0:T(8,128)(2,1)}, u32[]{:S(2)}, u32[]{:S(2)}) collective-permute-start(bf16[512,512]{1,0:T(8,128)(2,1)} %get-tuple-element.17), channel_id=1, source_target_pairs={{0,8},{4,12},{8,0},{12,4},{16,24},{20,28},{24,16},{28,20},{1,9},{5... | collective-permute-start | bytes 1572872 | tf_op jit(solution)/shard_map/ppermute | solution.py:347
  53.3 30.3 %copy-start = (bf16[512,1024]{1,0:T(8,128)(2,1)S(1)}, bf16[512,1024]{1,0:T(8,128)(2,1)}, u32[]{:S(2)}) copy-start(bf16[512,1024]{1,0:T(8,128)(2,1)} %refs_4_.3) | copy-start | bytes 3145732
  82.1 20.5 %collective-permute-start.6 = (bf16[512,512]{1,0:T(8,128)(2,1)}, bf16[512,512]{1,0:T(8,128)(2,1)}, u32[]{:S(2)}, u32[]{:S(2)}) collective-permute-start(bf16[512,512]{1,0:T(8,128)(2,1)} %collective-permute-done.5.refs_10_), channel_id=1, source_target_pairs={{0,4},{4,0},{8,12},{12,8},{16,20},{20,16},{24,28},{28,24},{1,5},{5... | collective-permute-start | bytes 1572872 | tf_op jit(solution)/shard_map/ppermute | solution.py:347
  94.2 7.8 %collective-permute-start.7 = (f32[3,8,8,64]{3,2,1,0:T(8,128)S(1)}, f32[3,8,8,64]{3,2,1,0:T(8,128)S(1)}, u32[]{:S(2)}, u32[]{:S(2)}) collective-permute-start(f32[3,8,8,64]{3,2,1,0:T(8,128)S(1)} %pad_maximum_fusion.7), channel_id=1, source_target_pairs={{0,16},{4,20},{8,24},{12,28},{16,0},{20,4},{24,8},{28,12},{1,17},{... | collective-permute-start | bytes 147464 | tf_op jit(solution)/shard_map/ppermute | solution.py:344
  96.3 32.0 %collective-permute-start.9 = (bf16[2,512,512]{2,1,0:T(8,128)(2,1)S(1)}, bf16[2,512,512]{2,1,0:T(8,128)(2,1)}, u32[]{:S(2)}, u32[]{:S(2)}) collective-permute-start(bf16[2,512,512]{2,1,0:T(8,128)(2,1)S(1)} %pad_maximum_fusion.1), channel_id=1, source_target_pairs={{0,8},{4,12},{8,0},{12,4},{16,24},{20,28},{24,16},{28,20},{1,9},{5... | collective-permute-start | bytes 3145736 | tf_op jit(solution)/shard_map/ppermute | solution.py:347
  122.7 29.9 %collective-permute-start.18 = (bf16[2,512,512]{2,1,0:T(8,128)(2,1)}, bf16[2,512,512]{2,1,0:T(8,128)(2,1)}, u32[]{:S(2)}, u32[]{:S(2)}) collective-permute-start(bf16[2,512,512]{2,1,0:T(8,128)(2,1)} %get-tuple-element.28), channel_id=1, source_target_pairs={{0,4},{4,0},{8,12},{12,8},{16,20},{20,16},{24,28},{28,24},{1,5},{5... | collective-permute-start | bytes 3145736 | tf_op jit(solution)/shard_map/ppermute | solution.py:347
  123.3 24.1 %collective-permute-start.8 = (bf16[512,512]{1,0:T(8,128)(2,1)}, bf16[512,512]{1,0:T(8,128)(2,1)}, u32[]{:S(2)}, u32[]{:S(2)}) collective-permute-start(bf16[512,512]{1,0:T(8,128)(2,1)} %get-tuple-element.19), channel_id=1, source_target_pairs={{0,16},{4,20},{8,24},{12,28},{16,0},{20,4},{24,8},{28,12},{1,17},{... | collective-permute-start | bytes 1572872 | tf_op jit(solution)/shard_map/ppermute | solution.py:344
  126.7 44.9 %collective-permute-start.14 = (bf16[2,512,512]{2,1,0:T(8,128)(2,1)}, bf16[2,512,512]{2,1,0:T(8,128)(2,1)}, u32[]{:S(2)}, u32[]{:S(2)}) collective-permute-start(bf16[2,512,512]{2,1,0:T(8,128)(2,1)} %get-tuple-element.24), channel_id=1, source_target_pairs={{0,4},{4,0},{8,12},{12,8},{16,20},{20,16},{24,28},{28,24},{1,5},{5... | collective-permute-start | bytes 3145736 | tf_op jit(solution)/shard_map/ppermute | solution.py:347
  128.2 19.1 %copy-start.4 = (bf16[512,512]{1,0:T(8,128)(2,1)S(1)}, bf16[512,512]{1,0:T(8,128)(2,1)}, u32[]{:S(2)}) copy-start(bf16[512,512]{1,0:T(8,128)(2,1)} %copy-done.3) | copy-start | bytes 1572868
  147.3 38.5 %collective-permute-start.20 = (bf16[2,512,512]{2,1,0:T(8,128)(2,1)S(1)}, bf16[2,512,512]{2,1,0:T(8,128)(2,1)S(1)}, u32[]{:S(2)}, u32[]{:S(2)}) collective-permute-start(bf16[2,512,512]{2,1,0:T(8,128)(2,1)S(1)} %get-tuple-element.30), channel_id=1, source_target_pairs={{0,8},{4,12},{8,0},{12,4},{16,24},{20,28},{24,16},{28,20},{1,9},{5... | collective-permute-start | bytes 3145736 | tf_op jit(solution)/shard_map/ppermute | solution.py:347
  148.5 48.6 %collective-permute-start.16 = (bf16[2,512,512]{2,1,0:T(8,128)(2,1)S(1)}, bf16[2,512,512]{2,1,0:T(8,128)(2,1)S(1)}, u32[]{:S(2)}, u32[]{:S(2)}) collective-permute-start(bf16[2,512,512]{2,1,0:T(8,128)(2,1)S(1)} %get-tuple-element.26), channel_id=1, source_target_pairs={{0,4},{4,0},{8,12},{12,8},{16,20},{20,16},{24,28},{28,24},{1,5},{5... | collective-permute-start | bytes 3145736 | tf_op jit(solution)/shard_map/ppermute | solution.py:347
  149.2 35.3 %collective-permute-start.10 = (bf16[512,512]{1,0:T(8,128)(2,1)S(1)}, bf16[512,512]{1,0:T(8,128)(2,1)S(1)}, u32[]{:S(2)}, u32[]{:S(2)}) collective-permute-start(bf16[512,512]{1,0:T(8,128)(2,1)S(1)} %get-tuple-element.22), channel_id=1, source_target_pairs={{0,16},{4,20},{8,24},{12,28},{16,0},{20,4},{24,8},{28,12},{1,17},{... | collective-permute-start | bytes 1572872 | tf_op jit(solution)/shard_map/ppermute | solution.py:344
  153.8 42.0 %collective-permute-start.19 = (bf16[512,512]{1,0:T(8,128)(2,1)S(1)}, bf16[512,512]{1,0:T(8,128)(2,1)S(1)}, u32[]{:S(2)}, u32[]{:S(2)}) collective-permute-start(bf16[512,512]{1,0:T(8,128)(2,1)S(1)} %fusion.6), channel_id=1, source_target_pairs={{0,8},{4,12},{8,0},{12,4},{16,24},{20,28},{24,16},{28,20},{1,9},{5... | collective-permute-start | bytes 1572872 | tf_op jit(solution)/shard_map/ppermute | solution.py:347
  173.6 38.9 %collective-permute-start.15 = (bf16[512,512]{1,0:T(8,128)(2,1)}, bf16[512,512]{1,0:T(8,128)(2,1)}, u32[]{:S(2)}, u32[]{:S(2)}) collective-permute-start(bf16[512,512]{1,0:T(8,128)(2,1)} %fusion.4), channel_id=1, source_target_pairs={{0,8},{4,12},{8,0},{12,4},{16,24},{20,28},{24,16},{28,20},{1,9},{5... | collective-permute-start | bytes 1572872 | tf_op jit(solution)/shard_map/ppermute | solution.py:347
  185.9 16.6 %collective-permute-start.21 = (bf16[512,512]{1,0:T(8,128)(2,1)S(1)}, bf16[512,512]{1,0:T(8,128)(2,1)S(1)}, u32[]{:S(2)}, u32[]{:S(2)}) collective-permute-start(bf16[512,512]{1,0:T(8,128)(2,1)S(1)} %fusion.7), channel_id=1, source_target_pairs={{0,4},{4,0},{8,12},{12,8},{16,20},{20,16},{24,28},{28,24},{1,5},{5... | collective-permute-start | bytes 1572872 | tf_op jit(solution)/shard_map/ppermute | solution.py:347
  197.1 6.6 %copy-start.8 = (bf16[2,512,512]{2,1,0:T(8,128)(2,1)}, bf16[2,512,512]{2,1,0:T(8,128)(2,1)S(1)}, u32[]{:S(2)}) copy-start(bf16[2,512,512]{2,1,0:T(8,128)(2,1)S(1)} %collective-permute-done.16) | copy-start | bytes 3145732
  198.2 16.8 %collective-permute-start.17 = (bf16[512,512]{1,0:T(8,128)(2,1)}, bf16[512,512]{1,0:T(8,128)(2,1)}, u32[]{:S(2)}, u32[]{:S(2)}) collective-permute-start(bf16[512,512]{1,0:T(8,128)(2,1)} %fusion.5), channel_id=1, source_target_pairs={{0,8},{4,12},{8,0},{12,4},{16,24},{20,28},{24,16},{28,20},{1,9},{5... | collective-permute-start | bytes 1572872 | tf_op jit(solution)/shard_map/ppermute | solution.py:347
  203.8 19.2 %all-to-all-start.1 = ((bf16[4,128,1024]{2,1,0:T(8,128)(2,1)}), bf16[4,128,1024]{2,1,0:T(8,128)(2,1)}, u32[]{:S(2)}, u32[]{:S(2)}) async-start(bf16[4,128,1024]{2,1,0:T(8,128)(2,1)} %bitcast.94), calls=%async_computation.1 | async-start | bytes 2097152 | tf_op jit(solution)/shard_map/all_to_all | solution.py:490
  208.1 7.0 %copy-start.9 = (bf16[2,512,512]{2,1,0:T(8,128)(2,1)S(1)}, bf16[2,512,512]{2,1,0:T(8,128)(2,1)}, u32[]{:S(2)}) copy-start(bf16[2,512,512]{2,1,0:T(8,128)(2,1)} %copy-done.8) | copy-start | bytes 3145732
  209.1 18.6 %collective-permute-start.11 = (bf16[128,1024]{1,0:T(8,128)(2,1)}, bf16[128,1024]{1,0:T(8,128)(2,1)}, u32[]{:S(2)}, u32[]{:S(2)}) collective-permute-start(bf16[128,1024]{1,0:T(8,128)(2,1)} %get-tuple-element.38), channel_id=1, source_target_pairs={{0,1},{1,2},{2,3},{3,0},{4,5},{5,6},{6,7},{7,4},{8,9},{9,10},{10,1... | collective-permute-start | bytes 786440 | tf_op jit(solution)/shard_map/ppermute | solution.py:513
  209.5 19.2 %collective-permute-start.12 = (bf16[128,1024]{1,0:T(8,128)(2,1)}, bf16[128,1024]{1,0:T(8,128)(2,1)}, u32[]{:S(2)}, u32[]{:S(2)}) collective-permute-start(bf16[128,1024]{1,0:T(8,128)(2,1)} %get-tuple-element.37), channel_id=1, source_target_pairs={{0,2},{1,3},{2,0},{3,1},{4,6},{5,7},{6,4},{7,5},{8,10},{9,11},{10,... | collective-permute-start | bytes 786440 | tf_op jit(solution)/shard_map/ppermute | solution.py:513
  211.2 20.7 %collective-permute-start.13 = (bf16[128,1024]{1,0:T(8,128)(2,1)}, bf16[128,1024]{1,0:T(8,128)(2,1)}, u32[]{:S(2)}, u32[]{:S(2)}) collective-permute-start(bf16[128,1024]{1,0:T(8,128)(2,1)} %get-tuple-element.36), channel_id=1, source_target_pairs={{0,3},{1,0},{2,1},{3,2},{4,7},{5,4},{6,5},{7,6},{8,11},{9,8},{10,9... | collective-permute-start | bytes 786440 | tf_op jit(solution)/shard_map/ppermute | solution.py:513
  216.3 15.6 %copy-start.11 = (bf16[1,128,1024]{2,1,0:T(8,128)(2,1)S(1)}, bf16[1,128,1024]{2,1,0:T(8,128)(2,1)}, u32[]{:S(2)}) copy-start(bf16[1,128,1024]{2,1,0:T(8,128)(2,1)} %get-tuple-element.35) | copy-start | bytes 786436
  223.0 21.9 %all-to-all-start = ((bf16[4,128,1024]{2,1,0:T(8,128)(2,1)}), bf16[4,128,1024]{2,1,0:T(8,128)(2,1)S(1)}, u32[]{:S(2)}, u32[]{:S(2)}) async-start(bf16[4,128,1024]{2,1,0:T(8,128)(2,1)} %bitcast.33), calls=%async_computation | async-start | bytes 2097152 | tf_op jit(solution)/shard_map/all_to_all | solution.py:490
  (6 other events, 17.5 us)
